TPU v7x, 32 devices: a whole 2x2x4 slice. The times are simulated.
32 devices in a mesh: dp: 2 (over y), space: 16 (over z, x, core).
Axes of the slice: x: 2, y: 2, z: 4, core: 2. Of those that a mesh axis runs over, the one named last changes fastest.
Arguments:
- inputs: bfloat16 [2, 16, 48, 4096], P('dp', 'space'), may hold values from -6 to 6
- cotangent: bfloat16 [2, 16, 48, 4096], P('dp', 'space'), may hold values from -6 to 6
- conv_one: bfloat16 [9, 48, 48], replicated, may hold values from -0.3125 to 0.3125
- bias_one: float32 [48], replicated, may hold values from -3 to 3
- conv_two: bfloat16 [9, 48, 48], replicated, may hold values from -0.3125 to 0.3125
- bias_two: float32 [48], replicated, may hold values from -3 to 3
- neighbours: int32 [16, 4, 3], replicated, may hold values from 0 to 15, as said below
- corner_rule: int32 [16, 4], replicated, may hold values from 0 to 2
Outputs:
- output: bfloat16 [2, 16, 48, 4096], P('dp', 'space')
- grad_in: bfloat16 [2, 16, 48, 4096], P('dp', 'space')
- grad_conv_one: float32 [9, 48, 48], P(None, 'dp')
- grad_bias_one: float32 [48], P('dp')
- grad_conv_two: float32 [9, 48, 48], P(None, 'dp')
- grad_bias_two: float32 [48], P('dp')
Inputs may be any that keep to these rules, and one draw needn't show every extreme that they name: Slot neighbours[t, e, 0] of a tile on the device block d (tiles d * 1 to d + 1 - 1) lies on block d - 1, d + 4, d + 1, d - 4 (cyclically over the 16 blocks) for e = 0, 1, 2, 3; neighbours[t, e, 1] and neighbours[t, e, 2] are 0 to 3.
All inputs are finite; a program needn't handle non-finite values.
Results may differ from a plain program's by a relative error of at most 0.009.
Values may be sent and summed in bfloat16 or wider, within the bound.
No kernel may reach another device: no remote copies, remote signals or barrier semaphores. Data moves between devices by JAX's collectives and lax.ppermute only.
A program may use at most 64 MiB of HBM per device.

v0:
```python
import functools
import math

import jax
import jax.numpy as jnp
from jax import lax
from jax.experimental import pallas as pl
from jax.experimental.pallas import tpu as pltpu
from jax.sharding import PartitionSpec as P

BF = jnp.bfloat16
F32 = jnp.float32
C = 48
SIDE = 64
PIX = SIDE * SIDE
LANES = 128
TILES = PIX // LANES
LINE_AT = (64, 0, 0, 0)
USER_AT = (0, 64, 64, 64)

VMEM = pl.BlockSpec(memory_space=pltpu.VMEM)
SMEM = pl.BlockSpec(memory_space=pltpu.SMEM)


def tap_of(edge, step):
    return (step, 3 * step + 2, 6 + step, 3 * step)[edge]


def offsets_of(spaces):
    return (-1, spaces // 4, 1, -(spaces // 4))


def dot(a, b):
    return jnp.dot(a, b, preferred_element_type=F32)


def dot_nt(a, b):
    return lax.dot_general(a, b, (((1,), (1,)), ((), ())), preferred_element_type=F32)


def iota(shape, axis):
    return lax.broadcasted_iota(jnp.int32, shape, axis)


def line_lanes(lane):
    z = lane - 128
    even = (z & 1) == 0
    left = jnp.where(z < 64, z, z - 63)
    right = jnp.where(z < 63, z + 2, jnp.where(z < 127, z - 63, 1))
    line = jnp.where(lane < 64, 0, jnp.where(lane < 128, 2, jnp.where(even, 3, 1)))
    place = jnp.where(lane < 64, lane, jnp.where(lane < 128, lane - 64, jnp.where(even, left, right)))
    return line, place


def lane_masks():
    lane = iota((C, LANES), 1) & 63
    return lane == 0, lane == 63


def tile(ref, t):
    return ref[:, t * LANES : (t + 1) * LANES]


def lines_from(tiles, first, last):
    total = tiles[0]
    for t in range(1, TILES):
        total = total + pltpu.roll(tiles[t], 2 * t, 1)
    low = iota((C, LANES), 1) < 64
    rows = jnp.where(low, first, last)
    return jnp.concatenate([rows, total], axis=1).astype(BF)


def edge_only(values):
    at_left, at_right = lane_masks()
    return jnp.where(at_left | at_right, values, 0.0)


def send_matrices(tables, rules, me, spaces):
    row = iota((256, LANES), 0)
    lane = iota((256, LANES), 1)
    line, place = line_lanes(row)
    out = []
    for edge, offset in enumerate(offsets_of(spaces)):
        target = lax.rem(me - offset + spaces, spaces)
        k = tables[target, edge, 1]
        r = tables[target, edge, 2]
        turned = (r == 1) | (r == 2)
        want = jnp.where(turned, 63 - place, place)
        top = (line == k) & (lane - LINE_AT[edge] == want)
        own = (line == (edge + 2) % 4) & (lane - USER_AT[edge] == place)
        out.append(jnp.concatenate([jnp.where(top, 1.0, 0.0), jnp.where(own, 1.0, 0.0)], axis=0).astype(BF))
    return out


def my_space():
    return lax.axis_index("space")


def send_kernel(spaces, tables, rules, x_ref, g_ref, *outs):
    me = my_space()

    def lines(ref):
        tiles = [edge_only(tile(ref, t).astype(F32)) for t in range(TILES)]
        return lines_from(tiles, tile(ref, 0).astype(F32), tile(ref, TILES - 1).astype(F32))

    both = jnp.concatenate([lines(x_ref), lines(g_ref)], axis=1)
    for out, matrix in zip(outs, send_matrices(tables, rules, me, spaces)):
        out[...] = dot(both, matrix).astype(BF)


def weights_of(rules, where, corner):
    rule = rules[where, corner]
    first = jnp.where(rule == 0, 1.0, jnp.where(rule == 1, 0.0, 0.5)).astype(F32)
    return first, 1.0 - first


def user_matrix(tables, rules, me, spaces, edge, step):
    used = (edge + 2) % 4
    user = lax.rem(me + offsets_of(spaces)[edge] + spaces, spaces)
    k = tables[user, used, 1]
    r = tables[user, used, 2]
    turned = (r == 1) | (r == 2)
    q = iota((LANES, 256), 0) - USER_AT[edge]
    line, place = line_lanes(iota((LANES, 256), 1))
    want = jnp.where(turned, 63 - place, place)
    value = jnp.where(q == want + 1 - step, 1.0, 0.0)
    which = used % 2
    corners = ((0, 1), (1, 3), (2, 3), (0, 2))[used]
    if step == 0:
        weight = weights_of(rules, user, corners[0])[which]
        value = value + jnp.where((want == 0) & (q == 0), weight, 0.0)
    if step == 2:
        weight = weights_of(rules, user, corners[1])[which]
        value = value + jnp.where((want == 63) & (q == 63), weight, 0.0)
    return jnp.where((line == k) & (q >= 0) & (q < 64), value, 0.0).astype(BF)


def halo_matrix(rules, me, step):
    row = iota((512, 256), 0)
    line, place = line_lanes(iota((1, 256), 1))
    at = place + step - 1
    base = line * 128 + jnp.where(line == 0, 64, 0)
    inside = (at >= 0) & (at < 64)
    value = jnp.where(inside & (row == base + at), 1.0, 0.0)
    side = (line == 3) | (line == 1)
    left = line == 3
    base0, base1, base2, base3 = 64, 128, 256, 384
    if step != 1:
        if step == 0:
            active = side & (place == 0)
            row_a = jnp.where(left, base0, base0 + 63)
            row_b = jnp.where(left, base3, base1)
            pair = (0, 1)
        else:
            active = side & (place == 63)
            row_a = jnp.where(left, base2, base2 + 63)
            row_b = jnp.where(left, base3 + 63, base1 + 63)
            pair = (2, 3)
        fl, sl = weights_of(rules, me, pair[0])
        fr, sr = weights_of(rules, me, pair[1])
        value = value + jnp.where(active & (row == row_a), jnp.where(left, fl, fr), 0.0)
        value = value + jnp.where(active & (row == row_b), jnp.where(left, sl, sr), 0.0)
    return value.astype(BF)


def half_shift(dst, ref, before, after):
    low = iota((C, LANES), 1) < 64
    for t in range(TILES + 1):
        here = tile(ref, t) if t < TILES else after
        prev = tile(ref, t - 1) if t > 0 else before
        mixed = jnp.where(low, here.astype(F32), prev.astype(F32))
        dst[:, t * LANES : (t + 1) * LANES] = pltpu.roll(mixed, 64, 1).astype(BF)


def stack_of(half, ref, start, width):
    at = start * LANES
    size = width * LANES
    return jnp.concatenate(
        [half[:, at : at + size], ref[:, at : at + size], half[:, at + LANES : at + LANES + size]], axis=0
    )


def conv_tiles(weights, half, ref, columns, visit):
    at_left, at_right = lane_masks()
    for chunk in range(TILES // 2):
        taps = dot(weights, stack_of(half, ref, 2 * chunk, 2))
        for part in range(2):
            t = 2 * chunk + part
            lanes = slice(part * LANES, (part + 1) * LANES)
            side = 0.0 if columns is None else pltpu.roll(columns, (LANES - 2 * t) % LANES, 1)
            left = jnp.where(at_left, side, pltpu.roll(taps[0:C, lanes], 1, 1))
            right = jnp.where(at_right, side, pltpu.roll(taps[2 * C : 3 * C, lanes], LANES - 1, 1))
            visit(t, taps[C : 2 * C, lanes] + left + right)


def prepare_kernel(spaces, tables, rules, x_ref, g_ref, wt_ref, d_act, g_side, x_side, route, halo, half):
    me = my_space()
    zero = jnp.zeros((C, LANES), BF)
    half_shift(half, g_ref, zero, zero)

    def visit(t, value):
        d_act[:, t * LANES : (t + 1) * LANES] = value

    conv_tiles(wt_ref[...], half, g_ref, None, visit)
    at_left, at_right = lane_masks()
    for t in range(TILES):
        at = slice(t * LANES, (t + 1) * LANES)
        g = tile(g_ref, t).astype(F32)
        x = tile(x_ref, t).astype(F32)
        g_side[0:C, at] = jnp.where(at_right, 0.0, pltpu.roll(g, LANES - 1, 1)).astype(BF)
        g_side[C : 2 * C, at] = jnp.where(at_left, 0.0, pltpu.roll(g, 1, 1)).astype(BF)
        x_side[0:C, at] = jnp.where(at_left, 0.0, pltpu.roll(x, 1, 1)).astype(BF)
        x_side[C : 2 * C, at] = jnp.where(at_right, 0.0, pltpu.roll(x, LANES - 1, 1)).astype(BF)
    for edge in range(4):
        for step in range(3):
            route[edge, :, step * 256 : (step + 1) * 256] = user_matrix(tables, rules, me, spaces, edge, step)
    for step in range(3):
        halo[:, step * 256 : (step + 1) * 256] = halo_matrix(rules, me, step)


def column_terms(weights, beside):
    stacked = jnp.concatenate([beside[:, s * 256 + 128 : (s + 1) * 256] for s in range(3)], axis=0)
    both = dot(jnp.concatenate([weights[0:C], weights[2 * C : 3 * C]], axis=0), stacked)
    even = (iota((C, LANES), 1) & 1) == 0
    return jnp.where(even, both[0:C], both[C : 2 * C])


def users_values(route, blocks):
    parts = []
    for edge in range(4):
        moved = dot(blocks[edge], route[edge]).astype(BF)
        parts += [moved[:, s * 256 : (s + 1) * 256] for s in range(3)]
    return jnp.concatenate(parts, axis=0)


def middle_kernel(
    spaces, tables, rules, x_ref, a0, a1, a2, a3, d_act, route, halo, wf, back, bias,
    act_ref, d_ref, p0, p1, p2, p3, beside_ref, users_ref, act_lines, d_lines, half,
):
    me = my_space()
    blocks = [a[...] for a in (a0, a1, a2, a3)]
    half_shift(half, x_ref, blocks[0], blocks[2])
    beside = dot(jnp.concatenate(blocks, axis=1), halo[...]).astype(BF)
    beside_ref[...] = beside
    columns = column_terms(wf[...], beside)
    users = users_values(route, blocks)
    users_ref[...] = users
    line_grads = dot(back[...], users)
    rows = line_grads[:, 0:LANES]
    sides = line_grads[:, LANES : 2 * LANES]
    low = iota((C, LANES), 1) < 64
    at_left, at_right = lane_masks()
    at_edge = at_left | at_right
    bias_now = jnp.broadcast_to(bias[...], (C, LANES))
    act_edges = []
    d_edges = []
    ends = {}

    def visit(t, value):
        at = slice(t * LANES, (t + 1) * LANES)
        pre = value + bias_now
        square = pre * pre
        inner = 0.7978845608028654 * pre * (1.0 + 0.044715 * square)
        wave = jnp.tanh(inner)
        cdf = 0.5 + 0.5 * wave
        slope = cdf + 0.5 * pre * (1.0 - wave * wave) * (0.7978845608028654 + 0.1070322243 * square)
        grad = d_act[:, at] + jnp.where(at_edge, pltpu.roll(sides, (LANES - 2 * t) % LANES, 1), 0.0)
        if t == 0:
            grad = grad + jnp.where(low, rows, 0.0)
        if t == TILES - 1:
            grad = grad + jnp.where(low, 0.0, rows)
        act = (pre * cdf).astype(BF)
        d_pre = (grad * slope).astype(BF)
        act_ref[:, at] = act
        d_ref[:, at] = d_pre
        act = act.astype(F32)
        d_pre = d_pre.astype(F32)
        act_edges.append(edge_only(act))
        d_edges.append(edge_only(d_pre))
        if t in (0, TILES - 1):
            ends[t] = (act, d_pre)

    conv_tiles(wf[...], half, x_ref, columns, visit)
    act_l = lines_from(act_edges, ends[0][0], ends[TILES - 1][0])
    d_l = lines_from(d_edges, ends[0][1], ends[TILES - 1][1])
    act_lines[...] = act_l
    d_lines[...] = d_l
    both = jnp.concatenate([act_l, d_l], axis=1)
    for out, matrix in zip((p0, p1, p2, p3), send_matrices(tables, rules, me, spaces)):
        out[...] = dot(both, matrix).astype(BF)


def grads_kernel(
    parts, x_ref, g_ref, act_ref, d_ref, g_side, x_side, beside, users, act_lines, d_lines, wt,
    sums, d_in, half_a, half_d, held_one, held_two, beside_one, beside_two,
):
    zero = jnp.zeros((C, LANES), BF)
    half_shift(half_a, act_ref, zero, zero)
    half_shift(half_d, d_ref, zero, zero)
    width = 4
    one = jnp.zeros((3 * C, 3 * C), F32)
    two = jnp.zeros((3 * C, 3 * C), F32)
    ones = jnp.zeros((C, 1), F32)
    twos = jnp.zeros((C, 1), F32)
    for start in range(0, TILES, width):
        at = slice(start * LANES, (start + width) * LANES)
        g_now = jnp.concatenate([g_side[0:C, at], g_ref[:, at], g_side[C : 2 * C, at]], axis=0)
        x_now = jnp.concatenate([x_side[0:C, at], x_ref[:, at], x_side[C : 2 * C, at]], axis=0)
        two = two + dot_nt(g_now, stack_of(half_a, act_ref, start, width))
        one = one + dot_nt(stack_of(half_d, d_ref, start, width), x_now)
        ones = ones + jnp.sum(d_ref[:, at].astype(F32), axis=1, keepdims=True)
        twos = twos + jnp.sum(g_ref[:, at].astype(F32), axis=1, keepdims=True)
    line, _ = line_lanes(iota((C, 256), 1))
    d_l = d_lines[...].astype(F32)
    by_edge = jnp.concatenate([jnp.where(line == e, d_l, 0.0) for e in range(4)], axis=0).astype(BF)
    side_one = dot_nt(by_edge, jnp.concatenate([beside[:, s * 256 : (s + 1) * 256] for s in range(3)], axis=0))
    held_one[...] = one
    held_two[...] = two
    beside_one[...] = side_one
    beside_two[...] = dot_nt(users[...], act_lines[...])
    share = C // parts
    for tap in range(9):
        a, b = tap // 3, tap % 3
        value_one = held_one[(2 - a) * C : (3 - a) * C, b * C : (b + 1) * C]
        value_two = held_two[b * C : (b + 1) * C, a * C : (a + 1) * C]
        for edge in range(4):
            for step in range(3):
                if tap_of(edge, step) == tap:
                    value_one = value_one + beside_one[edge * C : (edge + 1) * C, step * C : (step + 1) * C]
                    at = ((edge + 2) % 4) * 3 + step
                    value_two = value_two + beside_two[at * C : (at + 1) * C, :]
        tail = jnp.concatenate([ones, twos, jnp.zeros((C, 30), F32)], axis=1)
        whole = jnp.concatenate([value_one, value_two, tail], axis=1)
        for part in range(parts):
            sums[part, tap] = whole[part * share : (part + 1) * share].astype(BF)

    def visit(t, value):
        at = slice(t * LANES, (t + 1) * LANES)
        d_in[:, at] = value + g_ref[:, at].astype(F32)

    conv_tiles(wt[...], half_d, d_ref, None, visit)


def output_kernel(x_ref, act_ref, a0, a1, a2, a3, halo, wf, bias, out, half):
    blocks = [a[...] for a in (a0, a1, a2, a3)]
    half_shift(half, act_ref, blocks[0], blocks[2])
    beside = dot(jnp.concatenate(blocks, axis=1), halo[...]).astype(BF)
    columns = column_terms(wf[...], beside)
    bias_now = jnp.broadcast_to(bias[...], (C, LANES))

    def visit(t, value):
        at = slice(t * LANES, (t + 1) * LANES)
        out[:, at] = (value + bias_now + x_ref[:, at].astype(F32)).astype(BF)

    conv_tiles(wf[...], half, act_ref, columns, visit)


def grad_in_kernel(d_in, a0, a1, a2, a3, route, back, out):
    blocks = [a[...] for a in (a0, a1, a2, a3)]
    line_grads = dot(back[...], users_values(route, blocks))
    rows = line_grads[:, 0:LANES]
    sides = line_grads[:, LANES : 2 * LANES]
    low = iota((C, LANES), 1) < 64
    at_left, at_right = lane_masks()
    at_edge = at_left | at_right
    for t in range(TILES):
        at = slice(t * LANES, (t + 1) * LANES)
        value = d_in[:, at] + jnp.where(at_edge, pltpu.roll(sides, (LANES - 2 * t) % LANES, 1), 0.0)
        if t == 0:
            value = value + jnp.where(low, rows, 0.0)
        if t == TILES - 1:
            value = value + jnp.where(low, 0.0, rows)
        out[:, at] = value.astype(BF)


def call(kernel, outs, specs, args, scratch=(), flops=0, read=0):
    return pl.pallas_call(
        kernel,
        out_shape=[jax.ShapeDtypeStruct(shape, dtype) for shape, dtype in outs],
        in_specs=specs,
        out_specs=[VMEM] * len(outs),
        scratch_shapes=list(scratch),
        compiler_params=pltpu.CompilerParams(vmem_limit_bytes=32 * 1024 * 1024),
        cost_estimate=pl.CostEstimate(flops=flops, bytes_accessed=read, transcendentals=0),
    )(*args)


def exchange(blocks, spaces):
    arrived = []
    for block, offset in zip(blocks, offsets_of(spaces)):
        route = [((i + offset) % spaces, i) for i in range(spaces)]
        arrived.append(lax.ppermute(block, "space", route))
    return arrived


def paired(block, axis, distance):
    size = lax.axis_size(axis)
    return lax.ppermute(block, axis, [(i, i ^ distance) for i in range(size)])


def total_over_devices(sums, parts, spaces):
    me = lax.axis_index("dp")
    span = parts
    held = sums
    while span > 1:
        span //= 2
        upper = (me // span) % 2 == 1
        low, high = held[:span], held[span:]
        keep = jnp.where(upper, high, low)
        give = jnp.where(upper, low, high)
        got = paired(give, "dp", span)
        held = (keep.astype(F32) + got.astype(F32)).astype(BF)
    held = held[0]
    distance = 1
    while distance < spaces:
        got = paired(held, "space", distance)
        distance *= 2
        held = held.astype(F32) + got.astype(F32)
        if distance < spaces:
            held = held.astype(BF)
    return held


def conv_flops():
    return 2 * 9 * C * C * PIX


def on_device(inputs, cotangent, conv_one, bias_one, conv_two, bias_two, neighbours, corner_rule):
    parts = lax.axis_size("dp")
    spaces = lax.axis_size("space")
    x = inputs.reshape(C, PIX)
    g = cotangent.reshape(C, PIX)
    line = ((C, LANES), BF)
    image = ((C, PIX), BF)

    def forward(w):
        return w.reshape(3, 3, C, C).transpose(1, 2, 0, 3).reshape(3 * C, 3 * C)

    def backward(w):
        return w.reshape(3, 3, C, C)[::-1, ::-1].transpose(1, 3, 0, 2).reshape(3 * C, 3 * C)

    def returning(w):
        taps = [w[tap_of((edge + 2) % 4, step)].T for edge in range(4) for step in range(3)]
        return jnp.concatenate(taps, axis=1)

    sent = call(
        functools.partial(send_kernel, spaces), [line] * 4, [SMEM, SMEM, VMEM, VMEM],
        (neighbours, corner_rule, x, g), flops=10**6, read=10**6,
    )
    arrived = exchange(sent, spaces)
    half = pltpu.VMEM((C, PIX + LANES), BF)
    d_act, g_side, x_side, route, halo = call(
        functools.partial(prepare_kernel, spaces),
        [((C, PIX), F32), ((2 * C, PIX), BF), ((2 * C, PIX), BF), ((4, LANES, 768), BF), ((512, 768), BF)],
        [SMEM, SMEM, VMEM, VMEM, VMEM],
        (neighbours, corner_rule, x, g, backward(conv_two)), [half], flops=conv_flops(), read=4 * 10**6,
    )
    middle = call(
        functools.partial(middle_kernel, spaces),
        [image, image] + [line] * 4 + [((C, 768), BF), ((12 * C, 256), BF), ((C, 256), BF), ((C, 256), BF)],
        [SMEM, SMEM] + [VMEM] * 11,
        (neighbours, corner_rule, x, *arrived, d_act, route, halo, forward(conv_one), returning(conv_two),
         bias_one.reshape(C, 1)),
        [half], flops=conv_flops(), read=4 * 10**6,
    )
    act, d_pre = middle[:2]
    beside, users, act_lines, d_lines = middle[6:]
    again = exchange(middle[2:6], spaces)
    sums, d_in = call(
        functools.partial(grads_kernel, parts), [((parts, 9, C // parts, LANES), BF), ((C, PIX), F32)], [VMEM] * 11,
        (x, g, act, d_pre, g_side, x_side, beside, users, act_lines, d_lines, backward(conv_one)),
        [half, half, pltpu.VMEM((3 * C, 3 * C), F32), pltpu.VMEM((3 * C, 3 * C), F32),
         pltpu.VMEM((4 * C, 3 * C), F32), pltpu.VMEM((12 * C, C), F32)],
        flops=3 * conv_flops(), read=6 * 10**6,
    )
    (output,) = call(
        output_kernel, [image], [VMEM] * 9,
        (x, act, *again, halo, forward(conv_two), bias_two.reshape(C, 1)), [half],
        flops=conv_flops(), read=3 * 10**6,
    )
    (grad_in,) = call(
        grad_in_kernel, [image], [VMEM] * 7, (d_in, *again, route, returning(conv_one)),
        flops=10**6, read=3 * 10**6,
    )
    total = total_over_devices(sums, parts, spaces)
    shape = inputs.shape
    return (
        output.reshape(shape),
        grad_in.reshape(shape),
        total[:, :, 0:C],
        total[0, :, 2 * C],
        total[:, :, C : 2 * C],
        total[0, :, 2 * C + 1],
    )


def solution(mesh):
    tiles = P("dp", "space", None, None)
    return jax.shard_map(
        on_device,
        mesh=mesh,
        in_specs=(tiles, tiles, P(), P(), P(), P(), P(), P()),
        out_specs=(tiles, tiles, P(None, "dp", None), P("dp"), P(None, "dp", None), P("dp")),
        check_vma=False,
    )
```

profile of v0, /device:TPU:0, one launch (start us, length us, event | category | flops | bytes accessed | tf_op | source)
XLA Modules:
  0.0 58.4 jit_solution(4949337911579204261)
XLA Ops:
  0.6 0.8 %copy.56.tables = s32[16,4,3]{2,1,0:T(4,128)S(1)} copy(s32[16,4,3]{0,1,2:T(4,128)} %param.14) | data formatting | bytes 1536 | tf_op args[6]
  1.4 0.1 copy.57.rules
  1.5 1.0 %copy-done = bf16[1,1,48,4096]{3,2,1,0:T(8,128)(2,1)S(1)} copy-done((bf16[1,1,48,4096]{3,2,1,0:T(8,128)(2,1)S(1)}, bf16[1,1,48,4096]{3,2,1,0:T(8,128)(2,1)}, u32[]{:S(2)}) %copy-start) | copy-done | bytes 393240
  2.5 1.0 %copy-done.2 = bf16[1,1,48,4096]{3,2,1,0:T(8,128)(2,1)S(1)} copy-done((bf16[1,1,48,4096]{3,2,1,0:T(8,128)(2,1)S(1)}, bf16[1,1,48,4096]{3,2,1,0:T(8,128)(2,1)}, u32[]{:S(2)}) %copy-start.2) | copy-done | bytes 393240
  3.5 1.7 %shard_map.127 = (bf16[48,128]{1,0:T(8,128)(2,1)S(1)}, bf16[48,128]{1,0:T(8,128)(2,1)S(1)}, bf16[48,128]{1,0:T(8,128)(2,1)S(1)}, bf16[48,128]{1,0:T(8,128)(2,1)S(1)}) custom-call(s32[16,4,3]{2,1,0:T(4,128)S(1)} %copy.56.tables, s32[16,4]{1,0:T(8,128)S(1)} %copy.57.rules, bf16[48,4096]{1,0:T(8,128)(2,1)S(1)} %bitcast.66, bf16[48,4096]{1,0:T(8,128)(2,1)S(1)} %bitcast.71), custom_call_target="tpu_custom_call" | custom-call | flops 1000000 | bytes 1000000 | tf_op jit(solution)/shard_map/pallas_call | solution.py:377
  5.2 0.5 collective-permute-start
  5.7 4.7 %collective-permute-start.1 = (bf16[48,128]{1,0:T(8,128)(2,1)S(1)}, bf16[48,128]{1,0:T(8,128)(2,1)S(1)}, u32[]{:S(2)}, u32[]{:S(2)}) collective-permute-start(bf16[48,128]{1,0:T(8,128)(2,1)S(1)} %get-tuple-element.28), channel_id=1, source_target_pairs={{4,0},{5,1},{6,2},{7,3},{8,4},{9,5},{10,6},{11,7},{12,8},{13,9},{1... | collective-permute-start | bytes 36872 | tf_op jit(solution)/shard_map/ppermute | solution.py:392
  10.4 2.3 %collective-permute-start.2 = (bf16[48,128]{1,0:T(8,128)(2,1)S(1)}, bf16[48,128]{1,0:T(8,128)(2,1)S(1)}, u32[]{:S(2)}, u32[]{:S(2)}) collective-permute-start(bf16[48,128]{1,0:T(8,128)(2,1)S(1)} %get-tuple-element.29), channel_id=1, source_target_pairs={{1,0},{2,1},{3,2},{4,3},{5,4},{6,5},{7,6},{8,7},{9,8},{10,9},{11,1... | collective-permute-start | bytes 36872 | tf_op jit(solution)/shard_map/ppermute | solution.py:392
  12.7 0.1 copy.89
  12.8 0.1 copy.61
  12.9 0.7 %copy-done.7 = bf16[9,48,48]{2,1,0:T(8,128)(2,1)S(1)} copy-done((bf16[9,48,48]{2,1,0:T(8,128)(2,1)S(1)}, bf16[9,48,48]{2,1,0:T(8,128)(2,1)}, u32[]{:S(2)}) %copy-start.7) | copy-done | bytes 41496
  13.7 0.1 copy.72
  13.8 0.1 copy.73
  13.8 0.1 copy.74
  13.9 0.1 copy.75
  14.0 0.1 copy.76
  14.1 0.1 copy.77
  14.2 0.1 copy.70
  14.3 0.1 copy.71
  14.4 0.2 copy.44
  14.6 0.8 %rev.6 = bf16[3,3,48,48]{2,0,3,1:T(4,128)(2,1)S(1)} reverse(bf16[3,3,48,48]{2,0,3,1:T(4,128)(2,1)S(1)} %copy.44), dimensions={0,1} | reverse | bytes 82944 | tf_op jit(solution)/shard_map/rev | solution.py:440
  15.4 0.1 reshape.53.wt_ref
  15.6 0.1 reshape.55.wf
  15.7 0.4 copy-done.16
  16.1 0.1 copy.58.bias
  16.2 0.8 %rev.7 = bf16[3,3,48,48]{2,0,3,1:T(4,128)(2,1)S(1)} reverse(bf16[3,3,48,48]{2,0,3,1:T(4,128)(2,1)S(1)} %copy.61), dimensions={0,1} | reverse | bytes 82944 | tf_op jit(solution)/shard_map/rev | solution.py:440
  17.0 0.8 %reshape.60.wt = bf16[144,144]{1,0:T(8,128)(2,1)} reshape(bf16[3,48,3,48]{3,2,1,0:T(4,128)(2,1)S(1)} %bitcast.81) | data formatting | bytes 82944 | tf_op jit(solution)/shard_map/reshape | solution.py:440
  17.8 0.1 concatenate.6.back
  17.9 2.8 %shard_map.128 = (f32[48,4096]{1,0:T(8,128)S(1)}, bf16[96,4096]{1,0:T(8,128)(2,1)S(1)}, bf16[96,4096]{1,0:T(8,128)(2,1)S(1)}, bf16[4,128,768]{2,1,0:T(8,128)(2,1)S(1)}, bf16[512,768]{1,0:T(8,128)(2,1)S(1)}) custom-call(s32[16,4,3]{2,1,0:T(4,128)S(1)} %copy.56.tables, s32[16,4]{1,0:T(8,128)S(1)} %copy.57.rules, bf16[48,4096]{1,0:T(8,128)(2,1)S(1)} %bitcast.67, ...), custom_call_target="tpu_custom_call" | custom-call | flops 169869312 | bytes 4000000 | tf_op jit(solution)/shard_map/pallas_call | solution.py:377
  20.8 3.7 %shard_map.129 = (bf16[48,4096]{1,0:T(8,128)(2,1)S(1)}, bf16[48,4096]{1,0:T(8,128)(2,1)S(1)}, bf16[48,128]{1,0:T(8,128)(2,1)}, bf16[48,128]{1,0:T(8,128)(2,1)}, ...) custom-call(s32[16,4,3]{2,1,0:T(4,128)S(1)} %copy.56.tables, ...), custom_call_target="tpu_custom_call" | custom-call | flops 169869312 | bytes 4000000 | tf_op jit(solution)/shard_map/pallas_call | solution.py:377
  24.5 1.6 %shard_map.131 = (bf16[2,9,24,128]{3,2,1,0:T(8,128)(2,1)S(1)}, f32[48,4096]{1,0:T(8,128)S(1)}) custom-call(bf16[48,4096]{1,0:T(8,128)(2,1)S(1)} %bitcast.69, bf16[48,4096]{1,0:T(8,128)(2,1)S(1)} %bitcast.73, bf16[48,4096]{1,0:T(8,128)(2,1)S(1)} %get-tuple-element.34.act_ref, bf16[48,4096]{1,0:T(8,128)(2,1)S(1)} %get-tuple-element.39.d_ref, ...), custom_call_target="tpu_custom_call" | custom-call | flops 509607936 | bytes 6000000 | tf_op jit(solution)/shard_map/pallas_call | solution.py:377
  26.1 1.8 %collective-permute-start.8 = (bf16[1,9,24,128]{3,2,1,0:T(8,128)(2,1)S(1)}, bf16[1,9,24,128]{3,2,1,0:T(8,128)(2,1)S(1)}, u32[]{:S(2)}, u32[]{:S(2)}) collective-permute-start(bf16[1,9,24,128]{3,2,1,0:T(8,128)(2,1)S(1)} %broadcast_select_fusion), channel_id=1, source_target_pairs={{0,16},{16,0},{1,17},{17,1},{2,18},{18,2},{3,19},{19,3},{4,20},{20... | collective-permute-start | bytes 165896 | tf_op jit(solution)/shard_map/ppermute | solution.py:398
  27.9 2.4 %collective-permute-done.8 = bf16[1,9,24,128]{3,2,1,0:T(8,128)(2,1)S(1)} collective-permute-done((bf16[1,9,24,128]{3,2,1,0:T(8,128)(2,1)S(1)}, bf16[1,9,24,128]{3,2,1,0:T(8,128)(2,1)S(1)}, u32[]{:S(2)}, u32[]{:S(2)}) %collective-permute-start.8) | collective-permute-done | bytes 55328 | tf_op jit(solution)/shard_map/ppermute | solution.py:398
  30.3 0.1 collective-permute-start.9
  30.4 1.2 %collective-permute-done.9 = bf16[9,24,128]{2,1,0:T(8,128)(2,1)S(1)} collective-permute-done((bf16[9,24,128]{2,1,0:T(8,128)(2,1)S(1)}, bf16[9,24,128]{2,1,0:T(8,128)(2,1)S(1)}, u32[]{:S(2)}, u32[]{:S(2)}) %collective-permute-start.9) | collective-permute-done | bytes 55328 | tf_op jit(solution)/shard_map/ppermute | solution.py:398
  31.7 0.7 %collective-permute-start.10 = (bf16[9,24,128]{2,1,0:T(8,128)(2,1)S(1)}, bf16[9,24,128]{2,1,0:T(8,128)(2,1)S(1)}, u32[]{:S(2)}, u32[]{:S(2)}) collective-permute-start(bf16[9,24,128]{2,1,0:T(8,128)(2,1)S(1)} %add_convert_fusion.2), channel_id=1, source_target_pairs={{0,2},{1,3},{2,0},{3,1},{4,6},{5,7},{6,4},{7,5},{8,10},{9,11},{10,... | collective-permute-start | bytes 165896 | tf_op jit(solution)/shard_map/ppermute | solution.py:398
  32.3 3.6 %collective-permute-done.10 = bf16[9,24,128]{2,1,0:T(8,128)(2,1)S(1)} collective-permute-done((bf16[9,24,128]{2,1,0:T(8,128)(2,1)S(1)}, bf16[9,24,128]{2,1,0:T(8,128)(2,1)S(1)}, u32[]{:S(2)}, u32[]{:S(2)}) %collective-permute-start.10) | collective-permute-done | bytes 55328 | tf_op jit(solution)/shard_map/ppermute | solution.py:398
  35.9 0.1 collective-permute-start.11
  36.0 0.1 collective-permute-start.4
  36.1 3.9 %collective-permute-start.5 = (bf16[48,128]{1,0:T(8,128)(2,1)}, bf16[48,128]{1,0:T(8,128)(2,1)S(1)}, u32[]{:S(2)}, u32[]{:S(2)}) collective-permute-start(bf16[48,128]{1,0:T(8,128)(2,1)} %get-tuple-element.36), channel_id=1, source_target_pairs={{4,0},{5,1},{6,2},{7,3},{8,4},{9,5},{10,6},{11,7},{12,8},{13,9},{1... | collective-permute-start | bytes 36872 | tf_op jit(solution)/shard_map/ppermute | solution.py:392
  39.9 2.3 %collective-permute-start.6 = (bf16[48,128]{1,0:T(8,128)(2,1)}, bf16[48,128]{1,0:T(8,128)(2,1)S(1)}, u32[]{:S(2)}, u32[]{:S(2)}) collective-permute-start(bf16[48,128]{1,0:T(8,128)(2,1)} %get-tuple-element.37), channel_id=1, source_target_pairs={{1,0},{2,1},{3,2},{4,3},{5,4},{6,5},{7,6},{8,7},{9,8},{10,9},{11,1... | collective-permute-start | bytes 36872 | tf_op jit(solution)/shard_map/ppermute | solution.py:392
  42.2 0.6 %add_convert_fusion = bf16[9,24,128]{2,1,0:T(8,128)(2,1)} fusion(bf16[9,24,128]{2,1,0:T(8,128)(2,1)S(1)} %collective-permute-done.11, bf16[9,24,128]{2,1,0:T(8,128)(2,1)S(1)} %add_convert_fusion.1), kind=kLoop, calls=%fused_computation.3 | loop fusion | flops 110592 | bytes 165888 | tf_op jit(solution)/shard_map/convert_element_type | solution.py:420
  42.9 2.5 %collective-permute-start.12 = (bf16[9,24,128]{2,1,0:T(8,128)(2,1)}, bf16[9,24,128]{2,1,0:T(8,128)(2,1)}, u32[]{:S(2)}, u32[]{:S(2)}) collective-permute-start(bf16[9,24,128]{2,1,0:T(8,128)(2,1)} %add_convert_fusion), channel_id=1, source_target_pairs={{0,8},{1,9},{2,10},{3,11},{4,12},{5,13},{6,14},{7,15},{8,0},{9,1},... | collective-permute-start | bytes 165896 | tf_op jit(solution)/shard_map/ppermute | solution.py:398
  45.4 0.6 %fusion.2 = (bf16[1,48,48]{2,1,0:T(8,128)(2,1)S(1)}, bf16[1,48,48]{2,1,0:T(8,128)(2,1)S(1)}, bf16[1,48,48]{2,1,0:T(8,128)(2,1)S(1)}, bf16[1,48,48]{2,1,0:T(8,128...) fusion(bf16[9,48,48]{2,1,0:T(8,128)(2,1)S(1)} %copy-done.6), kind=kLoop, calls=%fused_computation.12 | loop fusion | bytes 73728 | tf_op jit(solution)/shard_map/slice | solution.py:443
  46.0 0.7 %copy.88 = bf16[3,3,48,48]{3,0,2,1:T(4,128)(2,1)} copy(bf16[3,3,48,48]{3,2,1,0:T(8,128)(2,1)S(1)} %bitcast.77) | data formatting | bytes 82944 | tf_op jit(solution)/shard_map/reshape | solution.py:440
  46.8 0.1 copy.78
  46.8 0.7 %copy.79 = bf16[1,48,48]{1,2,0:T(8,128)(2,1)} copy(bf16[1,48,48]{2,1,0:T(8,128)(2,1)S(1)} %get-tuple-element.58) | data formatting | bytes 9216
  47.5 0.1 copy.80
  47.6 0.1 copy.81
  47.7 0.7 %copy.82 = bf16[1,48,48]{1,2,0:T(8,128)(2,1)} copy(bf16[1,48,48]{2,1,0:T(8,128)(2,1)S(1)} %get-tuple-element.55) | data formatting | bytes 9216
  48.4 0.7 %copy.83 = bf16[1,48,48]{1,2,0:T(8,128)(2,1)} copy(bf16[1,48,48]{2,1,0:T(8,128)(2,1)S(1)} %get-tuple-element.54) | data formatting | bytes 9216
  49.1 0.7 %copy.84 = bf16[1,48,48]{1,2,0:T(8,128)(2,1)} copy(bf16[1,48,48]{2,1,0:T(8,128)(2,1)S(1)} %get-tuple-element.53) | data formatting | bytes 9216
  49.8 0.7 %copy.85 = bf16[1,48,48]{1,2,0:T(8,128)(2,1)} copy(bf16[1,48,48]{2,1,0:T(8,128)(2,1)S(1)} %get-tuple-element.52) | data formatting | bytes 9216
  50.5 0.1 reshape.57.wf
  50.6 0.6 %copy-done.17 = f32[48]{0:T(128)S(1)} copy-done((f32[48]{0:T(128)S(1)}, f32[48]{0:T(128)}, u32[]{:S(2)}) %copy-start.17) | copy-done | bytes 216
  51.3 0.1 copy.60.bias
  51.4 0.6 %copy-done.11 = bf16[1,48,48]{1,2,0:T(8,128)(2,1)S(1)} copy-done((bf16[1,48,48]{1,2,0:T(8,128)(2,1)S(1)}, bf16[1,48,48]{1,2,0:T(8,128)(2,1)}, u32[]{:S(2)}) %copy-start.11) | copy-done | bytes 4632
  52.0 0.1 copy-done.10
  52.1 0.8 %concatenate.7.back = bf16[48,576]{1,0:T(8,128)(2,1)S(1)} concatenate(bf16[48,48]{1,0:T(8,128)(2,1)S(1)} %bitcast.92, bf16[48,48]{1,0:T(8,128)(2,1)S(1)} %bitcast.104, bf16[48,48]{1,0:T(8,128)(2,1)S(1)} %bitcast.94, bf16[48,48]{1,0:T(8,128)(2,1)S(1)} %bitcast.96, bf16[48,48]{1,0:T(8,128)(2,1)S(1)} %bitcast.105, bf16[48,48]{1,0:T(8,128)(2,1)S(1)} %bitcast.93, ...), dimensions={1} | concatenate | bytes 110592 | tf_op jit(solution)/shard_map/concatenate | solution.py:444
  53.0 1.4 %shard_map.132 = bf16[48,4096]{1,0:T(8,128)(2,1)} custom-call(f32[48,4096]{1,0:T(8,128)S(1)} %get-tuple-element.46.d_in, bf16[48,128]{1,0:T(8,128)(2,1)S(1)} %collective-permute-done.4.a0, bf16[48,128]{1,0:T(8,128)(2,1)S(1)} %collective-permute-done.5.a1, bf16[48,128]{1,0:T(8,128)(2,1)S(1)} %collective-permute-done.6.a2, ...), custom_call_target="tpu_custom_call" | custom-call | flops 1000000 | bytes 3000000 | tf_op jit(solution)/shard_map/pallas_call | solution.py:377
  54.4 1.7 %shard_map.130 = bf16[48,4096]{1,0:T(8,128)(2,1)} custom-call(bf16[48,4096]{1,0:T(8,128)(2,1)S(1)} %bitcast.70, bf16[48,4096]{1,0:T(8,128)(2,1)S(1)} %get-tuple-element.34.act_ref, bf16[48,128]{1,0:T(8,128)(2,1)S(1)} %collective-permute-done.4.a0, bf16[48,128]{1,0:T(8,128)(2,1)S(1)} %collective-permute-done.5.a1, ...), custom_call_target="tpu_custom_call" | custom-call | flops 169869312 | bytes 3000000 | tf_op jit(solution)/shard_map/pallas_call | solution.py:377
  56.1 0.9 %convert_add_fusion = f32[9,24,128]{2,1,0:T(8,128)S(1)} fusion(bf16[9,24,128]{2,1,0:T(8,128)(2,1)} %collective-permute-done.12, bf16[9,24,128]{2,1,0:T(8,128)(2,1)} %add_convert_fusion), kind=kLoop, calls=%fused_computation.2 | loop fusion | flops 82944 | bytes 221184 | tf_op jit(solution)/shard_map/add | solution.py:418
  57.0 0.7 %fusion.1 = (f32[9,24,48]{2,1,0:T(8,128)}, f32[9,24,48]{2,1,0:T(8,128)}) fusion(f32[9,24,128]{2,1,0:T(8,128)S(1)} %convert_add_fusion), kind=kLoop, calls=%fused_computation.11 | loop fusion | bytes 165888 | tf_op jit(solution)/shard_map/slice | solution.py:492
  57.7 0.7 %slice_reduce_fusion = (f32[24]{0:T(128)}, f32[24]{0:T(128)}) fusion(f32[9,24,128]{2,1,0:T(8,128)S(1)} %convert_add_fusion), kind=kLoop, calls=%fused_computation.9 | loop fusion | bytes 384 | tf_op jit(solution)/shard_map/slice | solution.py:493
  (46 shorter events, 0.2 us)
Async XLA Ops:
  0.6 0.8 %copy-start.15 = (s32[16,4]{0,1:T(4,128)S(1)}, s32[16,4]{0,1:T(4,128)}, u32[]{:S(2)}) copy-start(s32[16,4]{0,1:T(4,128)} %param.15) | copy-start | bytes 772
  1.5 1.0 %copy-start = (bf16[1,1,48,4096]{3,2,1,0:T(8,128)(2,1)S(1)}, bf16[1,1,48,4096]{3,2,1,0:T(8,128)(2,1)}, u32[]{:S(2)}) copy-start(bf16[1,1,48,4096]{3,2,1,0:T(8,128)(2,1)} %param.8) | copy-start | bytes 1179652
  2.5 1.0 %copy-start.2 = (bf16[1,1,48,4096]{3,2,1,0:T(8,128)(2,1)S(1)}, bf16[1,1,48,4096]{3,2,1,0:T(8,128)(2,1)}, u32[]{:S(2)}) copy-start(bf16[1,1,48,4096]{3,2,1,0:T(8,128)(2,1)} %param.9) | copy-start | bytes 1179652
  3.5 9.2 %copy-start.5 = (bf16[9,48,48]{2,1,0:T(8,128)(2,1)S(1)}, bf16[9,48,48]{2,1,0:T(8,128)(2,1)}, u32[]{:S(2)}) copy-start(bf16[9,48,48]{2,1,0:T(8,128)(2,1)} %param.10) | copy-start | bytes 124420
  5.2 15.5 %collective-permute-start = (bf16[48,128]{1,0:T(8,128)(2,1)S(1)}, bf16[48,128]{1,0:T(8,128)(2,1)S(1)}, u32[]{:S(2)}, u32[]{:S(2)}) collective-permute-start(bf16[48,128]{1,0:T(8,128)(2,1)S(1)} %get-tuple-element.27), channel_id=1, source_target_pairs={{15,0},{0,1},{1,2},{2,3},{3,4},{4,5},{5,6},{6,7},{7,8},{8,9},{9,10... | collective-permute-start | bytes 36872 | tf_op jit(solution)/shard_map/ppermute | solution.py:392
  5.7 15.0 %collective-permute-start.1 = (bf16[48,128]{1,0:T(8,128)(2,1)S(1)}, bf16[48,128]{1,0:T(8,128)(2,1)S(1)}, u32[]{:S(2)}, u32[]{:S(2)}) collective-permute-start(bf16[48,128]{1,0:T(8,128)(2,1)S(1)} %get-tuple-element.28), channel_id=1, source_target_pairs={{4,0},{5,1},{6,2},{7,3},{8,4},{9,5},{10,6},{11,7},{12,8},{13,9},{1... | collective-permute-start | bytes 36872 | tf_op jit(solution)/shard_map/ppermute | solution.py:392
  10.4 10.4 %collective-permute-start.2 = (bf16[48,128]{1,0:T(8,128)(2,1)S(1)}, bf16[48,128]{1,0:T(8,128)(2,1)S(1)}, u32[]{:S(2)}, u32[]{:S(2)}) collective-permute-start(bf16[48,128]{1,0:T(8,128)(2,1)S(1)} %get-tuple-element.29), channel_id=1, source_target_pairs={{1,0},{2,1},{3,2},{4,3},{5,4},{6,5},{7,6},{8,7},{9,8},{10,9},{11,1... | collective-permute-start | bytes 36872 | tf_op jit(solution)/shard_map/ppermute | solution.py:392
  12.7 8.1 %collective-permute-start.3 = (bf16[48,128]{1,0:T(8,128)(2,1)S(1)}, bf16[48,128]{1,0:T(8,128)(2,1)S(1)}, u32[]{:S(2)}, u32[]{:S(2)}) collective-permute-start(bf16[48,128]{1,0:T(8,128)(2,1)S(1)} %get-tuple-element.30), channel_id=1, source_target_pairs={{12,0},{13,1},{14,2},{15,3},{0,4},{1,5},{2,6},{3,7},{4,8},{5,9},{6... | collective-permute-start | bytes 36872 | tf_op jit(solution)/shard_map/ppermute | solution.py:392
  12.8 0.9 %copy-start.7 = (bf16[9,48,48]{2,1,0:T(8,128)(2,1)S(1)}, bf16[9,48,48]{2,1,0:T(8,128)(2,1)}, u32[]{:S(2)}) copy-start(bf16[9,48,48]{2,1,0:T(8,128)(2,1)} %param.12) | copy-start | bytes 124420
  15.4 0.7 %copy-start.16 = (f32[48]{0:T(128)S(1)}, f32[48]{0:T(128)}, u32[]{:S(2)}) copy-start(f32[48]{0:T(128)} %param.11) | copy-start | bytes 580
  15.6 2.3 %copy-start.3 = (bf16[1,1,48,4096]{3,2,1,0:T(8,128)(2,1)S(1)}, bf16[1,1,48,4096]{3,2,1,0:T(8,128)(2,1)}, u32[]{:S(2)}) copy-start(bf16[1,1,48,4096]{3,2,1,0:T(8,128)(2,1)} %param.9) | copy-start | bytes 1179652
  15.7 2.2 %copy-start.1 = (bf16[1,1,48,4096]{3,2,1,0:T(8,128)(2,1)S(1)}, bf16[1,1,48,4096]{3,2,1,0:T(8,128)(2,1)}, u32[]{:S(2)}) copy-start(bf16[1,1,48,4096]{3,2,1,0:T(8,128)(2,1)} %param.8) | copy-start | bytes 1179652
  20.8 3.7 %copy-start.4 = (bf16[144,144]{1,0:T(8,128)(2,1)S(1)}, bf16[144,144]{1,0:T(8,128)(2,1)}, u32[]{:S(2)}) copy-start(bf16[144,144]{1,0:T(8,128)(2,1)} %reshape.60.wt) | copy-start | bytes 124420
  26.1 4.2 %collective-permute-start.8 = (bf16[1,9,24,128]{3,2,1,0:T(8,128)(2,1)S(1)}, bf16[1,9,24,128]{3,2,1,0:T(8,128)(2,1)S(1)}, u32[]{:S(2)}, u32[]{:S(2)}) collective-permute-start(bf16[1,9,24,128]{3,2,1,0:T(8,128)(2,1)S(1)} %broadcast_select_fusion), channel_id=1, source_target_pairs={{0,16},{16,0},{1,17},{17,1},{2,18},{18,2},{3,19},{19,3},{4,20},{20... | collective-permute-start | bytes 165896 | tf_op jit(solution)/shard_map/ppermute | solution.py:398
  30.3 1.3 %collective-permute-start.9 = (bf16[9,24,128]{2,1,0:T(8,128)(2,1)S(1)}, bf16[9,24,128]{2,1,0:T(8,128)(2,1)S(1)}, u32[]{:S(2)}, u32[]{:S(2)}) collective-permute-start(bf16[9,24,128]{2,1,0:T(8,128)(2,1)S(1)} %fusion), channel_id=1, source_target_pairs={{0,1},{1,0},{2,3},{3,2},{4,5},{5,4},{6,7},{7,6},{8,9},{9,8},{10,11... | collective-permute-start | bytes 165896 | tf_op jit(solution)/shard_map/ppermute | solution.py:398
  31.7 4.2 %collective-permute-start.10 = (bf16[9,24,128]{2,1,0:T(8,128)(2,1)S(1)}, bf16[9,24,128]{2,1,0:T(8,128)(2,1)S(1)}, u32[]{:S(2)}, u32[]{:S(2)}) collective-permute-start(bf16[9,24,128]{2,1,0:T(8,128)(2,1)S(1)} %add_convert_fusion.2), channel_id=1, source_target_pairs={{0,2},{1,3},{2,0},{3,1},{4,6},{5,7},{6,4},{7,5},{8,10},{9,11},{10,... | collective-permute-start | bytes 165896 | tf_op jit(solution)/shard_map/ppermute | solution.py:398
  35.9 9.5 %copy-start.6 = (bf16[9,48,48]{2,1,0:T(8,128)(2,1)S(1)}, bf16[9,48,48]{2,1,0:T(8,128)(2,1)}, u32[]{:S(2)}) copy-start(bf16[9,48,48]{2,1,0:T(8,128)(2,1)} %param.10) | copy-start | bytes 124420
  35.9 6.3 %collective-permute-start.11 = (bf16[9,24,128]{2,1,0:T(8,128)(2,1)S(1)}, bf16[9,24,128]{2,1,0:T(8,128)(2,1)S(1)}, u32[]{:S(2)}, u32[]{:S(2)}) collective-permute-start(bf16[9,24,128]{2,1,0:T(8,128)(2,1)S(1)} %add_convert_fusion.1), channel_id=1, source_target_pairs={{0,4},{1,5},{2,6},{3,7},{4,0},{5,1},{6,2},{7,3},{8,12},{9,13},{10,... | collective-permute-start | bytes 165896 | tf_op jit(solution)/shard_map/ppermute | solution.py:398
  36.0 16.9 %collective-permute-start.4 = (bf16[48,128]{1,0:T(8,128)(2,1)}, bf16[48,128]{1,0:T(8,128)(2,1)S(1)}, u32[]{:S(2)}, u32[]{:S(2)}) collective-permute-start(bf16[48,128]{1,0:T(8,128)(2,1)} %get-tuple-element.35), channel_id=1, source_target_pairs={{15,0},{0,1},{1,2},{2,3},{3,4},{4,5},{5,6},{6,7},{7,8},{8,9},{9,10... | collective-permute-start | bytes 36872 | tf_op jit(solution)/shard_map/ppermute | solution.py:392
  36.1 16.9 %collective-permute-start.5 = (bf16[48,128]{1,0:T(8,128)(2,1)}, bf16[48,128]{1,0:T(8,128)(2,1)S(1)}, u32[]{:S(2)}, u32[]{:S(2)}) collective-permute-start(bf16[48,128]{1,0:T(8,128)(2,1)} %get-tuple-element.36), channel_id=1, source_target_pairs={{4,0},{5,1},{6,2},{7,3},{8,4},{9,5},{10,6},{11,7},{12,8},{13,9},{1... | collective-permute-start | bytes 36872 | tf_op jit(solution)/shard_map/ppermute | solution.py:392
  39.9 13.0 %collective-permute-start.6 = (bf16[48,128]{1,0:T(8,128)(2,1)}, bf16[48,128]{1,0:T(8,128)(2,1)S(1)}, u32[]{:S(2)}, u32[]{:S(2)}) collective-permute-start(bf16[48,128]{1,0:T(8,128)(2,1)} %get-tuple-element.37), channel_id=1, source_target_pairs={{1,0},{2,1},{3,2},{4,3},{5,4},{6,5},{7,6},{8,7},{9,8},{10,9},{11,1... | collective-permute-start | bytes 36872 | tf_op jit(solution)/shard_map/ppermute | solution.py:392
  42.2 10.7 %collective-permute-start.7 = (bf16[48,128]{1,0:T(8,128)(2,1)S(1)}, bf16[48,128]{1,0:T(8,128)(2,1)S(1)}, u32[]{:S(2)}, u32[]{:S(2)}) collective-permute-start(bf16[48,128]{1,0:T(8,128)(2,1)S(1)} %get-tuple-element.38), channel_id=1, source_target_pairs={{12,0},{13,1},{14,2},{15,3},{0,4},{1,5},{2,6},{3,7},{4,8},{5,9},{6... | collective-permute-start | bytes 36872 | tf_op jit(solution)/shard_map/ppermute | solution.py:392
  42.9 3.1 %copy-start.8 = (bf16[9,48,48]{2,1,0:T(8,128)(2,1)S(1)}, bf16[9,48,48]{2,1,0:T(8,128)(2,1)}, u32[]{:S(2)}) copy-start(bf16[9,48,48]{2,1,0:T(8,128)(2,1)} %param.12) | copy-start | bytes 124420
  42.9 13.2 %collective-permute-start.12 = (bf16[9,24,128]{2,1,0:T(8,128)(2,1)}, bf16[9,24,128]{2,1,0:T(8,128)(2,1)}, u32[]{:S(2)}, u32[]{:S(2)}) collective-permute-start(bf16[9,24,128]{2,1,0:T(8,128)(2,1)} %add_convert_fusion), channel_id=1, source_target_pairs={{0,8},{1,9},{2,10},{3,11},{4,12},{5,13},{6,14},{7,15},{8,0},{9,1},... | collective-permute-start | bytes 165896 | tf_op jit(solution)/shard_map/ppermute | solution.py:398
  46.0 0.7 %copy-start.14 = (bf16[1,48,48]{2,1,0:T(8,128)(2,1)S(1)}, bf16[1,48,48]{2,1,0:T(8,128)(2,1)}, u32[]{:S(2)}) copy-start(bf16[1,48,48]{2,1,0:T(8,128)(2,1)} %get-tuple-element.59) | copy-start | bytes 13828
  46.0 1.6 %copy-start.13 = (bf16[1,48,48]{2,1,0:T(8,128)(2,1)S(1)}, bf16[1,48,48]{2,1,0:T(8,128)(2,1)}, u32[]{:S(2)}) copy-start(bf16[1,48,48]{2,1,0:T(8,128)(2,1)} %get-tuple-element.56) | copy-start | bytes 13828
  46.8 3.7 %copy-start.9 = (bf16[3,3,48,48]{3,0,2,1:T(4,128)(2,1)S(1)}, bf16[3,3,48,48]{3,0,2,1:T(4,128)(2,1)}, u32[]{:S(2)}) copy-start(bf16[3,3,48,48]{3,0,2,1:T(4,128)(2,1)} %copy.88) | copy-start | bytes 124420
  50.6 0.7 %copy-start.17 = (f32[48]{0:T(128)S(1)}, f32[48]{0:T(128)}, u32[]{:S(2)}) copy-start(f32[48]{0:T(128)} %param.13) | copy-start | bytes 580
  51.3 0.7 %copy-start.11 = (bf16[1,48,48]{1,2,0:T(8,128)(2,1)S(1)}, bf16[1,48,48]{1,2,0:T(8,128)(2,1)}, u32[]{:S(2)}) copy-start(bf16[1,48,48]{1,2,0:T(8,128)(2,1)} %copy.79) | copy-start | bytes 13828
  51.3 0.7 %copy-start.12 = (bf16[1,48,48]{1,2,0:T(8,128)(2,1)S(1)}, bf16[1,48,48]{1,2,0:T(8,128)(2,1)}, u32[]{:S(2)}) copy-start(bf16[1,48,48]{1,2,0:T(8,128)(2,1)} %copy.82) | copy-start | bytes 13828
  51.4 0.7 %copy-start.10 = (bf16[1,48,48]{1,2,0:T(8,128)(2,1)S(1)}, bf16[1,48,48]{1,2,0:T(8,128)(2,1)}, u32[]{:S(2)}) copy-start(bf16[1,48,48]{1,2,0:T(8,128)(2,1)} %copy.84) | copy-start | bytes 13828
where the time goes:
time: 59 us; the launch traced here: 58.4 us
  starting transfers between devices  18.8 us (32%)
  local copies, waits for them, and re-layouts  16.9 us (29%)
  Pallas kernels  12.9 us (22%)
  waiting for transfers between devices  7.23 us (12%)
  other arithmetic  1.58 us (3%)
  between operations  0.96 us (2%)
    ppermute x8, starting transfers between devices, exchange(): arrived.append(lax.ppermute(block, 'space', route))  13.7 us
    pallas_call x6, Pallas kernels, call(): pl.pallas_call(kernel, out_shape=[jax.ShapeDtypeStruct(shape, dtype) for...  12.9 us
    unnamed x54, local copies, waits for them, and re-layouts  9.84 us
    ppermute x5, waiting for transfers between devices, paired(): return lax.ppermute(block, axis, [(i, i ^ distance) for i in range(size)])  7.21 us
    ppermute x5, starting transfers between devices, paired(): return lax.ppermute(block, axis, [(i, i ^ distance) for i in range(size)])  5.13 us
    reshape x4, local copies, waits for them, and re-layouts, backward(): w.reshape(3, 3, C, C)[::-1, ::-1].transpose(1, 3, 0, 2)  1.76 us
    rev x2, local copies, waits for them, and re-layouts, backward(): w.reshape(3, 3, C, C)[::-1, ::-1].transpose(1, 3, 0, 2)  1.62 us
  transfers between devices with their start and end apart: 13, of which 3 were waited for; matrix products, arithmetic and copies ran while one was open for 18% of the time, Pallas kernels for 10%

commit v1 on v0

v1 whole, which is shorter than its diff:
```python
import functools

import jax
import jax.numpy as jnp
from jax import lax
from jax.experimental import pallas as pl
from jax.experimental.pallas import tpu as pltpu
from jax.sharding import PartitionSpec as P

BF = jnp.bfloat16
F32 = jnp.float32
C = 48
SIDE = 64
PIX = SIDE * SIDE
LANES = 128
TILES = PIX // LANES

VMEM = pl.BlockSpec(memory_space=pltpu.VMEM)
SMEM = pl.BlockSpec(memory_space=pltpu.SMEM)


def tap_of(edge, step):
    return (step, 3 * step + 2, 6 + step, 3 * step)[edge]


def offsets_of(spaces):
    return (-1, spaces // 4, 1, -(spaces // 4))


def dot(a, b):
    return jnp.dot(a, b, preferred_element_type=F32)


def dot_nt(a, b):
    return lax.dot_general(a, b, (((1,), (1,)), ((), ())), preferred_element_type=F32)


def iota(shape, axis):
    return lax.broadcasted_iota(jnp.int32, shape, axis)


def line_lanes(lane):
    z = lane - 128
    even = (z & 1) == 0
    left = jnp.where(z < 64, z, z - 63)
    right = jnp.where(z < 63, z + 2, jnp.where(z < 127, z - 63, 1))
    line = jnp.where(lane < 64, 0, jnp.where(lane < 128, 2, jnp.where(even, 3, 1)))
    place = jnp.where(lane < 64, lane, jnp.where(lane < 128, lane - 64, jnp.where(even, left, right)))
    return line, place


def lane_masks():
    lane = iota((C, LANES), 1) & 63
    return lane == 0, lane == 63


def tile(ref, t):
    return ref[:, t * LANES : (t + 1) * LANES]


def lines_from(tiles, first, last):
    total = tiles[0]
    for t in range(1, TILES):
        total = total + pltpu.roll(tiles[t], 2 * t, 1)
    low = iota((C, LANES), 1) < 64
    rows = jnp.where(low, first, last)
    return jnp.concatenate([rows, total], axis=1).astype(BF)


def edge_only(values):
    at_left, at_right = lane_masks()
    return jnp.where(at_left | at_right, values, 0.0)


def roles(spaces):
    me = lax.axis_index("space")
    return me, (me % 2) == 0, ((me // (spaces // 4)) % 2) == 0


def swap_edges(even, inner):
    return (
        jnp.where(even, 0, 2),
        jnp.where(even, 2, 0),
        jnp.where(inner, 3, 1),
        jnp.where(inner, 1, 3),
    )


def send_matrices(tables, spaces):
    me, even, inner = roles(spaces)
    hop = spaces // 4
    row = iota((256, LANES), 0)
    lane = iota((256, LANES), 1)
    line, place = line_lanes(row)
    out = []
    for edge in swap_edges(even, inner):
        offset = jnp.where(edge == 0, -1, jnp.where(edge == 1, hop, jnp.where(edge == 2, 1, -hop)))
        target = lax.rem(me - offset + spaces, spaces)
        k = tables[1, edge, target]
        r = tables[2, edge, target]
        turned = (r == 1) | (r == 2)
        want = jnp.where(turned, 63 - place, place)
        top = (line == k) & (lane == want)
        own = (line == lax.rem(edge + 2, 4)) & (lane - 64 == place)
        out.append(jnp.concatenate([jnp.where(top, 1.0, 0.0), jnp.where(own, 1.0, 0.0)], axis=0).astype(BF))
    return out


def by_edge(spaces, swaps):
    _, even, inner = roles(spaces)
    m1, m2, n1, n2 = [ref[...].astype(F32) for ref in swaps]
    order = (
        jnp.where(even, m2, m1),
        jnp.where(inner, n1, n2),
        jnp.where(even, m1, m2),
        jnp.where(inner, n2, n1),
    )
    low = iota((C, LANES), 1) < 64
    turned = [pltpu.roll(block, 64, 1) for block in order]
    lines = [jnp.where(low, order[e], turned[e + 1]) for e in (0, 2)]
    return jnp.concatenate(lines, axis=1).astype(BF), [block.astype(BF)[:, 0:64] for block in turned]


CHUNKS = 4


def send_kernel(spaces, tables_hbm, x_hbm, g_hbm, m1, m2, n1, n2, tables, x_ref, g_ref, table_sem, x_sem, g_sem):
    wide = PIX // CHUNKS
    fetch = pltpu.make_async_copy(tables_hbm, tables, table_sem)
    fetch.start()
    copies = []
    for part in range(CHUNKS):
        at = slice(part * wide, (part + 1) * wide)
        pair = [
            pltpu.make_async_copy(x_hbm.at[:, at], x_ref.at[:, at], x_sem.at[part]),
            pltpu.make_async_copy(g_hbm.at[:, at], g_ref.at[:, at], g_sem.at[part]),
        ]
        for copy in pair:
            copy.start()
        copies.append(pair)
    fetch.wait()
    matrices = send_matrices(tables, spaces)
    parts = [[], []]
    for part in range(CHUNKS):
        for field, ref in enumerate((x_ref, g_ref)):
            copies[part][field].wait()
            for t in range(part * TILES // CHUNKS, (part + 1) * TILES // CHUNKS):
                parts[field].append(edge_only(tile(ref, t).astype(F32)))
    both = [
        lines_from(parts[field], tile(ref, 0).astype(F32), tile(ref, TILES - 1).astype(F32))
        for field, ref in enumerate((x_ref, g_ref))
    ]
    both = jnp.concatenate(both, axis=1)
    for out, matrix in zip((m1, m2, n1, n2), matrices):
        out[...] = dot(both, matrix).astype(BF)


def weights_of(rules, where, corner):
    rule = rules[corner, where]
    first = jnp.where(rule == 0, 1.0, jnp.where(rule == 1, 0.0, 0.5)).astype(F32)
    return first, 1.0 - first


def user_matrix(tables, rules, me, spaces, edge, step):
    used = (edge + 2) % 4
    user = lax.rem(me + offsets_of(spaces)[edge] + spaces, spaces)
    k = tables[1, used, user]
    r = tables[2, used, user]
    turned = (r == 1) | (r == 2)
    q = iota((SIDE, 256), 0)
    line, place = line_lanes(iota((1, 256), 1))
    want = jnp.where(turned, 63 - place, place)
    mine = line == k
    value = jnp.where(mine & (q == want + 1 - step), 1.0, 0.0)
    which = used % 2
    corners = ((0, 1), (1, 3), (2, 3), (0, 2))[used]
    if step == 0:
        weight = weights_of(rules, user, corners[0])[which]
        value = value + jnp.where(mine & (want == 0) & (q == 0), weight, 0.0)
    if step == 2:
        weight = weights_of(rules, user, corners[1])[which]
        value = value + jnp.where(mine & (want == 63) & (q == 63), weight, 0.0)
    return value.astype(BF)


def halo_matrix(rules, me, step):
    row = iota((256, 256), 0)
    line, place = line_lanes(iota((1, 256), 1))
    at = place + step - 1
    inside = (at >= 0) & (at < 64)
    value = jnp.where(inside & (row == line * 64 + at), 1.0, 0.0)
    side = (line == 3) | (line == 1)
    left = line == 3
    if step != 1:
        if step == 0:
            active = side & (place == 0)
            row_a = jnp.where(left, 0, 63)
            row_b = jnp.where(left, 192, 64)
            pair = (0, 1)
        else:
            active = side & (place == 63)
            row_a = jnp.where(left, 128, 191)
            row_b = jnp.where(left, 255, 127)
            pair = (2, 3)
        fl, sl = weights_of(rules, me, pair[0])
        fr, sr = weights_of(rules, me, pair[1])
        value = value + jnp.where(active & (row == row_a), jnp.where(left, fl, fr), 0.0)
        value = value + jnp.where(active & (row == row_b), jnp.where(left, sl, sr), 0.0)
    return value.astype(BF)


def half_shift(dst, ref, before, after):
    low = iota((C, LANES), 1) < 64
    for t in range(TILES + 1):
        here = tile(ref, t) if t < TILES else after
        prev = tile(ref, t - 1) if t > 0 else before
        mixed = jnp.where(low, here.astype(F32), prev.astype(F32))
        dst[:, t * LANES : (t + 1) * LANES] = pltpu.roll(mixed, 64, 1).astype(BF)


def stack_of(half, ref, start, width):
    at = start * LANES
    size = width * LANES
    return jnp.concatenate(
        [half[:, at : at + size], ref[:, at : at + size], half[:, at + LANES : at + LANES + size]], axis=0
    )


def conv_tiles(weights, half, ref, columns, visit):
    at_left, at_right = lane_masks()
    for chunk in range(TILES // 2):
        taps = dot(weights, stack_of(half, ref, 2 * chunk, 2))
        for part in range(2):
            t = 2 * chunk + part
            lanes = slice(part * LANES, (part + 1) * LANES)
            side = 0.0 if columns is None else pltpu.roll(columns, (LANES - 2 * t) % LANES, 1)
            left = jnp.where(at_left, side, pltpu.roll(taps[0:C, lanes], 1, 1))
            right = jnp.where(at_right, side, pltpu.roll(taps[2 * C : 3 * C, lanes], LANES - 1, 1))
            visit(t, taps[C : 2 * C, lanes] + left + right)


def block_rows(taps, order):
    return jnp.concatenate([jnp.concatenate([taps[t] for t in row], axis=1) for row in order], axis=0)


def forward_form(taps):
    return block_rows(taps, [[b, 3 + b, 6 + b] for b in range(3)]).astype(BF)


def backward_form(taps):
    return block_rows(taps, [[8 - 3 * a - b for b in range(3)] for a in range(3)]).T.astype(BF)


def row_form(taps):
    return block_rows(taps, [[0, 1, 2], [6, 7, 8]]).astype(BF)


def return_form(taps):
    order = [[tap_of((edge + 2) % 4, step)] for edge in range(4) for step in range(3)]
    return block_rows(taps, order).T.astype(BF)


def float_taps(ref):
    return [ref[t].astype(F32) for t in range(9)]


def column(bias):
    row = jnp.broadcast_to(bias[...], (C, C))
    eye = iota((C, C), 0) == iota((C, C), 1)
    return jnp.broadcast_to(jnp.sum(jnp.where(eye, row, 0.0), axis=1, keepdims=True), (C, LANES))


def prepare_kernel(
    spaces, tables, rules, x_ref, g_ref, w1_ref, w2_ref,
    d_act, pre_in, x_side, route, halo, wf1, wr1, back2, half,
):
    me = lax.axis_index("space")
    taps1 = float_taps(w1_ref)
    taps2 = float_taps(w2_ref)
    wf1[...] = forward_form(taps1)
    wr1[...] = row_form(taps1)
    back2[...] = return_form(taps2)
    zero = jnp.zeros((C, LANES), BF)
    half_shift(half, g_ref, zero, zero)

    def keep(ref):
        def visit(t, value):
            ref[:, t * LANES : (t + 1) * LANES] = value

        return visit

    conv_tiles(backward_form(taps2), half, g_ref, None, keep(d_act))
    half_shift(half, x_ref, zero, zero)
    conv_tiles(wf1[...], half, x_ref, None, keep(pre_in))
    at_left, at_right = lane_masks()
    for t in range(TILES):
        at = slice(t * LANES, (t + 1) * LANES)
        x = tile(x_ref, t).astype(F32)
        x_side[0:C, at] = jnp.where(at_left, 0.0, pltpu.roll(x, 1, 1)).astype(BF)
        x_side[C : 2 * C, at] = jnp.where(at_right, 0.0, pltpu.roll(x, LANES - 1, 1)).astype(BF)
    for edge in range(4):
        for step in range(3):
            route[edge, :, step * 256 : (step + 1) * 256] = user_matrix(tables, rules, me, spaces, edge, step)
    for step in range(3):
        halo[:, step * 256 : (step + 1) * 256] = halo_matrix(rules, me, step)


def edge_terms(wf, wr, beside):
    stacked = jnp.concatenate([beside[:, s * 256 : (s + 1) * 256] for s in range(3)], axis=0)
    rows = dot(wr, stacked[:, 0:LANES])
    sides = dot(jnp.concatenate([wf[0:C], wf[2 * C : 3 * C]], axis=0), stacked[:, LANES:])
    lane = iota((C, LANES), 1)
    rows = jnp.where(lane < 64, rows[0:C], rows[C : 2 * C])
    return rows, jnp.where((lane & 1) == 0, sides[0:C], sides[C : 2 * C])


def add_edges(t, value, rows, sides):
    at_left, at_right = lane_masks()
    low = iota((C, LANES), 1) < 64
    value = value + jnp.where(at_left | at_right, pltpu.roll(sides, (LANES - 2 * t) % LANES, 1), 0.0)
    if t == 0:
        value = value + jnp.where(low, rows, 0.0)
    if t == TILES - 1:
        value = value + jnp.where(low, 0.0, rows)
    return value


def users_values(route, borders):
    parts = []
    for edge in range(4):
        moved = dot(borders[edge], route[edge]).astype(BF)
        parts += [moved[:, s * 256 : (s + 1) * 256] for s in range(3)]
    return jnp.concatenate(parts, axis=0)


def middle_kernel(
    spaces, tables, m1, m2, n1, n2, d_act, pre_in, route, halo, wf, wr, back, bias,
    act_ref, d_ref, p0, p1, p2, p3, beside_ref, users_ref, act_lines, d_lines,
):
    lines, borders = by_edge(spaces, (m1, m2, n1, n2))
    beside = dot(lines, halo[...]).astype(BF)
    beside_ref[...] = beside
    rows, sides = edge_terms(wf[...], wr[...], beside)
    users = users_values(route, borders)
    users_ref[...] = users
    line_grads = dot(back[...], users)
    d_rows = line_grads[:, 0:LANES]
    d_sides = line_grads[:, LANES : 2 * LANES]
    bias_now = column(bias)
    act_edges = []
    d_edges = []
    ends = {}
    for t in range(TILES):
        at = slice(t * LANES, (t + 1) * LANES)
        pre = add_edges(t, pre_in[:, at], rows, sides) + bias_now
        square = pre * pre
        inner = 0.7978845608028654 * pre * (1.0 + 0.044715 * square)
        wave = jnp.tanh(inner)
        cdf = 0.5 + 0.5 * wave
        slope = cdf + 0.5 * pre * (1.0 - wave * wave) * (0.7978845608028654 + 0.1070322243 * square)
        grad = add_edges(t, d_act[:, at], d_rows, d_sides)
        act = (pre * cdf).astype(BF)
        d_pre = (grad * slope).astype(BF)
        act_ref[:, at] = act
        d_ref[:, at] = d_pre
        act = act.astype(F32)
        d_pre = d_pre.astype(F32)
        act_edges.append(edge_only(act))
        d_edges.append(edge_only(d_pre))
        if t in (0, TILES - 1):
            ends[t] = (act, d_pre)
    act_l = lines_from(act_edges, ends[0][0], ends[TILES - 1][0])
    d_l = lines_from(d_edges, ends[0][1], ends[TILES - 1][1])
    act_lines[...] = act_l
    d_lines[...] = d_l
    both = jnp.concatenate([act_l, d_l], axis=1)
    for out, matrix in zip((p0, p1, p2, p3), send_matrices(tables, spaces)):
        out[...] = dot(both, matrix).astype(BF)


WIDE = 512
BIAS_AT = 9 * C


def grads_kernel(
    parts, x_ref, g_ref, act_ref, d_ref, x_side, beside, users, act_lines, d_lines,
    mine, other, half_a, half_d, held_one, held_two, near_one, near_two,
):
    zero = jnp.zeros((C, LANES), BF)
    half_shift(half_a, act_ref, zero, zero)
    half_shift(half_d, d_ref, zero, zero)
    width = 4
    at_left, at_right = lane_masks()
    one = jnp.zeros((3 * C, 3 * C), F32)
    two = jnp.zeros((3 * C, 3 * C), F32)
    ones = jnp.zeros((C, LANES), F32)
    twos = jnp.zeros((C, LANES), F32)
    for start in range(0, TILES, width):
        at = slice(start * LANES, (start + width) * LANES)
        g_tiles = [tile(g_ref, t).astype(F32) for t in range(start, start + width)]
        after = [jnp.where(at_right, 0.0, pltpu.roll(g, LANES - 1, 1)).astype(BF) for g in g_tiles]
        before = [jnp.where(at_left, 0.0, pltpu.roll(g, 1, 1)).astype(BF) for g in g_tiles]
        g_now = [jnp.concatenate(after, axis=1), g_ref[:, at], jnp.concatenate(before, axis=1)]
        g_now = jnp.concatenate(g_now, axis=0)
        x_now = jnp.concatenate([x_side[0:C, at], x_ref[:, at], x_side[C : 2 * C, at]], axis=0)
        two = two + dot_nt(g_now, stack_of(half_a, act_ref, start, width))
        one = one + dot_nt(stack_of(half_d, d_ref, start, width), x_now)
        for t in range(start, start + width):
            ones = ones + tile(d_ref, t).astype(F32)
            twos = twos + g_tiles[t - start]
    held_one[...] = one
    held_two[...] = two
    line, _ = line_lanes(iota((C, 256), 1))
    d_l = d_lines[...].astype(F32)
    d_by_edge = jnp.concatenate([jnp.where(line == e, d_l, 0.0) for e in range(4)], axis=0).astype(BF)
    near_one[...] = dot_nt(d_by_edge, jnp.concatenate([beside[:, s * 256 : (s + 1) * 256] for s in range(3)], axis=0))
    near_two[...] = dot_nt(users[...], act_lines[...])

    def block_one(a, b):
        value = held_one[(2 - a) * C : (3 - a) * C, b * C : (b + 1) * C]
        for edge in range(4):
            for step in range(3):
                if tap_of(edge, step) == 3 * a + b:
                    value = value + near_one[edge * C : (edge + 1) * C, step * C : (step + 1) * C]
        return value

    def block_two(a, b):
        value = held_two[b * C : (b + 1) * C, a * C : (a + 1) * C]
        for edge in range(4):
            for step in range(3):
                if tap_of(edge, step) == 3 * a + b:
                    at = ((edge + 2) % 4) * 3 + step
                    value = value + near_two[at * C : (at + 1) * C, :]
        return value

    def whole(block, bias):
        tail = jnp.broadcast_to(jnp.sum(bias, axis=1, keepdims=True), (C, WIDE - BIAS_AT))
        return jnp.concatenate([block(a, b) for a in range(3) for b in range(3)] + [tail], axis=1)

    first = whole(block_one, ones)
    second = whole(block_two, twos)
    even = (lax.axis_index("space") % 2) == 0
    keep = jnp.where(even, first, second)
    give = jnp.where(even, second, first)
    share = C // parts
    for part in range(parts):
        mine[part] = keep[part * share : (part + 1) * share]
        other[part] = give[part * share : (part + 1) * share]


def inner_kernel(g_ref, d_ref, w_ref, d_in, half):
    zero = jnp.zeros((C, LANES), BF)
    half_shift(half, d_ref, zero, zero)

    def visit(t, value):
        at = slice(t * LANES, (t + 1) * LANES)
        d_in[:, at] = value + g_ref[:, at].astype(F32)

    conv_tiles(backward_form(float_taps(w_ref)), half, d_ref, None, visit)


def output_kernel(spaces, x_ref, act_ref, m1, m2, n1, n2, halo, w_ref, bias, out, half):
    lines, _ = by_edge(spaces, (m1, m2, n1, n2))
    taps = float_taps(w_ref)
    wf = forward_form(taps)
    zero = jnp.zeros((C, LANES), BF)
    half_shift(half, act_ref, zero, zero)
    beside = dot(lines, halo[...]).astype(BF)
    rows, sides = edge_terms(wf, row_form(taps), beside)
    bias_now = column(bias)

    def visit(t, value):
        at = slice(t * LANES, (t + 1) * LANES)
        out[:, at] = (add_edges(t, value, rows, sides) + bias_now + x_ref[:, at].astype(F32)).astype(BF)

    conv_tiles(wf, half, act_ref, None, visit)


def grad_in_kernel(spaces, d_in, m1, m2, n1, n2, route, w_ref, out):
    _, borders = by_edge(spaces, (m1, m2, n1, n2))
    line_grads = dot(return_form(float_taps(w_ref)), users_values(route, borders))
    for t in range(TILES):
        at = slice(t * LANES, (t + 1) * LANES)
        out[:, at] = add_edges(t, d_in[:, at], line_grads[:, 0:LANES], line_grads[:, LANES : 2 * LANES]).astype(BF)


def unpack_kernel(share, own, got, grad_one, bias_one, grad_two, bias_two):
    even = (lax.axis_index("space") % 2) == 0
    first = jnp.where(even, own[...], got[...])
    second = jnp.where(even, got[...], own[...])
    eye = iota((share, LANES), 0) == iota((share, LANES), 1)
    for value, grad, bias in ((first, grad_one, bias_one), (second, grad_two, bias_two)):
        for tap in range(9):
            grad[tap] = value[:, tap * C : (tap + 1) * C]
        tail = jnp.broadcast_to(value[:, BIAS_AT : BIAS_AT + 1], (share, LANES))
        bias[...] = jnp.sum(jnp.where(eye, tail, 0.0), axis=0, keepdims=True)[:, 0:share]


def call(kernel, outs, specs, args, scratch=(), read=0, room=16 * 2**20):
    return pl.pallas_call(
        kernel,
        out_shape=[jax.ShapeDtypeStruct(shape, dtype) for shape, dtype in outs],
        in_specs=specs,
        out_specs=[VMEM] * len(outs),
        scratch_shapes=list(scratch),
        compiler_params=pltpu.CompilerParams(vmem_limit_bytes=room),
        cost_estimate=pl.CostEstimate(flops=0, bytes_accessed=read, transcendentals=0),
    )(*args)


HBM = pl.BlockSpec(memory_space=pltpu.HBM)


def exchange(blocks, spaces):
    hop = spaces // 4

    def first(i, step):
        return (i + step) % spaces if (i // step) % 2 == 0 else (i - step) % spaces

    def second(i, step):
        return (i - step) % spaces if (i // step) % 2 == 0 else (i + step) % spaces

    partner = (lambda i: first(i, 1), lambda i: second(i, 1), lambda i: first(i, hop), lambda i: second(i, hop))
    return [lax.ppermute(b, "space", [(i, to(i)) for i in range(spaces)]) for b, to in zip(blocks, partner)]


def swapped(block, mask, devices):
    return lax.ppermute(block, ("dp", "space"), [(i, i ^ mask) for i in range(devices)])


def total_over_chips(held, parts, spaces):
    devices = parts * spaces
    part_bits = [1 << bit for bit in reversed(range(parts.bit_length() - 1))]
    space_bits = [1 << bit for bit in range(1, spaces.bit_length() - 1)]
    rounds = [[(True, bit)] for bit in part_bits]
    for bit in space_bits:
        if len(rounds[-1]) == 1:
            rounds[-1].append((False, bit))
        elif len(rounds[0]) == 1:
            next(r for r in rounds if len(r) == 1).append((False, bit))
        else:
            rounds.append([(False, bit)])
    where = lax.axis_index("dp")
    for bits in rounds:
        keep = give = held.astype(BF)
        masks = []
        for is_part, bit in bits:
            masks.append(bit * spaces if is_part else bit)
            if is_part:
                upper = (where // bit) % 2 == 1
                low, high = keep[: keep.shape[0] // 2], keep[keep.shape[0] // 2 :]
                keep, give = jnp.where(upper, high, low), jnp.where(upper, low, high)
        split = bits[0][0]
        got = [swapped(give if split else keep, masks[0], devices)]
        if len(masks) == 2:
            got.append(swapped(keep, masks[1], devices))
            got.append(swapped(give if split else keep, masks[0] ^ masks[1], devices))
        terms = [value.astype(F32) for value in [keep] + got]
        held = terms[0] + terms[1]
        if len(masks) == 2:
            held = held + (terms[2] + terms[3])
    return held[0]


COST = 3_690_000


def on_device(inputs, cotangent, conv_one, bias_one, conv_two, bias_two, neighbours, corner_rule):
    parts = lax.axis_size("dp")
    spaces = lax.axis_size("space")
    share = C // parts
    x = inputs.reshape(C, PIX)
    g = cotangent.reshape(C, PIX)
    line = ((C, LANES), BF)
    image = ((C, PIX), BF)
    wide = ((C, PIX), F32)
    half = pltpu.VMEM((C, PIX + LANES), BF)
    tables = neighbours.transpose(2, 1, 0)
    rules = corner_rule.transpose(1, 0)

    sent = call(
        functools.partial(send_kernel, spaces), [line] * 4, [HBM, HBM, HBM], (tables, x, g),
        [pltpu.SMEM(tables.shape, jnp.int32), pltpu.VMEM((C, PIX), BF), pltpu.VMEM((C, PIX), BF),
         pltpu.SemaphoreType.DMA, pltpu.SemaphoreType.DMA((CHUNKS,)), pltpu.SemaphoreType.DMA((CHUNKS,))],
        read=COST * 2, room=66_900_000,
    )
    arrived = exchange(sent, spaces)
    square = ((3 * C, 3 * C), BF)
    rows = ((2 * C, 3 * C), BF)
    back = ((C, 12 * C), BF)
    d_act, pre_in, x_side, route, halo, wf1, wr1, back2 = call(
        functools.partial(prepare_kernel, spaces),
        [wide, wide, ((2 * C, PIX), BF), ((4, SIDE, 768), BF), ((256, 768), BF), square, rows, back],
        [SMEM, SMEM, VMEM, VMEM, VMEM, VMEM],
        (tables, rules, x, g, conv_one, conv_two), [half], read=COST * 3,
    )
    middle = call(
        functools.partial(middle_kernel, spaces),
        [image, image] + [line] * 4 + [((C, 768), BF), ((12 * C, 256), BF), ((C, 256), BF), ((C, 256), BF)],
        [SMEM] + [VMEM] * 12,
        (tables, *arrived, d_act, pre_in, route, halo, wf1, wr1, back2, bias_one.reshape(1, C)),
        read=COST * 9 // 4,
    )
    act, d_pre = middle[:2]
    beside, users, act_lines, d_lines = middle[6:]
    packed = ((parts, share, WIDE), F32)
    mine, other = call(
        functools.partial(grads_kernel, parts), [packed, packed], [VMEM] * 9,
        (x, g, act, d_pre, x_side, beside, users, act_lines, d_lines),
        [half, half, pltpu.VMEM((3 * C, 3 * C), F32), pltpu.VMEM((3 * C, 3 * C), F32),
         pltpu.VMEM((4 * C, 3 * C), F32), pltpu.VMEM((12 * C, C), F32)],
        read=COST * 5 // 4,
    )
    devices = parts * spaces
    held = mine + swapped(other, 1, devices)
    held, *blocks = lax.optimization_barrier((held, *middle[2:6]))
    again = exchange(blocks, spaces)
    own = total_over_chips(held, parts, spaces)
    (d_in,) = call(inner_kernel, [wide], [VMEM] * 3, (g, d_pre, conv_one), [half], read=COST)
    (output,) = call(
        functools.partial(output_kernel, spaces), [image], [VMEM] * 9,
        (x, act, *again, halo, conv_two, bias_two.reshape(1, C)), [half], read=COST * 3 // 2,
    )
    (grad_in,) = call(
        functools.partial(grad_in_kernel, spaces), [image], [VMEM] * 7, (d_in, *again, route, conv_one),
        read=COST * 7 // 4,
    )
    own, output, grad_in = lax.optimization_barrier((own, output, grad_in))
    got = swapped(own, 1, devices)
    taps = ((9, share, C), F32)
    bias = ((1, share), F32)
    grad_one, sum_one, grad_two, sum_two = call(
        functools.partial(unpack_kernel, share), [taps, bias, taps, bias], [VMEM] * 2, (own, got), read=10**5
    )
    shape = inputs.shape
    return (
        output.reshape(shape),
        grad_in.reshape(shape),
        grad_one,
        sum_one.reshape(share),
        grad_two,
        sum_two.reshape(share),
    )


def solution(mesh):
    tiles = P("dp", "space", None, None)
    return jax.shard_map(
        on_device,
        mesh=mesh,
        in_specs=(tiles, tiles, P(), P(), P(), P(), P(), P()),
        out_specs=(tiles, tiles, P(None, "dp", None), P("dp"), P(None, "dp", None), P("dp")),
        check_vma=False,
    )
```

time: 59 us -> 45.1 us (0.76)
  local copies, waits for them, and re-layouts: 16.9 us -> 4.21 us
  other arithmetic: 1.58 us -> 0.06 us
  waiting for transfers between devices: 7.23 us -> 5.9 us
  starting transfers between devices: 18.8 us -> 20.1 us
  Pallas kernels: 12.9 us -> 13.7 us
    unnamed x54 -> x22, local copies, waits for them, and re-layouts: 9.84 us -> 4.21 us
    reshape x10 -> x0, local copies, waits for them, and re-layouts: 2.39 us -> none  [the longest x4 1.76 us: backward(): w.reshape(3, 3, C, C)[::-1, ::-1].transpose(1, 3, 0, 2)]
    slice x4 -> x0, local copies, waits for them, and re-layouts: 2.07 us -> none  [the longest x1 0.75 us: on_device(): total[:, :, C:2 * C]]
    rev x2 -> x0, local copies, waits for them, and re-layouts: 1.62 us -> none  [backward(): w.reshape(3, 3, C, C)[::-1, ::-1].transpose(1, 3, 0, 2)]
    ppermute x13 -> x16, waiting for transfers between devices: 7.23 us -> 5.9 us  [the longest x8 3.55 us: swapped(): lax.ppermute(block, ('dp', 'space'), [(i, i ^ mask) for i in range(device...]
    ppermute x13 -> x16, starting transfers between devices: 18.8 us -> 20.1 us  [the longest x8 11.9 us: exchange(): lax.ppermute(b, 'space', [(i, to(i)) for i in range(spaces)])]
    concatenate x2 -> x0, local copies, waits for them, and re-layouts: 0.97 us -> none  [returning(): return jnp.concatenate(taps, axis=1)]
    add x1, other arithmetic: 0.85 us -> 0.02 us  [on_device(): held = mine + swapped(other, 1, devices)]
  transfers between devices with their start and end apart: 13 -> 16, of which waited for: 3 -> 5; matrix products, arithmetic and copies ran while one was open for 18% -> 0% of each run, Pallas kernels for 10% -> 16%
where the time goes in v1:
time: 45.1 us; the launch traced here: 44.8 us
  starting transfers between devices  20.1 us (45%)
  Pallas kernels  13.7 us (30%)
  waiting for transfers between devices  5.9 us (13%)
  local copies, waits for them, and re-layouts  4.21 us (9%)
  between operations  0.83 us (2%)
    pallas_call x8, Pallas kernels, call(): pl.pallas_call(kernel, out_shape=[jax.ShapeDtypeStruct(shape, dtype) for...  13.7 us
    ppermute x8, starting transfers between devices, exchange(): lax.ppermute(b, 'space', [(i, to(i)) for i in range(spaces)])  11.9 us
    ppermute x8, starting transfers between devices, swapped(): lax.ppermute(block, ('dp', 'space'), [(i, i ^ mask) for i in range(device...  8.15 us
    unnamed x22, local copies, waits for them, and re-layouts  4.21 us
    ppermute x8, waiting for transfers between devices, swapped(): lax.ppermute(block, ('dp', 'space'), [(i, i ^ mask) for i in range(device...  3.55 us
    ppermute x8, waiting for transfers between devices, exchange(): lax.ppermute(b, 'space', [(i, to(i)) for i in range(spaces)])  2.35 us
  transfers between devices with their start and end apart: 16, of which 5 were waited for; matrix products, arithmetic and copies ran while one was open for 0% of the time, Pallas kernels for 16%

profile of v1, /device:TPU:0, one launch (start us, length us, event | category | flops | bytes accessed | tf_op | source)
XLA Modules:
  0.0 44.8 jit_solution(6042627598178344326)
XLA Ops:
  0.6 0.0 copy-start.4
  0.6 2.4 %shard_map.127 = (bf16[48,128]{1,0:T(8,128)(2,1)}, bf16[48,128]{1,0:T(8,128)(2,1)}, bf16[48,128]{1,0:T(8,128)(2,1)}, bf16[48,128]{1,0:T(8,128)(2,1)}) custom-call(s32[3,4,16]{2,1,0:T(4,128)} %bitcast.20, bf16[48,4096]{1,0:T(8,128)(2,1)} %bitcast.16, bf16[48,4096]{1,0:T(8,128)(2,1)} %bitcast.12), custom_call_target="tpu_custom_call" | custom-call | bytes 7380000 | tf_op jit(solution)/shard_map/pallas_call | solution.py:500
  3.0 0.0 copy-start.7
  3.0 0.5 %collective-permute-start = (bf16[48,128]{1,0:T(8,128)(2,1)}, bf16[48,128]{1,0:T(8,128)(2,1)S(1)}, u32[]{:S(2)}, u32[]{:S(2)}) collective-permute-start(bf16[48,128]{1,0:T(8,128)(2,1)} %get-tuple-element.42), channel_id=1, source_target_pairs={{0,1},{1,0},{2,3},{3,2},{4,5},{5,4},{6,7},{7,6},{8,9},{9,8},{10,11... | collective-permute-start | bytes 36872 | tf_op jit(solution)/shard_map/ppermute | solution.py:524
  3.5 5.6 %collective-permute-start.1 = (bf16[48,128]{1,0:T(8,128)(2,1)}, bf16[48,128]{1,0:T(8,128)(2,1)S(1)}, u32[]{:S(2)}, u32[]{:S(2)}) collective-permute-start(bf16[48,128]{1,0:T(8,128)(2,1)} %get-tuple-element.43), channel_id=1, source_target_pairs={{0,15},{1,2},{2,1},{3,4},{4,3},{5,6},{6,5},{7,8},{8,7},{9,10},{10,... | collective-permute-start | bytes 36872 | tf_op jit(solution)/shard_map/ppermute | solution.py:524
  9.2 0.0 copy-start.8
  9.2 0.0 collective-permute-start.2
  9.2 0.9 %collective-permute-start.3 = (bf16[48,128]{1,0:T(8,128)(2,1)}, bf16[48,128]{1,0:T(8,128)(2,1)S(1)}, u32[]{:S(2)}, u32[]{:S(2)}) collective-permute-start(bf16[48,128]{1,0:T(8,128)(2,1)} %get-tuple-element.45), channel_id=1, source_target_pairs={{0,12},{1,13},{2,14},{3,15},{4,8},{5,9},{6,10},{7,11},{8,4},{9,5},... | collective-permute-start | bytes 36872 | tf_op jit(solution)/shard_map/ppermute | solution.py:524
  10.1 0.0 copy-done.4
  10.1 0.0 copy-done.7
  10.1 0.0 copy-done.8
  10.1 0.0 copy-start
  10.1 1.0 %copy-done = bf16[1,1,48,4096]{3,2,1,0:T(8,128)(2,1)S(1)} copy-done((bf16[1,1,48,4096]{3,2,1,0:T(8,128)(2,1)S(1)}, bf16[1,1,48,4096]{3,2,1,0:T(8,128)(2,1)}, u32[]{:S(2)}) %copy-start) | copy-done | bytes 393240
  11.1 0.0 copy-start.2
  11.1 1.0 %copy-done.2 = bf16[1,1,48,4096]{3,2,1,0:T(8,128)(2,1)S(1)} copy-done((bf16[1,1,48,4096]{3,2,1,0:T(8,128)(2,1)S(1)}, bf16[1,1,48,4096]{3,2,1,0:T(8,128)(2,1)}, u32[]{:S(2)}) %copy-start.2) | copy-done | bytes 393240
  12.1 0.0 copy-start.5
  12.1 0.9 %copy-done.5 = bf16[9,48,48]{2,1,0:T(8,128)(2,1)S(1)} copy-done((bf16[9,48,48]{2,1,0:T(8,128)(2,1)S(1)}, bf16[9,48,48]{2,1,0:T(8,128)(2,1)}, u32[]{:S(2)}) %copy-start.5) | copy-done | bytes 41496
  13.0 3.0 %shard_map.128 = (f32[48,4096]{1,0:T(8,128)S(1)}, f32[48,4096]{1,0:T(8,128)S(1)}, bf16[96,4096]{1,0:T(8,128)(2,1)S(1)}, bf16[4,64,768]{2,1,0:T(8,128)(2,1)S(1)},...) custom-call(s32[3,4,16]{2,1,0:T(4,128)S(1)} %bitcast.21, ...), custom_call_target="tpu_custom_call" | custom-call | bytes 11070000 | tf_op jit(solution)/shard_map/pallas_call | solution.py:500
  16.0 0.0 collective-permute-done.m1
  16.0 0.0 collective-permute-done.1.m2
  16.0 0.0 collective-permute-done.2.n1
  16.0 0.0 collective-permute-done.3.n2
  16.0 0.0 copy-start.10
  16.0 0.6 %copy-done.10 = f32[48]{0:T(128)S(1)} copy-done((f32[48]{0:T(128)S(1)}, f32[48]{0:T(128)}, u32[]{:S(2)}) %copy-start.10) | copy-done | bytes 216
  16.7 0.0 copy-start.1
  16.7 0.0 copy-start.3
  16.7 2.2 %shard_map.129 = (bf16[48,4096]{1,0:T(8,128)(2,1)S(1)}, bf16[48,4096]{1,0:T(8,128)(2,1)S(1)}, bf16[48,128]{1,0:T(8,128)(2,1)S(1)}, bf16[48,128]{1,0:T(8,128)(2,1...) custom-call(s32[3,4,16]{2,1,0:T(4,128)S(1)} %bitcast.22, ...), custom_call_target="tpu_custom_call" | custom-call | bytes 8302500 | tf_op jit(solution)/shard_map/pallas_call | solution.py:500
  18.9 0.0 copy-done.1
  18.9 0.0 copy-done.3
  19.0 1.2 %shard_map.130 = (f32[2,24,512]{2,1,0:T(8,128)S(1)}, f32[2,24,512]{2,1,0:T(8,128)S(1)}) custom-call(bf16[48,4096]{1,0:T(8,128)(2,1)S(1)} %bitcast.18, bf16[48,4096]{1,0:T(8,128)(2,1)S(1)} %bitcast.14, bf16[48,4096]{1,0:T(8,128)(2,1)S(1)} %get-tuple-element.53.act_ref, bf16[48,4096]{1,0:T(8,128)(2,1)S(1)} %get-tuple-element.54.d_ref, ...), custom_call_target="tpu_custom_call" | custom-call | bytes 4612500 | tf_op jit(solution)/shard_map/pallas_call | solution.py:500
  20.2 0.1 collective-permute-start.4
  20.3 1.3 %collective-permute-done.4 = f32[2,24,512]{2,1,0:T(8,128)S(1)} collective-permute-done((f32[2,24,512]{2,1,0:T(8,128)S(1)}, f32[2,24,512]{2,1,0:T(8,128)S(1)}, u32[]{:S(2)}, u32[]{:S(2)}) %collective-permute-start.4) | collective-permute-done | bytes 98336 | tf_op jit(solution)/shard_map/ppermute | solution.py:528
  21.6 1.6 %collective-permute-start.5 = (bf16[1,24,512]{2,1,0:T(8,128)(2,1)S(1)}, bf16[1,24,512]{2,1,0:T(8,128)(2,1)S(1)}, u32[]{:S(2)}, u32[]{:S(2)}) collective-permute-start(bf16[1,24,512]{2,1,0:T(8,128)(2,1)S(1)} %get-tuple-element.79), channel_id=1, source_target_pairs={{0,16},{1,17},{2,18},{3,19},{4,20},{5,21},{6,22},{7,23},{8,24},{9,... | collective-permute-start | bytes 73736 | tf_op jit(solution)/shard_map/ppermute | solution.py:528
  23.2 0.8 %collective-permute-start.6 = (bf16[1,24,512]{2,1,0:T(8,128)(2,1)S(1)}, bf16[1,24,512]{2,1,0:T(8,128)(2,1)S(1)}, u32[]{:S(2)}, u32[]{:S(2)}) collective-permute-start(bf16[1,24,512]{2,1,0:T(8,128)(2,1)S(1)} %get-tuple-element.78), channel_id=1, source_target_pairs={{0,2},{1,3},{2,0},{3,1},{4,6},{5,7},{6,4},{7,5},{8,10},{9,11},{10,... | collective-permute-start | bytes 73736 | tf_op jit(solution)/shard_map/ppermute | solution.py:528
  24.0 1.1 %collective-permute-start.7 = (bf16[1,24,512]{2,1,0:T(8,128)(2,1)S(1)}, bf16[1,24,512]{2,1,0:T(8,128)(2,1)S(1)}, u32[]{:S(2)}, u32[]{:S(2)}) collective-permute-start(bf16[1,24,512]{2,1,0:T(8,128)(2,1)S(1)} %get-tuple-element.79), channel_id=1, source_target_pairs={{0,18},{1,19},{2,16},{3,17},{4,22},{5,23},{6,20},{7,21},{8,26},{9,... | collective-permute-start | bytes 73736 | tf_op jit(solution)/shard_map/ppermute | solution.py:528
  25.2 0.0 collective-permute-start.11
  25.2 2.5 %collective-permute-start.12 = (bf16[48,128]{1,0:T(8,128)(2,1)S(1)}, bf16[48,128]{1,0:T(8,128)(2,1)S(1)}, u32[]{:S(2)}, u32[]{:S(2)}) collective-permute-start(bf16[48,128]{1,0:T(8,128)(2,1)S(1)} %get-tuple-element.68), channel_id=1, source_target_pairs={{0,15},{1,2},{2,1},{3,4},{4,3},{5,6},{6,5},{7,8},{8,7},{9,10},{10,... | collective-permute-start | bytes 36872 | tf_op jit(solution)/shard_map/ppermute | solution.py:524
  27.7 0.0 collective-permute-done.5
  27.7 0.0 collective-permute-done.6
  27.7 1.0 %collective-permute-done.7 = bf16[1,24,512]{2,1,0:T(8,128)(2,1)S(1)} collective-permute-done((bf16[1,24,512]{2,1,0:T(8,128)(2,1)S(1)}, bf16[1,24,512]{2,1,0:T(8,128)(2,1)S(1)}, u32[]{:S(2)}, u32[]{:S(2)}) %collective-permute-start.7) | collective-permute-done | bytes 24608 | tf_op jit(solution)/shard_map/ppermute | solution.py:528
  28.8 2.2 %collective-permute-start.10 = (bf16[1,24,512]{2,1,0:T(8,128)(2,1)S(1)}, bf16[1,24,512]{2,1,0:T(8,128)(2,1)S(1)}, u32[]{:S(2)}, u32[]{:S(2)}) collective-permute-start(bf16[1,24,512]{2,1,0:T(8,128)(2,1)S(1)} %add_convert_fusion), channel_id=1, source_target_pairs={{0,12},{1,13},{2,14},{3,15},{4,8},{5,9},{6,10},{7,11},{8,4},{9,5},... | collective-permute-start | bytes 73736 | tf_op jit(solution)/shard_map/ppermute | solution.py:528
  30.9 0.2 collective-permute-start.8
  31.1 2.1 %collective-permute-start.9 = (bf16[1,24,512]{2,1,0:T(8,128)(2,1)S(1)}, bf16[1,24,512]{2,1,0:T(8,128)(2,1)S(1)}, u32[]{:S(2)}, u32[]{:S(2)}) collective-permute-start(bf16[1,24,512]{2,1,0:T(8,128)(2,1)S(1)} %add_convert_fusion), channel_id=1, source_target_pairs={{0,8},{1,9},{2,10},{3,11},{4,12},{5,13},{6,14},{7,15},{8,0},{9,1},... | collective-permute-start | bytes 73736 | tf_op jit(solution)/shard_map/ppermute | solution.py:528
  33.2 0.0 collective-permute-done.11.m1
  33.2 0.0 collective-permute-start.13
  33.2 0.0 collective-permute-done.12.m2
  33.2 2.3 %collective-permute-start.14 = (bf16[48,128]{1,0:T(8,128)(2,1)S(1)}, bf16[48,128]{1,0:T(8,128)(2,1)S(1)}, u32[]{:S(2)}, u32[]{:S(2)}) collective-permute-start(bf16[48,128]{1,0:T(8,128)(2,1)S(1)} %get-tuple-element.70), channel_id=1, source_target_pairs={{0,12},{1,13},{2,14},{3,15},{4,8},{5,9},{6,10},{7,11},{8,4},{9,5},... | collective-permute-start | bytes 36872 | tf_op jit(solution)/shard_map/ppermute | solution.py:524
  35.5 0.9 %shard_map.132.d_in = f32[48,4096]{1,0:T(8,128)S(1)} custom-call(bf16[48,4096]{1,0:T(8,128)(2,1)S(1)} %bitcast.15, bf16[48,4096]{1,0:T(8,128)(2,1)S(1)} %get-tuple-element.54.d_ref, bf16[9,48,48]{2,1,0:T(8,128)(2,1)S(1)} %copy-done.4), custom_call_target="tpu_custom_call" | custom-call | bytes 3690000 | tf_op jit(solution)/shard_map/pallas_call | solution.py:500
  36.4 0.0 copy-start.6
  36.5 0.5 %collective-permute-done.13.n1 = bf16[48,128]{1,0:T(8,128)(2,1)S(1)} collective-permute-done((bf16[48,128]{1,0:T(8,128)(2,1)S(1)}, bf16[48,128]{1,0:T(8,128)(2,1)S(1)}, u32[]{:S(2)}, u32[]{:S(2)}) %collective-permute-start.13) | collective-permute-done | bytes 12320 | tf_op jit(solution)/shard_map/ppermute | solution.py:524
  36.9 1.9 %collective-permute-done.14.n2 = bf16[48,128]{1,0:T(8,128)(2,1)S(1)} collective-permute-done((bf16[48,128]{1,0:T(8,128)(2,1)S(1)}, bf16[48,128]{1,0:T(8,128)(2,1)S(1)}, u32[]{:S(2)}, u32[]{:S(2)}) %collective-permute-start.14) | collective-permute-done | bytes 12320 | tf_op jit(solution)/shard_map/ppermute | solution.py:524
  38.8 1.4 %shard_map.133 = bf16[48,4096]{1,0:T(8,128)(2,1)} custom-call(f32[48,4096]{1,0:T(8,128)S(1)} %shard_map.132.d_in, bf16[48,128]{1,0:T(8,128)(2,1)S(1)} %collective-permute-done.11.m1, bf16[48,128]{1,0:T(8,128)(2,1)S(1)} %collective-permute-done.12.m2, bf16[48,128]{1,0:T(8,128)(2,1)S(1)} %collective-permute-done.13.n1, ...), custom_call_target="tpu_custom_call" | custom-call | bytes 6457500 | tf_op jit(solution)/shard_map/pallas_call | solution.py:500
  40.2 0.0 copy-start.9
  40.2 0.0 copy-done.6
  40.2 0.7 %copy-done.9 = f32[48]{0:T(128)S(1)} copy-done((f32[48]{0:T(128)S(1)}, f32[48]{0:T(128)}, u32[]{:S(2)}) %copy-start.9) | copy-done | bytes 216
  40.9 1.8 %shard_map.131 = bf16[48,4096]{1,0:T(8,128)(2,1)} custom-call(bf16[48,4096]{1,0:T(8,128)(2,1)S(1)} %bitcast.19, bf16[48,4096]{1,0:T(8,128)(2,1)S(1)} %get-tuple-element.53.act_ref, bf16[48,128]{1,0:T(8,128)(2,1)S(1)} %collective-permute-done.11.m1, bf16[48,128]{1,0:T(8,128)(2,1)S(1)} %collective-permute-done.12.m2, ...), custom_call_target="tpu_custom_call" | custom-call | bytes 5535000 | tf_op jit(solution)/shard_map/pallas_call | solution.py:500
  42.7 0.0 collective-permute-done.10
  42.7 0.0 collective-permute-done.8
  42.7 0.0 collective-permute-done.9
  42.7 0.1 collective-permute-start.15
  42.8 1.2 %collective-permute-done.15.got = f32[24,512]{1,0:T(8,128)S(1)} collective-permute-done((f32[24,512]{1,0:T(8,128)S(1)}, f32[24,512]{1,0:T(8,128)S(1)}, u32[]{:S(2)}, u32[]{:S(2)}) %collective-permute-start.15) | collective-permute-done | bytes 49184 | tf_op jit(solution)/shard_map/ppermute | solution.py:528
  44.0 0.8 %shard_map.134 = (f32[9,24,48]{2,1,0:T(8,128)}, f32[1,24]{1,0:T(1,128)}, f32[9,24,48]{2,1,0:T(8,128)}, f32[1,24]{1,0:T(1,128)}) custom-call(f32[24,512]{1,0:T(8,128)S(1)} %add_bitcast_fusion.own, f32[24,512]{1,0:T(8,128)S(1)} %collective-permute-done.15.got), custom_call_target="tpu_custom_call" | custom-call | bytes 100000 | tf_op jit(solution)/shard_map/pallas_call | solution.py:500
  (4 shorter events, 0.1 us)
Async XLA Ops:
  0.6 9.5 %copy-start.4 = (bf16[9,48,48]{2,1,0:T(8,128)(2,1)S(1)}, bf16[9,48,48]{2,1,0:T(8,128)(2,1)}, u32[]{:S(2)}) copy-start(bf16[9,48,48]{2,1,0:T(8,128)(2,1)} %w_ref.5) | copy-start | bytes 124420
  3.0 7.1 %copy-start.7 = (s32[16,4,3]{0,1,2:T(4,128)S(1)}, s32[16,4,3]{0,1,2:T(4,128)}, u32[]{:S(2)}) copy-start(s32[16,4,3]{0,1,2:T(4,128)} %param.14) | copy-start | bytes 2308
  3.0 12.9 %collective-permute-start = (bf16[48,128]{1,0:T(8,128)(2,1)}, bf16[48,128]{1,0:T(8,128)(2,1)S(1)}, u32[]{:S(2)}, u32[]{:S(2)}) collective-permute-start(bf16[48,128]{1,0:T(8,128)(2,1)} %get-tuple-element.42), channel_id=1, source_target_pairs={{0,1},{1,0},{2,3},{3,2},{4,5},{5,4},{6,7},{7,6},{8,9},{9,8},{10,11... | collective-permute-start | bytes 36872 | tf_op jit(solution)/shard_map/ppermute | solution.py:524
  3.5 12.4 %collective-permute-start.1 = (bf16[48,128]{1,0:T(8,128)(2,1)}, bf16[48,128]{1,0:T(8,128)(2,1)S(1)}, u32[]{:S(2)}, u32[]{:S(2)}) collective-permute-start(bf16[48,128]{1,0:T(8,128)(2,1)} %get-tuple-element.43), channel_id=1, source_target_pairs={{0,15},{1,2},{2,1},{3,4},{4,3},{5,6},{6,5},{7,8},{8,7},{9,10},{10,... | collective-permute-start | bytes 36872 | tf_op jit(solution)/shard_map/ppermute | solution.py:524
  9.2 0.9 %copy-start.8 = (s32[16,4]{0,1:T(4,128)S(1)}, s32[16,4]{0,1:T(4,128)}, u32[]{:S(2)}) copy-start(s32[16,4]{0,1:T(4,128)} %param.15) | copy-start | bytes 772
  9.2 6.8 %collective-permute-start.2 = (bf16[48,128]{1,0:T(8,128)(2,1)}, bf16[48,128]{1,0:T(8,128)(2,1)S(1)}, u32[]{:S(2)}, u32[]{:S(2)}) collective-permute-start(bf16[48,128]{1,0:T(8,128)(2,1)} %get-tuple-element.44), channel_id=1, source_target_pairs={{0,4},{1,5},{2,6},{3,7},{4,0},{5,1},{6,2},{7,3},{8,12},{9,13},{10,... | collective-permute-start | bytes 36872 | tf_op jit(solution)/shard_map/ppermute | solution.py:524
  9.2 6.8 %collective-permute-start.3 = (bf16[48,128]{1,0:T(8,128)(2,1)}, bf16[48,128]{1,0:T(8,128)(2,1)S(1)}, u32[]{:S(2)}, u32[]{:S(2)}) collective-permute-start(bf16[48,128]{1,0:T(8,128)(2,1)} %get-tuple-element.45), channel_id=1, source_target_pairs={{0,12},{1,13},{2,14},{3,15},{4,8},{5,9},{6,10},{7,11},{8,4},{9,5},... | collective-permute-start | bytes 36872 | tf_op jit(solution)/shard_map/ppermute | solution.py:524
  10.1 1.0 %copy-start = (bf16[1,1,48,4096]{3,2,1,0:T(8,128)(2,1)S(1)}, bf16[1,1,48,4096]{3,2,1,0:T(8,128)(2,1)}, u32[]{:S(2)}) copy-start(bf16[1,1,48,4096]{3,2,1,0:T(8,128)(2,1)} %param.9) | copy-start | bytes 1179652
  11.1 1.0 %copy-start.2 = (bf16[1,1,48,4096]{3,2,1,0:T(8,128)(2,1)S(1)}, bf16[1,1,48,4096]{3,2,1,0:T(8,128)(2,1)}, u32[]{:S(2)}) copy-start(bf16[1,1,48,4096]{3,2,1,0:T(8,128)(2,1)} %param.8) | copy-start | bytes 1179652
  12.1 0.9 %copy-start.5 = (bf16[9,48,48]{2,1,0:T(8,128)(2,1)S(1)}, bf16[9,48,48]{2,1,0:T(8,128)(2,1)}, u32[]{:S(2)}) copy-start(bf16[9,48,48]{2,1,0:T(8,128)(2,1)} %w_ref.3) | copy-start | bytes 124420
  16.0 0.7 %copy-start.10 = (f32[48]{0:T(128)S(1)}, f32[48]{0:T(128)}, u32[]{:S(2)}) copy-start(f32[48]{0:T(128)} %param.11) | copy-start | bytes 580
  16.7 2.3 %copy-start.1 = (bf16[1,1,48,4096]{3,2,1,0:T(8,128)(2,1)S(1)}, bf16[1,1,48,4096]{3,2,1,0:T(8,128)(2,1)}, u32[]{:S(2)}) copy-start(bf16[1,1,48,4096]{3,2,1,0:T(8,128)(2,1)} %param.9) | copy-start | bytes 1179652
  16.7 2.3 %copy-start.3 = (bf16[1,1,48,4096]{3,2,1,0:T(8,128)(2,1)S(1)}, bf16[1,1,48,4096]{3,2,1,0:T(8,128)(2,1)}, u32[]{:S(2)}) copy-start(bf16[1,1,48,4096]{3,2,1,0:T(8,128)(2,1)} %param.8) | copy-start | bytes 1179652
  20.2 1.4 %collective-permute-start.4 = (f32[2,24,512]{2,1,0:T(8,128)S(1)}, f32[2,24,512]{2,1,0:T(8,128)S(1)}, u32[]{:S(2)}, u32[]{:S(2)}) collective-permute-start(f32[2,24,512]{2,1,0:T(8,128)S(1)} %get-tuple-element.61), channel_id=1, source_target_pairs={{0,1},{1,0},{2,3},{3,2},{4,5},{5,4},{6,7},{7,6},{8,9},{9,8},{10,11... | collective-permute-start | bytes 294920 | tf_op jit(solution)/shard_map/ppermute | solution.py:528
  21.6 6.1 %collective-permute-start.5 = (bf16[1,24,512]{2,1,0:T(8,128)(2,1)S(1)}, bf16[1,24,512]{2,1,0:T(8,128)(2,1)S(1)}, u32[]{:S(2)}, u32[]{:S(2)}) collective-permute-start(bf16[1,24,512]{2,1,0:T(8,128)(2,1)S(1)} %get-tuple-element.79), channel_id=1, source_target_pairs={{0,16},{1,17},{2,18},{3,19},{4,20},{5,21},{6,22},{7,23},{8,24},{9,... | collective-permute-start | bytes 73736 | tf_op jit(solution)/shard_map/ppermute | solution.py:528
  23.2 4.5 %collective-permute-start.6 = (bf16[1,24,512]{2,1,0:T(8,128)(2,1)S(1)}, bf16[1,24,512]{2,1,0:T(8,128)(2,1)S(1)}, u32[]{:S(2)}, u32[]{:S(2)}) collective-permute-start(bf16[1,24,512]{2,1,0:T(8,128)(2,1)S(1)} %get-tuple-element.78), channel_id=1, source_target_pairs={{0,2},{1,3},{2,0},{3,1},{4,6},{5,7},{6,4},{7,5},{8,10},{9,11},{10,... | collective-permute-start | bytes 73736 | tf_op jit(solution)/shard_map/ppermute | solution.py:528
  24.0 4.7 %collective-permute-start.7 = (bf16[1,24,512]{2,1,0:T(8,128)(2,1)S(1)}, bf16[1,24,512]{2,1,0:T(8,128)(2,1)S(1)}, u32[]{:S(2)}, u32[]{:S(2)}) collective-permute-start(bf16[1,24,512]{2,1,0:T(8,128)(2,1)S(1)} %get-tuple-element.79), channel_id=1, source_target_pairs={{0,18},{1,19},{2,16},{3,17},{4,22},{5,23},{6,20},{7,21},{8,26},{9,... | collective-permute-start | bytes 73736 | tf_op jit(solution)/shard_map/ppermute | solution.py:528
  25.2 8.1 %collective-permute-start.11 = (bf16[48,128]{1,0:T(8,128)(2,1)S(1)}, bf16[48,128]{1,0:T(8,128)(2,1)S(1)}, u32[]{:S(2)}, u32[]{:S(2)}) collective-permute-start(bf16[48,128]{1,0:T(8,128)(2,1)S(1)} %get-tuple-element.67), channel_id=1, source_target_pairs={{0,1},{1,0},{2,3},{3,2},{4,5},{5,4},{6,7},{7,6},{8,9},{9,8},{10,11... | collective-permute-start | bytes 36872 | tf_op jit(solution)/shard_map/ppermute | solution.py:524
  25.2 8.1 %collective-permute-start.12 = (bf16[48,128]{1,0:T(8,128)(2,1)S(1)}, bf16[48,128]{1,0:T(8,128)(2,1)S(1)}, u32[]{:S(2)}, u32[]{:S(2)}) collective-permute-start(bf16[48,128]{1,0:T(8,128)(2,1)S(1)} %get-tuple-element.68), channel_id=1, source_target_pairs={{0,15},{1,2},{2,1},{3,4},{4,3},{5,6},{6,5},{7,8},{8,7},{9,10},{10,... | collective-permute-start | bytes 36872 | tf_op jit(solution)/shard_map/ppermute | solution.py:524
  28.8 13.9 %collective-permute-start.10 = (bf16[1,24,512]{2,1,0:T(8,128)(2,1)S(1)}, bf16[1,24,512]{2,1,0:T(8,128)(2,1)S(1)}, u32[]{:S(2)}, u32[]{:S(2)}) collective-permute-start(bf16[1,24,512]{2,1,0:T(8,128)(2,1)S(1)} %add_convert_fusion), channel_id=1, source_target_pairs={{0,12},{1,13},{2,14},{3,15},{4,8},{5,9},{6,10},{7,11},{8,4},{9,5},... | collective-permute-start | bytes 73736 | tf_op jit(solution)/shard_map/ppermute | solution.py:528
  30.9 11.7 %collective-permute-start.8 = (bf16[1,24,512]{2,1,0:T(8,128)(2,1)S(1)}, bf16[1,24,512]{2,1,0:T(8,128)(2,1)S(1)}, u32[]{:S(2)}, u32[]{:S(2)}) collective-permute-start(bf16[1,24,512]{2,1,0:T(8,128)(2,1)S(1)} %add_convert_fusion), channel_id=1, source_target_pairs={{0,4},{1,5},{2,6},{3,7},{4,0},{5,1},{6,2},{7,3},{8,12},{9,13},{10,... | collective-permute-start | bytes 73736 | tf_op jit(solution)/shard_map/ppermute | solution.py:528
  31.1 11.5 %collective-permute-start.9 = (bf16[1,24,512]{2,1,0:T(8,128)(2,1)S(1)}, bf16[1,24,512]{2,1,0:T(8,128)(2,1)S(1)}, u32[]{:S(2)}, u32[]{:S(2)}) collective-permute-start(bf16[1,24,512]{2,1,0:T(8,128)(2,1)S(1)} %add_convert_fusion), channel_id=1, source_target_pairs={{0,8},{1,9},{2,10},{3,11},{4,12},{5,13},{6,14},{7,15},{8,0},{9,1},... | collective-permute-start | bytes 73736 | tf_op jit(solution)/shard_map/ppermute | solution.py:528
  33.2 3.7 %collective-permute-start.13 = (bf16[48,128]{1,0:T(8,128)(2,1)S(1)}, bf16[48,128]{1,0:T(8,128)(2,1)S(1)}, u32[]{:S(2)}, u32[]{:S(2)}) collective-permute-start(bf16[48,128]{1,0:T(8,128)(2,1)S(1)} %get-tuple-element.69), channel_id=1, source_target_pairs={{0,4},{1,5},{2,6},{3,7},{4,0},{5,1},{6,2},{7,3},{8,12},{9,13},{10,... | collective-permute-start | bytes 36872 | tf_op jit(solution)/shard_map/ppermute | solution.py:524
  33.2 5.6 %collective-permute-start.14 = (bf16[48,128]{1,0:T(8,128)(2,1)S(1)}, bf16[48,128]{1,0:T(8,128)(2,1)S(1)}, u32[]{:S(2)}, u32[]{:S(2)}) collective-permute-start(bf16[48,128]{1,0:T(8,128)(2,1)S(1)} %get-tuple-element.70), channel_id=1, source_target_pairs={{0,12},{1,13},{2,14},{3,15},{4,8},{5,9},{6,10},{7,11},{8,4},{9,5},... | collective-permute-start | bytes 36872 | tf_op jit(solution)/shard_map/ppermute | solution.py:524
  36.4 3.8 %copy-start.6 = (bf16[9,48,48]{2,1,0:T(8,128)(2,1)S(1)}, bf16[9,48,48]{2,1,0:T(8,128)(2,1)}, u32[]{:S(2)}) copy-start(bf16[9,48,48]{2,1,0:T(8,128)(2,1)} %w_ref.3) | copy-start | bytes 124420
  40.2 0.7 %copy-start.9 = (f32[48]{0:T(128)S(1)}, f32[48]{0:T(128)}, u32[]{:S(2)}) copy-start(f32[48]{0:T(128)} %param.13) | copy-start | bytes 580
  42.7 1.3 %collective-permute-start.15 = (f32[24,512]{1,0:T(8,128)S(1)}, f32[24,512]{1,0:T(8,128)S(1)}, u32[]{:S(2)}, u32[]{:S(2)}) collective-permute-start(f32[24,512]{1,0:T(8,128)S(1)} %add_bitcast_fusion.own), channel_id=1, source_target_pairs={{0,1},{1,0},{2,3},{3,2},{4,5},{5,4},{6,7},{7,6},{8,9},{9,8},{10,11... | collective-permute-start | bytes 147464 | tf_op jit(solution)/shard_map/ppermute | solution.py:528

commit v2 on v1

--- a/solution.py
+++ b/solution.py
@@ -16,7 +16,6 @@
 TILES = PIX // LANES
 
 VMEM = pl.BlockSpec(memory_space=pltpu.VMEM)
-SMEM = pl.BlockSpec(memory_space=pltpu.SMEM)
 
 
 def tap_of(edge, step):
@@ -108,7 +107,7 @@
 
 def by_edge(spaces, swaps):
     _, even, inner = roles(spaces)
-    m1, m2, n1, n2 = [ref[...].astype(F32) for ref in swaps]
+    m1, m2, n1, n2 = [ref[0:C].astype(F32) for ref in swaps]
     order = (
         jnp.where(even, m2, m1),
         jnp.where(inner, n1, n2),
@@ -124,7 +123,9 @@
 CHUNKS = 4
 
 
-def send_kernel(spaces, tables_hbm, x_hbm, g_hbm, m1, m2, n1, n2, tables, x_ref, g_ref, table_sem, x_sem, g_sem):
+def send_kernel(
+    spaces, tables_hbm, x_hbm, g_hbm, m1, m2, n1, n2, x_ref, g_ref, tables, table_sem, x_sem, g_sem,
+):
     wide = PIX // CHUNKS
     fetch = pltpu.make_async_copy(tables_hbm, tables, table_sem)
     fetch.start()
@@ -184,21 +185,20 @@
 
 
 def halo_matrix(rules, me, step):
-    row = iota((256, 256), 0)
-    line, place = line_lanes(iota((1, 256), 1))
+    row = iota((256, LANES), 0)
+    line, place = line_lanes(iota((1, LANES), 1) + LANES)
     at = place + step - 1
     inside = (at >= 0) & (at < 64)
     value = jnp.where(inside & (row == line * 64 + at), 1.0, 0.0)
-    side = (line == 3) | (line == 1)
     left = line == 3
     if step != 1:
         if step == 0:
-            active = side & (place == 0)
+            active = place == 0
             row_a = jnp.where(left, 0, 63)
             row_b = jnp.where(left, 192, 64)
             pair = (0, 1)
         else:
-            active = side & (place == 63)
+            active = place == 63
             row_a = jnp.where(left, 128, 191)
             row_b = jnp.where(left, 255, 127)
             pair = (2, 3)
@@ -207,6 +207,24 @@
         value = value + jnp.where(active & (row == row_a), jnp.where(left, fl, fr), 0.0)
         value = value + jnp.where(active & (row == row_b), jnp.where(left, sl, sr), 0.0)
     return value.astype(BF)
+
+
+def beside_lines(lines, halo):
+    columns = dot(lines, halo[...]).astype(BF)
+    low = iota((C, LANES), 1) < 64
+    at_left, at_right = lane_masks()
+    upper = lines[:, 0:LANES].astype(F32)
+    lower = lines[:, LANES:].astype(F32)
+    rows = jnp.where(low, upper, pltpu.roll(lower, 64, 1))
+    moved = (
+        jnp.where(at_left, 0.0, pltpu.roll(rows, 1, 1)),
+        rows,
+        jnp.where(at_right, 0.0, pltpu.roll(rows, LANES - 1, 1)),
+    )
+    parts = [
+        jnp.concatenate([moved[s].astype(BF), columns[:, s * LANES : (s + 1) * LANES]], axis=1) for s in range(3)
+    ]
+    return jnp.concatenate(parts, axis=0)
 
 
 def half_shift(dst, ref, before, after):
@@ -271,15 +289,27 @@
 
 
 def prepare_kernel(
-    spaces, tables, rules, x_ref, g_ref, w1_ref, w2_ref,
-    d_act, pre_in, x_side, route, halo, wf1, wr1, back2, half,
+    spaces, tables_hbm, rules_hbm, x_ref, g_ref, w1_ref, w2_ref, b1_ref, b2_ref,
+    d_act, pre_in, x_side, route, halo, w_edge, back2, w1_out, w2_out, b1_out, b2_out,
+    half, tables, rules, table_sem,
 ):
+    fetches = [
+        pltpu.make_async_copy(tables_hbm, tables, table_sem.at[0]),
+        pltpu.make_async_copy(rules_hbm, rules, table_sem.at[1]),
+    ]
+    for fetch in fetches:
+        fetch.start()
     me = lax.axis_index("space")
     taps1 = float_taps(w1_ref)
     taps2 = float_taps(w2_ref)
-    wf1[...] = forward_form(taps1)
-    wr1[...] = row_form(taps1)
+    wf1 = forward_form(taps1)
+    w_edge[0 : 2 * C] = row_form(taps1)
+    w_edge[2 * C :] = jnp.concatenate([wf1[0:C], wf1[2 * C : 3 * C]], axis=0)
     back2[...] = return_form(taps2)
+    w1_out[...] = w1_ref[...]
+    w2_out[...] = w2_ref[...]
+    b1_out[...] = column(b1_ref)
+    b2_out[...] = column(b2_ref)
     zero = jnp.zeros((C, LANES), BF)
     half_shift(half, g_ref, zero, zero)
 
@@ -291,24 +321,25 @@
 
     conv_tiles(backward_form(taps2), half, g_ref, None, keep(d_act))
     half_shift(half, x_ref, zero, zero)
-    conv_tiles(wf1[...], half, x_ref, None, keep(pre_in))
+    conv_tiles(wf1, half, x_ref, None, keep(pre_in))
     at_left, at_right = lane_masks()
     for t in range(TILES):
         at = slice(t * LANES, (t + 1) * LANES)
         x = tile(x_ref, t).astype(F32)
         x_side[0:C, at] = jnp.where(at_left, 0.0, pltpu.roll(x, 1, 1)).astype(BF)
         x_side[C : 2 * C, at] = jnp.where(at_right, 0.0, pltpu.roll(x, LANES - 1, 1)).astype(BF)
+    for fetch in fetches:
+        fetch.wait()
     for edge in range(4):
         for step in range(3):
             route[edge, :, step * 256 : (step + 1) * 256] = user_matrix(tables, rules, me, spaces, edge, step)
     for step in range(3):
-        halo[:, step * 256 : (step + 1) * 256] = halo_matrix(rules, me, step)
-
-
-def edge_terms(wf, wr, beside):
-    stacked = jnp.concatenate([beside[:, s * 256 : (s + 1) * 256] for s in range(3)], axis=0)
-    rows = dot(wr, stacked[:, 0:LANES])
-    sides = dot(jnp.concatenate([wf[0:C], wf[2 * C : 3 * C]], axis=0), stacked[:, LANES:])
+        halo[:, step * LANES : (step + 1) * LANES] = halo_matrix(rules, me, step)
+
+
+def edge_terms(w_sides, w_rows, stacked):
+    rows = dot(w_rows, stacked[:, 0:LANES])
+    sides = dot(w_sides, stacked[:, LANES:])
     lane = iota((C, LANES), 1)
     rows = jnp.where(lane < 64, rows[0:C], rows[C : 2 * C])
     return rows, jnp.where((lane & 1) == 0, sides[0:C], sides[C : 2 * C])
@@ -334,19 +365,21 @@
 
 
 def middle_kernel(
-    spaces, tables, m1, m2, n1, n2, d_act, pre_in, route, halo, wf, wr, back, bias,
-    act_ref, d_ref, p0, p1, p2, p3, beside_ref, users_ref, act_lines, d_lines,
+    spaces, tables_hbm, m1, m2, n1, n2, d_act, pre_in, route, halo, w_edge, back, bias,
+    act_ref, d_ref, p0, p1, p2, p3, beside_ref, users_ref, act_lines, d_lines, tables, table_sem,
 ):
+    fetch = pltpu.make_async_copy(tables_hbm, tables, table_sem)
+    fetch.start()
     lines, borders = by_edge(spaces, (m1, m2, n1, n2))
-    beside = dot(lines, halo[...]).astype(BF)
+    beside = beside_lines(lines, halo)
     beside_ref[...] = beside
-    rows, sides = edge_terms(wf[...], wr[...], beside)
+    rows, sides = edge_terms(w_edge[2 * C :], w_edge[0 : 2 * C], beside)
     users = users_values(route, borders)
     users_ref[...] = users
     line_grads = dot(back[...], users)
     d_rows = line_grads[:, 0:LANES]
     d_sides = line_grads[:, LANES : 2 * LANES]
-    bias_now = column(bias)
+    bias_now = bias[...]
     act_edges = []
     d_edges = []
     ends = {}
@@ -374,6 +407,7 @@
     act_lines[...] = act_l
     d_lines[...] = d_l
     both = jnp.concatenate([act_l, d_l], axis=1)
+    fetch.wait()
     for out, matrix in zip((p0, p1, p2, p3), send_matrices(tables, spaces)):
         out[...] = dot(both, matrix).astype(BF)
 
@@ -413,7 +447,7 @@
     line, _ = line_lanes(iota((C, 256), 1))
     d_l = d_lines[...].astype(F32)
     d_by_edge = jnp.concatenate([jnp.where(line == e, d_l, 0.0) for e in range(4)], axis=0).astype(BF)
-    near_one[...] = dot_nt(d_by_edge, jnp.concatenate([beside[:, s * 256 : (s + 1) * 256] for s in range(3)], axis=0))
+    near_one[...] = dot_nt(d_by_edge, beside[...])
     near_two[...] = dot_nt(users[...], act_lines[...])
 
     def block_one(a, b):
@@ -444,8 +478,9 @@
     give = jnp.where(even, second, first)
     share = C // parts
     for part in range(parts):
-        mine[part] = keep[part * share : (part + 1) * share]
-        other[part] = give[part * share : (part + 1) * share]
+        at = slice(part * share, (part + 1) * share)
+        mine[part] = jnp.concatenate([keep[at, j * LANES : (j + 1) * LANES] for j in range(WIDE // LANES)], axis=0)
+        other[part] = jnp.concatenate([give[at, j * LANES : (j + 1) * LANES] for j in range(WIDE // LANES)], axis=0)
 
 
 def inner_kernel(g_ref, d_ref, w_ref, d_in, half):
@@ -459,35 +494,41 @@
     conv_tiles(backward_form(float_taps(w_ref)), half, d_ref, None, visit)
 
 
-def output_kernel(spaces, x_ref, act_ref, m1, m2, n1, n2, halo, w_ref, bias, out, half):
-    lines, _ = by_edge(spaces, (m1, m2, n1, n2))
-    taps = float_taps(w_ref)
+def partial_kernel(x_ref, act_ref, w1_ref, w2_ref, bias, out, sides, back, half):
+    taps = float_taps(w2_ref)
     wf = forward_form(taps)
+    sides[0 : 2 * C] = row_form(taps)
+    sides[2 * C :] = jnp.concatenate([wf[0:C], wf[2 * C : 3 * C]], axis=0)
+    back[...] = return_form(float_taps(w1_ref))
     zero = jnp.zeros((C, LANES), BF)
     half_shift(half, act_ref, zero, zero)
-    beside = dot(lines, halo[...]).astype(BF)
-    rows, sides = edge_terms(wf, row_form(taps), beside)
-    bias_now = column(bias)
+    bias_now = bias[...]
 
     def visit(t, value):
         at = slice(t * LANES, (t + 1) * LANES)
-        out[:, at] = (add_edges(t, value, rows, sides) + bias_now + x_ref[:, at].astype(F32)).astype(BF)
+        out[:, at] = value + bias_now + x_ref[:, at].astype(F32)
 
     conv_tiles(wf, half, act_ref, None, visit)
 
 
-def grad_in_kernel(spaces, d_in, m1, m2, n1, n2, route, w_ref, out):
-    _, borders = by_edge(spaces, (m1, m2, n1, n2))
-    line_grads = dot(return_form(float_taps(w_ref)), users_values(route, borders))
+def finish_kernel(spaces, partial, d_in, m1, m2, n1, n2, halo, route, sides_ref, back, out, grad_in):
+    lines, borders = by_edge(spaces, (m1, m2, n1, n2))
+    rows, sides = edge_terms(sides_ref[2 * C :], sides_ref[0 : 2 * C], beside_lines(lines, halo))
+    line_grads = dot(back[...], users_values(route, borders))
     for t in range(TILES):
         at = slice(t * LANES, (t + 1) * LANES)
-        out[:, at] = add_edges(t, d_in[:, at], line_grads[:, 0:LANES], line_grads[:, LANES : 2 * LANES]).astype(BF)
+        out[:, at] = add_edges(t, partial[:, at], rows, sides).astype(BF)
+        grad_in[:, at] = add_edges(t, d_in[:, at], line_grads[:, 0:LANES], line_grads[:, LANES : 2 * LANES]).astype(BF)
 
 
 def unpack_kernel(share, own, got, grad_one, bias_one, grad_two, bias_two):
     even = (lax.axis_index("space") % 2) == 0
-    first = jnp.where(even, own[...], got[...])
-    second = jnp.where(even, got[...], own[...])
+    one = jnp.where(even, own[...], got[...])
+    two = jnp.where(even, got[...], own[...])
+    first, second = [
+        jnp.concatenate([value[j * share : (j + 1) * share] for j in range(WIDE // LANES)], axis=1)
+        for value in (one, two)
+    ]
     eye = iota((share, LANES), 0) == iota((share, LANES), 1)
     for value, grad, bias in ((first, grad_one, bias_one), (second, grad_two, bias_two)):
         for tap in range(9):
@@ -511,55 +552,70 @@
 HBM = pl.BlockSpec(memory_space=pltpu.HBM)
 
 
-def exchange(blocks, spaces):
-    hop = spaces // 4
-
-    def first(i, step):
-        return (i + step) % spaces if (i // step) % 2 == 0 else (i - step) % spaces
-
-    def second(i, step):
-        return (i - step) % spaces if (i // step) % 2 == 0 else (i + step) % spaces
-
-    partner = (lambda i: first(i, 1), lambda i: second(i, 1), lambda i: first(i, hop), lambda i: second(i, hop))
-    return [lax.ppermute(b, "space", [(i, to(i)) for i in range(spaces)]) for b, to in zip(blocks, partner)]
+def in_hbm(value):
+    return pltpu.with_memory_space_constraint(value, pltpu.HBM)
 
 
 def swapped(block, mask, devices):
     return lax.ppermute(block, ("dp", "space"), [(i, i ^ mask) for i in range(devices)])
 
 
-def total_over_chips(held, parts, spaces):
-    devices = parts * spaces
-    part_bits = [1 << bit for bit in reversed(range(parts.bit_length() - 1))]
-    space_bits = [1 << bit for bit in range(1, spaces.bit_length() - 1)]
-    rounds = [[(True, bit)] for bit in part_bits]
-    for bit in space_bits:
-        if len(rounds[-1]) == 1:
-            rounds[-1].append((False, bit))
-        elif len(rounds[0]) == 1:
-            next(r for r in rounds if len(r) == 1).append((False, bit))
+def swap_along(blocks, spaces, more=1):
+    def second(i):
+        return (i - 1) % spaces if i % 2 == 0 else (i + 1) % spaces
+
+    return [
+        lax.ppermute(blocks[0], "space", [(i, i ^ 1) for i in range(spaces)]),
+        lax.ppermute(jnp.concatenate([blocks[1]] * more, axis=0) if more > 1 else blocks[1], "space", [(i, second(i)) for i in range(spaces)]),
+    ]
+
+
+def swap_across(blocks, spaces, devices):
+    hop = spaces // 4
+    return [swapped(blocks[0], hop, devices), swapped(blocks[1], hop ^ 2 * hop, devices)]
+
+
+def first_rounds(parts, spaces):
+    rounds = [[(True, 1 << bit)] for bit in reversed(range(parts.bit_length() - 1))]
+    bit = 2
+    while bit < spaces // 4:
+        single = [r for r in rounds if len(r) == 1]
+        if single:
+            single[0].append((False, bit))
         else:
             rounds.append([(False, bit)])
+        bit *= 2
+    return rounds
+
+
+def total_of(a, b, c, d):
+    return (a.astype(F32) + b.astype(F32)) + (c.astype(F32) + d.astype(F32))
+
+
+def last_round(held, blocks, spaces, devices):
+    hop = spaces // 4
+    held = held.astype(BF)
+    joined = [jnp.concatenate([block, held], axis=0) for block in blocks]
+    near, far = swap_across(joined, spaces, devices)
+    opposite = swapped(held, 2 * hop, devices)
+    return near, far, total_of(held, near[C:], opposite, far[C:])
+
+
+def reduced(held, bits, devices, spaces, beside):
     where = lax.axis_index("dp")
-    for bits in rounds:
-        keep = give = held.astype(BF)
-        masks = []
-        for is_part, bit in bits:
-            masks.append(bit * spaces if is_part else bit)
-            if is_part:
-                upper = (where // bit) % 2 == 1
-                low, high = keep[: keep.shape[0] // 2], keep[keep.shape[0] // 2 :]
-                keep, give = jnp.where(upper, high, low), jnp.where(upper, low, high)
-        split = bits[0][0]
-        got = [swapped(give if split else keep, masks[0], devices)]
-        if len(masks) == 2:
-            got.append(swapped(keep, masks[1], devices))
-            got.append(swapped(give if split else keep, masks[0] ^ masks[1], devices))
-        terms = [value.astype(F32) for value in [keep] + got]
-        held = terms[0] + terms[1]
-        if len(masks) == 2:
-            held = held + (terms[2] + terms[3])
-    return held[0]
+    keep = give = held.astype(BF)
+    masks = []
+    for is_part, bit in bits:
+        masks.append(bit * spaces if is_part else bit)
+        if is_part:
+            upper = (where // bit) % 2 == 1
+            low, high = keep[: keep.shape[0] // 2], keep[keep.shape[0] // 2 :]
+            keep, give = jnp.where(upper, high, low), jnp.where(upper, low, high)
+    first = swapped(give, masks[0], devices)
+    kept, *beside = lax.optimization_barrier((keep, *beside))
+    if len(masks) == 1:
+        return kept.astype(F32) + first.astype(F32), beside
+    return total_of(kept, first, swapped(keep, masks[1], devices), swapped(give, masks[0] ^ masks[1], devices)), beside
 
 
 COST = 3_690_000
@@ -578,32 +634,38 @@
     tables = neighbours.transpose(2, 1, 0)
     rules = corner_rule.transpose(1, 0)
 
-    sent = call(
-        functools.partial(send_kernel, spaces), [line] * 4, [HBM, HBM, HBM], (tables, x, g),
-        [pltpu.SMEM(tables.shape, jnp.int32), pltpu.VMEM((C, PIX), BF), pltpu.VMEM((C, PIX), BF),
-         pltpu.SemaphoreType.DMA, pltpu.SemaphoreType.DMA((CHUNKS,)), pltpu.SemaphoreType.DMA((CHUNKS,))],
-        read=COST * 2, room=66_900_000,
-    )
-    arrived = exchange(sent, spaces)
-    square = ((3 * C, 3 * C), BF)
-    rows = ((2 * C, 3 * C), BF)
+    weights = (conv_one.shape, BF)
+    bias = ((C, LANES), F32)
+    *sent, x_near, g_near = call(
+        functools.partial(send_kernel, spaces), [line] * 4 + [image, image], [HBM] * 3, (in_hbm(tables), in_hbm(x), in_hbm(g)),
+        [pltpu.SMEM(tables.shape, jnp.int32), pltpu.SemaphoreType.DMA, pltpu.SemaphoreType.DMA((CHUNKS,)),
+         pltpu.SemaphoreType.DMA((CHUNKS,))],
+        read=COST * 2,
+    )
+    devices = parts * spaces
+    arrived = swap_along(sent[:2], spaces, 4) + swap_across(sent[2:], spaces, devices)
+    edges = ((4 * C, 3 * C), BF)
     back = ((C, 12 * C), BF)
-    d_act, pre_in, x_side, route, halo, wf1, wr1, back2 = call(
+    d_act, pre_in, x_side, route, halo, w_edge, back2, w_one, w_two, b_one, b_two = call(
         functools.partial(prepare_kernel, spaces),
-        [wide, wide, ((2 * C, PIX), BF), ((4, SIDE, 768), BF), ((256, 768), BF), square, rows, back],
-        [SMEM, SMEM, VMEM, VMEM, VMEM, VMEM],
-        (tables, rules, x, g, conv_one, conv_two), [half], read=COST * 3,
+        [wide, wide, ((2 * C, PIX), BF), ((4, SIDE, 768), BF), ((256, 384), BF), edges, back,
+         weights, weights, bias, bias],
+        [HBM, HBM] + [VMEM] * 6,
+        (in_hbm(tables), in_hbm(rules), x_near, g_near, conv_one, conv_two, bias_one.reshape(1, C), bias_two.reshape(1, C)),
+        [half, pltpu.SMEM(tables.shape, jnp.int32), pltpu.SMEM(rules.shape, jnp.int32), pltpu.SemaphoreType.DMA((2,))],
+        read=COST * 3,
     )
     middle = call(
         functools.partial(middle_kernel, spaces),
-        [image, image] + [line] * 4 + [((C, 768), BF), ((12 * C, 256), BF), ((C, 256), BF), ((C, 256), BF)],
-        [SMEM] + [VMEM] * 12,
-        (tables, *arrived, d_act, pre_in, route, halo, wf1, wr1, back2, bias_one.reshape(1, C)),
+        [image, image] + [line] * 4 + [((3 * C, 256), BF), ((12 * C, 256), BF), ((C, 256), BF), ((C, 256), BF)],
+        [HBM] + [VMEM] * 11,
+        (in_hbm(tables), *arrived, d_act, pre_in, route, halo, w_edge, back2, b_one),
+        [pltpu.SMEM(tables.shape, jnp.int32), pltpu.SemaphoreType.DMA],
         read=COST * 9 // 4,
     )
     act, d_pre = middle[:2]
     beside, users, act_lines, d_lines = middle[6:]
-    packed = ((parts, share, WIDE), F32)
+    packed = ((parts, share * WIDE // LANES, LANES), F32)
     mine, other = call(
         functools.partial(grads_kernel, parts), [packed, packed], [VMEM] * 9,
         (x, g, act, d_pre, x_side, beside, users, act_lines, d_lines),
@@ -611,22 +673,22 @@
          pltpu.VMEM((4 * C, 3 * C), F32), pltpu.VMEM((12 * C, C), F32)],
         read=COST * 5 // 4,
     )
-    devices = parts * spaces
+    (d_in,) = call(inner_kernel, [wide], [VMEM] * 3, (g, d_pre, w_one), [half], read=COST)
+    partial, edges_two, back_one = call(
+        partial_kernel, [wide, edges, back], [VMEM] * 5, (x, act, w_one, w_two, b_two), [half], read=COST * 3 // 2
+    )
     held = mine + swapped(other, 1, devices)
-    held, *blocks = lax.optimization_barrier((held, *middle[2:6]))
-    again = exchange(blocks, spaces)
-    own = total_over_chips(held, parts, spaces)
-    (d_in,) = call(inner_kernel, [wide], [VMEM] * 3, (g, d_pre, conv_one), [half], read=COST)
-    (output,) = call(
-        functools.partial(output_kernel, spaces), [image], [VMEM] * 9,
-        (x, act, *again, halo, conv_two, bias_two.reshape(1, C)), [half], read=COST * 3 // 2,
-    )
-    (grad_in,) = call(
-        functools.partial(grad_in_kernel, spaces), [image], [VMEM] * 7, (d_in, *again, route, conv_one),
-        read=COST * 7 // 4,
-    )
-    own, output, grad_in = lax.optimization_barrier((own, output, grad_in))
+    held, d_in, *blocks = lax.optimization_barrier((held, d_in, *middle[2:6]))
+    again = swap_along(blocks[:2], spaces, 4)
+    for bits in first_rounds(parts, spaces):
+        held, again = reduced(held, bits, devices, spaces, again)
+    held, partial = lax.optimization_barrier((held, partial))
+    near, far, own = last_round(held[0], blocks[2:], spaces, devices)
     got = swapped(own, 1, devices)
+    output, grad_in = call(
+        functools.partial(finish_kernel, spaces), [image, image], [VMEM] * 10,
+        (partial, d_in, *again, near, far, halo, route, edges_two, back_one), read=COST * 3 // 2,
+    )
     taps = ((9, share, C), F32)
     bias = ((1, share), F32)
     grad_one, sum_one, grad_two, sum_two = call(

time: 45.1 us -> 36.8 us (0.82)
  local copies, waits for them, and re-layouts: 4.21 us -> 0.68 us
  starting transfers between devices: 20.1 us -> 16.9 us
  Pallas kernels: 13.7 us -> 11.8 us
    ppermute x8 -> x4, starting transfers between devices: 11.9 us -> 7.97 us  [the longest x2 7.97 us: swap_along(): lax.ppermute(jnp.concatenate([blocks[1]] * more, axis=0) if more > 1 else...]
    unnamed x22 -> x12, local copies, waits for them, and re-layouts: 4.21 us -> 0.68 us
    ppermute x8 -> x10, waiting for transfers between devices: 3.55 us -> 5.91 us  [swapped(): lax.ppermute(block, ('dp', 'space'), [(i, i ^ mask) for i in range(device...]
    ppermute x8 -> x4, waiting for transfers between devices: 2.35 us -> 0.34 us  [the longest x2 0.34 us: swap_along(): lax.ppermute(blocks[0], 'space', [(i, i ^ 1) for i in range(spaces)])]
    pallas_call x8, Pallas kernels: 13.7 us -> 11.8 us  [call(): pl.pallas_call(kernel, out_shape=[jax.ShapeDtypeStruct(shape, dtype) for...]
    ppermute x8 -> x10, starting transfers between devices: 8.15 us -> 8.92 us  [swapped(): lax.ppermute(block, ('dp', 'space'), [(i, i ^ mask) for i in range(device...]
  transfers between devices with their start and end apart: 16 -> 14, of which waited for: 5 -> 6; matrix products, arithmetic and copies ran while one was open for 0% -> 0% of each run, Pallas kernels for 16% -> 16%
where the time goes in v2:
time: 36.8 us; the launch traced here: 36.5 us
  starting transfers between devices  16.9 us (46%)
  Pallas kernels  11.8 us (32%)
  waiting for transfers between devices  6.25 us (17%)
  between operations  0.81 us (2%)
  local copies, waits for them, and re-layouts  0.68 us (2%)
    pallas_call x8, Pallas kernels, call(): pl.pallas_call(kernel, out_shape=[jax.ShapeDtypeStruct(shape, dtype) for...  11.8 us
    ppermute x10, starting transfers between devices, swapped(): lax.ppermute(block, ('dp', 'space'), [(i, i ^ mask) for i in range(device...  8.92 us
    ppermute x2, starting transfers between devices, swap_along(): lax.ppermute(jnp.concatenate([blocks[1]] * more, axis=0) if more > 1 else...  7.97 us
    ppermute x10, waiting for transfers between devices, swapped(): lax.ppermute(block, ('dp', 'space'), [(i, i ^ mask) for i in range(device...  5.91 us
  transfers between devices with their start and end apart: 14, of which 6 were waited for; matrix products, arithmetic and copies ran while one was open for 0% of the time, Pallas kernels for 16%

profile of v2, /device:TPU:0, one launch (start us, length us, event | category | flops | bytes accessed | tf_op | source)
XLA Modules:
  0.0 36.5 jit_solution(15954473006400485994)
XLA Ops:
  0.6 0.0 copy-start.2
  0.6 0.0 copy-start.3
  0.7 1.8 %shard_map.127 = (bf16[48,128]{1,0:T(8,128)(2,1)S(1)}, bf16[48,128]{1,0:T(8,128)(2,1)S(1)}, bf16[48,128]{1,0:T(8,128)(2,1)S(1)}, bf16[48,128]{1,0:T(8,128)(2,1)S...) custom-call(s32[3,4,16]{2,1,0:T(4,128)} %bitcast.24, bf16[48,4096]{1,0:T(8,128)(2,1)} %bitcast.17, ...), custom_call_target="tpu_custom_call" | custom-call | bytes 7380000 | tf_op jit(solution)/shard_map/pallas_call | solution.py:541
  2.4 5.5 %collective-permute-start.1 = (bf16[192,128]{1,0:T(8,128)(2,1)S(1)}, bf16[192,128]{1,0:T(8,128)(2,1)S(1)}, u32[]{:S(2)}, u32[]{:S(2)}) collective-permute-start(bf16[192,128]{1,0:T(8,128)(2,1)S(1)} %pad_maximum_fusion), channel_id=1, source_target_pairs={{0,15},{1,2},{2,1},{3,4},{4,3},{5,6},{6,5},{7,8},{8,7},{9,10},{10,... | collective-permute-start | bytes 147464 | tf_op jit(solution)/shard_map/ppermute | solution.py:569
  7.9 0.0 collective-permute-start
  7.9 0.0 collective-permute-start.2
  7.9 1.7 %collective-permute-start.3 = (bf16[48,128]{1,0:T(8,128)(2,1)S(1)}, bf16[48,128]{1,0:T(8,128)(2,1)S(1)}, u32[]{:S(2)}, u32[]{:S(2)}) collective-permute-start(bf16[48,128]{1,0:T(8,128)(2,1)S(1)} %get-tuple-element.58), channel_id=1, source_target_pairs={{0,12},{1,13},{2,14},{3,15},{4,8},{5,9},{6,10},{7,11},{8,4},{9,5},... | collective-permute-start | bytes 36872 | tf_op jit(solution)/shard_map/ppermute | solution.py:560
  9.6 0.0 copy-start.4
  9.6 0.0 copy-start.5
  9.6 0.0 copy-done.2
  9.6 0.0 copy-done.3
  9.6 0.6 %copy-done.4 = f32[48]{0:T(128)S(1)} copy-done((f32[48]{0:T(128)S(1)}, f32[48]{0:T(128)}, u32[]{:S(2)}) %copy-start.4) | copy-done | bytes 216
  10.3 0.0 copy-done.5
  10.3 2.3 %shard_map.128 = (f32[48,4096]{1,0:T(8,128)S(1)}, f32[48,4096]{1,0:T(8,128)S(1)}, bf16[96,4096]{1,0:T(8,128)(2,1)S(1)}, bf16[4,64,768]{2,1,0:T(8,128)(2,1)S(1)},...) custom-call(s32[3,4,16]{2,1,0:T(4,128)} %bitcast.25, ...), custom_call_target="tpu_custom_call" | custom-call | bytes 11070000 | tf_op jit(solution)/shard_map/pallas_call | solution.py:541
  12.6 0.0 collective-permute-done.m1
  12.6 0.0 collective-permute-done.2.n1
  12.6 0.8 %collective-permute-done.3.n2 = bf16[48,128]{1,0:T(8,128)(2,1)S(1)} collective-permute-done((bf16[48,128]{1,0:T(8,128)(2,1)S(1)}, bf16[48,128]{1,0:T(8,128)(2,1)S(1)}, u32[]{:S(2)}, u32[]{:S(2)}) %collective-permute-start.3) | collective-permute-done | bytes 12320 | tf_op jit(solution)/shard_map/ppermute | solution.py:560
  13.4 0.0 collective-permute-done.1.m2
  13.4 0.0 copy-start
  13.4 0.0 copy-start.1
  13.4 2.3 %shard_map.129 = (bf16[48,4096]{1,0:T(8,128)(2,1)S(1)}, bf16[48,4096]{1,0:T(8,128)(2,1)S(1)}, bf16[48,128]{1,0:T(8,128)(2,1)S(1)}, bf16[48,128]{1,0:T(8,128)(2,1...) custom-call(s32[3,4,16]{2,1,0:T(4,128)} %bitcast.26, ...), custom_call_target="tpu_custom_call" | custom-call | bytes 8302500 | tf_op jit(solution)/shard_map/pallas_call | solution.py:541
  15.8 0.0 copy-done
  15.8 0.0 copy-done.1
  15.8 1.3 %shard_map.130 = (f32[2,96,128]{2,1,0:T(8,128)S(1)}, f32[2,96,128]{2,1,0:T(8,128)S(1)}) custom-call(bf16[48,4096]{1,0:T(8,128)(2,1)S(1)} %bitcast.18, bf16[48,4096]{1,0:T(8,128)(2,1)S(1)} %bitcast.15, bf16[48,4096]{1,0:T(8,128)(2,1)S(1)} %get-tuple-element.68.act_ref, bf16[48,4096]{1,0:T(8,128)(2,1)S(1)} %get-tuple-element.69.d_ref, ...), custom_call_target="tpu_custom_call" | custom-call | bytes 4612500 | tf_op jit(solution)/shard_map/pallas_call | solution.py:541
  17.0 0.1 collective-permute-start.4
  17.1 0.9 %shard_map.131.d_in = f32[48,4096]{1,0:T(8,128)S(1)} custom-call(bf16[48,4096]{1,0:T(8,128)(2,1)S(1)} %bitcast.16, bf16[48,4096]{1,0:T(8,128)(2,1)S(1)} %get-tuple-element.69.d_ref, bf16[9,48,48]{2,1,0:T(8,128)(2,1)S(1)} %get-tuple-element.77.w_ref.w1_ref), custom_call_target="tpu_custom_call" | custom-call | bytes 3690000 | tf_op jit(solution)/shard_map/pallas_call | solution.py:541
  18.0 0.4 %collective-permute-done.4 = f32[2,96,128]{2,1,0:T(8,128)S(1)} collective-permute-done((f32[2,96,128]{2,1,0:T(8,128)S(1)}, f32[2,96,128]{2,1,0:T(8,128)S(1)}, u32[]{:S(2)}, u32[]{:S(2)}) %collective-permute-start.4) | collective-permute-done | bytes 98336 | tf_op jit(solution)/shard_map/ppermute | solution.py:560
  18.4 2.5 %collective-permute-start.6 = (bf16[192,128]{1,0:T(8,128)(2,1)S(1)}, bf16[192,128]{1,0:T(8,128)(2,1)S(1)}, u32[]{:S(2)}, u32[]{:S(2)}) collective-permute-start(bf16[192,128]{1,0:T(8,128)(2,1)S(1)} %pad_maximum_fusion.1), channel_id=1, source_target_pairs={{0,15},{1,2},{2,1},{3,4},{4,3},{5,6},{6,5},{7,8},{8,7},{9,10},{10,... | collective-permute-start | bytes 147464 | tf_op jit(solution)/shard_map/ppermute | solution.py:569
  20.9 1.6 %collective-permute-start.7 = (bf16[1,96,128]{2,1,0:T(8,128)(2,1)S(1)}, bf16[1,96,128]{2,1,0:T(8,128)(2,1)S(1)}, u32[]{:S(2)}, u32[]{:S(2)}) collective-permute-start(bf16[1,96,128]{2,1,0:T(8,128)(2,1)S(1)} %get-tuple-element.105), channel_id=1, source_target_pairs={{0,16},{1,17},{2,18},{3,19},{4,20},{5,21},{6,22},{7,23},{8,24},{9,... | collective-permute-start | bytes 73736 | tf_op jit(solution)/shard_map/ppermute | solution.py:560
  22.5 0.0 collective-permute-start.8
  22.5 2.0 %collective-permute-start.9 = (bf16[1,96,128]{2,1,0:T(8,128)(2,1)S(1)}, bf16[1,96,128]{2,1,0:T(8,128)(2,1)S(1)}, u32[]{:S(2)}, u32[]{:S(2)}) collective-permute-start(bf16[1,96,128]{2,1,0:T(8,128)(2,1)S(1)} %get-tuple-element.105), channel_id=1, source_target_pairs={{0,18},{1,19},{2,16},{3,17},{4,22},{5,23},{6,20},{7,21},{8,26},{9,... | collective-permute-start | bytes 73736 | tf_op jit(solution)/shard_map/ppermute | solution.py:560
  24.5 0.0 collective-permute-start.5
  24.5 0.8 %shard_map.132 = (f32[48,4096]{1,0:T(8,128)S(1)}, bf16[192,144]{1,0:T(8,128)(2,1)S(1)}, bf16[48,576]{1,0:T(8,128)(2,1)S(1)}) custom-call(bf16[48,4096]{1,0:T(8,128)(2,1)S(1)} %bitcast.19, bf16[48,4096]{1,0:T(8,128)(2,1)S(1)} %get-tuple-element.68.act_ref, bf16[9,48,48]{2,1,0:T(8,128)(2,1)S(1)} %get-tuple-element.77.w_ref.w1_ref, ...), custom_call_target="tpu_custom_call" | custom-call | bytes 5535000 | tf_op jit(solution)/shard_map/pallas_call | solution.py:541
  25.3 0.3 collective-permute-done.5.m1
  25.7 0.0 collective-permute-done.6.m2
  25.7 0.0 collective-permute-done.7
  25.7 0.7 %collective-permute-done.8 = bf16[1,96,128]{2,1,0:T(8,128)(2,1)S(1)} collective-permute-done((bf16[1,96,128]{2,1,0:T(8,128)(2,1)S(1)}, bf16[1,96,128]{2,1,0:T(8,128)(2,1)S(1)}, u32[]{:S(2)}, u32[]{:S(2)}) %collective-permute-start.8) | collective-permute-done | bytes 24608 | tf_op jit(solution)/shard_map/ppermute | solution.py:560
  26.3 0.9 %collective-permute-done.9 = bf16[1,96,128]{2,1,0:T(8,128)(2,1)S(1)} collective-permute-done((bf16[1,96,128]{2,1,0:T(8,128)(2,1)S(1)}, bf16[1,96,128]{2,1,0:T(8,128)(2,1)S(1)}, u32[]{:S(2)}, u32[]{:S(2)}) %collective-permute-start.9) | collective-permute-done | bytes 24608 | tf_op jit(solution)/shard_map/ppermute | solution.py:560
  27.3 0.1 collective-permute-start.10
  27.4 1.8 %collective-permute-start.11 = (bf16[144,128]{1,0:T(8,128)(2,1)S(1)}, bf16[144,128]{1,0:T(8,128)(2,1)S(1)}, u32[]{:S(2)}, u32[]{:S(2)}) collective-permute-start(bf16[144,128]{1,0:T(8,128)(2,1)S(1)} %get-tuple-element.106), channel_id=1, source_target_pairs={{0,12},{1,13},{2,14},{3,15},{4,8},{5,9},{6,10},{7,11},{8,4},{9,5},... | collective-permute-start | bytes 110600 | tf_op jit(solution)/shard_map/ppermute | solution.py:560
  29.2 1.7 %collective-permute-start.12 = (bf16[96,128]{1,0:T(8,128)(2,1)S(1)}, bf16[96,128]{1,0:T(8,128)(2,1)S(1)}, u32[]{:S(2)}, u32[]{:S(2)}) collective-permute-start(bf16[96,128]{1,0:T(8,128)(2,1)S(1)} %bitcast.23), channel_id=1, source_target_pairs={{0,8},{1,9},{2,10},{3,11},{4,12},{5,13},{6,14},{7,15},{8,0},{9,1},... | collective-permute-start | bytes 73736 | tf_op jit(solution)/shard_map/ppermute | solution.py:560
  30.8 3.1 %collective-permute-done.12 = bf16[96,128]{1,0:T(8,128)(2,1)S(1)} collective-permute-done((bf16[96,128]{1,0:T(8,128)(2,1)S(1)}, bf16[96,128]{1,0:T(8,128)(2,1)S(1)}, u32[]{:S(2)}, u32[]{:S(2)}) %collective-permute-start.12) | collective-permute-done | bytes 24608 | tf_op jit(solution)/shard_map/ppermute | solution.py:560
  33.9 0.0 collective-permute-done.10.n1
  33.9 0.0 collective-permute-done.11.n2
  34.0 0.1 collective-permute-start.13
  34.0 1.7 %shard_map.133 = (bf16[48,4096]{1,0:T(8,128)(2,1)}, bf16[48,4096]{1,0:T(8,128)(2,1)}) custom-call(f32[48,4096]{1,0:T(8,128)S(1)} %get-tuple-element.89.partial, f32[48,4096]{1,0:T(8,128)S(1)} %shard_map.131.d_in, bf16[48,128]{1,0:T(8,128)(2,1)S(1)} %collective-permute-done.5.m1, bf16[192,128]{1,0:T(8,128)(2,1)S(1)} %collective-permute-done.6.m2, ...), custom_call_target="tpu_custom_call" | custom-call | bytes 5535000 | tf_op jit(solution)/shard_map/pallas_call | solution.py:541
  35.7 0.0 collective-permute-done.13.got
  35.7 0.8 %shard_map.134 = (f32[9,24,48]{2,1,0:T(8,128)}, f32[1,24]{1,0:T(1,128)}, f32[9,24,48]{2,1,0:T(8,128)}, f32[1,24]{1,0:T(1,128)}) custom-call(f32[96,128]{1,0:T(8,128)S(1)} %add_add_fusion.own, f32[96,128]{1,0:T(8,128)S(1)} %collective-permute-done.13.got), custom_call_target="tpu_custom_call" | custom-call | bytes 100000 | tf_op jit(solution)/shard_map/pallas_call | solution.py:541
  (7 shorter events, 0.1 us)
Async XLA Ops:
  0.6 9.0 %copy-start.2 = (bf16[9,48,48]{2,1,0:T(8,128)(2,1)S(1)}, bf16[9,48,48]{2,1,0:T(8,128)(2,1)}, u32[]{:S(2)}) copy-start(bf16[9,48,48]{2,1,0:T(8,128)(2,1)} %w1_ref.1) | copy-start | bytes 124420
  0.6 9.0 %copy-start.3 = (bf16[9,48,48]{2,1,0:T(8,128)(2,1)S(1)}, bf16[9,48,48]{2,1,0:T(8,128)(2,1)}, u32[]{:S(2)}) copy-start(bf16[9,48,48]{2,1,0:T(8,128)(2,1)} %w2_ref.1) | copy-start | bytes 124420
  2.4 11.0 %collective-permute-start.1 = (bf16[192,128]{1,0:T(8,128)(2,1)S(1)}, bf16[192,128]{1,0:T(8,128)(2,1)S(1)}, u32[]{:S(2)}, u32[]{:S(2)}) collective-permute-start(bf16[192,128]{1,0:T(8,128)(2,1)S(1)} %pad_maximum_fusion), channel_id=1, source_target_pairs={{0,15},{1,2},{2,1},{3,4},{4,3},{5,6},{6,5},{7,8},{8,7},{9,10},{10,... | collective-permute-start | bytes 147464 | tf_op jit(solution)/shard_map/ppermute | solution.py:569
  7.9 4.6 %collective-permute-start = (bf16[48,128]{1,0:T(8,128)(2,1)S(1)}, bf16[48,128]{1,0:T(8,128)(2,1)S(1)}, u32[]{:S(2)}, u32[]{:S(2)}) collective-permute-start(bf16[48,128]{1,0:T(8,128)(2,1)S(1)} %get-tuple-element.55), channel_id=1, source_target_pairs={{0,1},{1,0},{2,3},{3,2},{4,5},{5,4},{6,7},{7,6},{8,9},{9,8},{10,11... | collective-permute-start | bytes 36872 | tf_op jit(solution)/shard_map/ppermute | solution.py:568
  7.9 4.7 %collective-permute-start.2 = (bf16[48,128]{1,0:T(8,128)(2,1)S(1)}, bf16[48,128]{1,0:T(8,128)(2,1)S(1)}, u32[]{:S(2)}, u32[]{:S(2)}) collective-permute-start(bf16[48,128]{1,0:T(8,128)(2,1)S(1)} %get-tuple-element.57), channel_id=1, source_target_pairs={{0,4},{1,5},{2,6},{3,7},{4,0},{5,1},{6,2},{7,3},{8,12},{9,13},{10,... | collective-permute-start | bytes 36872 | tf_op jit(solution)/shard_map/ppermute | solution.py:560
  7.9 5.5 %collective-permute-start.3 = (bf16[48,128]{1,0:T(8,128)(2,1)S(1)}, bf16[48,128]{1,0:T(8,128)(2,1)S(1)}, u32[]{:S(2)}, u32[]{:S(2)}) collective-permute-start(bf16[48,128]{1,0:T(8,128)(2,1)S(1)} %get-tuple-element.58), channel_id=1, source_target_pairs={{0,12},{1,13},{2,14},{3,15},{4,8},{5,9},{6,10},{7,11},{8,4},{9,5},... | collective-permute-start | bytes 36872 | tf_op jit(solution)/shard_map/ppermute | solution.py:560
  9.6 0.7 %copy-start.4 = (f32[48]{0:T(128)S(1)}, f32[48]{0:T(128)}, u32[]{:S(2)}) copy-start(f32[48]{0:T(128)} %param.11) | copy-start | bytes 580
  9.6 0.7 %copy-start.5 = (f32[48]{0:T(128)S(1)}, f32[48]{0:T(128)}, u32[]{:S(2)}) copy-start(f32[48]{0:T(128)} %param.13) | copy-start | bytes 580
  13.4 2.3 %copy-start = (bf16[1,1,48,4096]{3,2,1,0:T(8,128)(2,1)S(1)}, bf16[1,1,48,4096]{3,2,1,0:T(8,128)(2,1)}, u32[]{:S(2)}) copy-start(bf16[1,1,48,4096]{3,2,1,0:T(8,128)(2,1)} %param.9) | copy-start | bytes 1179652
  13.4 2.3 %copy-start.1 = (bf16[1,1,48,4096]{3,2,1,0:T(8,128)(2,1)S(1)}, bf16[1,1,48,4096]{3,2,1,0:T(8,128)(2,1)}, u32[]{:S(2)}) copy-start(bf16[1,1,48,4096]{3,2,1,0:T(8,128)(2,1)} %param.8) | copy-start | bytes 1179652
  17.0 1.4 %collective-permute-start.4 = (f32[2,96,128]{2,1,0:T(8,128)S(1)}, f32[2,96,128]{2,1,0:T(8,128)S(1)}, u32[]{:S(2)}, u32[]{:S(2)}) collective-permute-start(f32[2,96,128]{2,1,0:T(8,128)S(1)} %get-tuple-element.76), channel_id=1, source_target_pairs={{0,1},{1,0},{2,3},{3,2},{4,5},{5,4},{6,7},{7,6},{8,9},{9,8},{10,11... | collective-permute-start | bytes 294920 | tf_op jit(solution)/shard_map/ppermute | solution.py:560
  18.4 7.2 %collective-permute-start.6 = (bf16[192,128]{1,0:T(8,128)(2,1)S(1)}, bf16[192,128]{1,0:T(8,128)(2,1)S(1)}, u32[]{:S(2)}, u32[]{:S(2)}) collective-permute-start(bf16[192,128]{1,0:T(8,128)(2,1)S(1)} %pad_maximum_fusion.1), channel_id=1, source_target_pairs={{0,15},{1,2},{2,1},{3,4},{4,3},{5,6},{6,5},{7,8},{8,7},{9,10},{10,... | collective-permute-start | bytes 147464 | tf_op jit(solution)/shard_map/ppermute | solution.py:569
  20.9 4.7 %collective-permute-start.7 = (bf16[1,96,128]{2,1,0:T(8,128)(2,1)S(1)}, bf16[1,96,128]{2,1,0:T(8,128)(2,1)S(1)}, u32[]{:S(2)}, u32[]{:S(2)}) collective-permute-start(bf16[1,96,128]{2,1,0:T(8,128)(2,1)S(1)} %get-tuple-element.105), channel_id=1, source_target_pairs={{0,16},{1,17},{2,18},{3,19},{4,20},{5,21},{6,22},{7,23},{8,24},{9,... | collective-permute-start | bytes 73736 | tf_op jit(solution)/shard_map/ppermute | solution.py:560
  22.5 3.8 %collective-permute-start.8 = (bf16[1,96,128]{2,1,0:T(8,128)(2,1)S(1)}, bf16[1,96,128]{2,1,0:T(8,128)(2,1)S(1)}, u32[]{:S(2)}, u32[]{:S(2)}) collective-permute-start(bf16[1,96,128]{2,1,0:T(8,128)(2,1)S(1)} %get-tuple-element.85), channel_id=1, source_target_pairs={{0,2},{1,3},{2,0},{3,1},{4,6},{5,7},{6,4},{7,5},{8,10},{9,11},{10,... | collective-permute-start | bytes 73736 | tf_op jit(solution)/shard_map/ppermute | solution.py:560
  22.5 4.7 %collective-permute-start.9 = (bf16[1,96,128]{2,1,0:T(8,128)(2,1)S(1)}, bf16[1,96,128]{2,1,0:T(8,128)(2,1)S(1)}, u32[]{:S(2)}, u32[]{:S(2)}) collective-permute-start(bf16[1,96,128]{2,1,0:T(8,128)(2,1)S(1)} %get-tuple-element.105), channel_id=1, source_target_pairs={{0,18},{1,19},{2,16},{3,17},{4,22},{5,23},{6,20},{7,21},{8,26},{9,... | collective-permute-start | bytes 73736 | tf_op jit(solution)/shard_map/ppermute | solution.py:560
  24.5 1.2 %collective-permute-start.5 = (bf16[48,128]{1,0:T(8,128)(2,1)S(1)}, bf16[48,128]{1,0:T(8,128)(2,1)S(1)}, u32[]{:S(2)}, u32[]{:S(2)}) collective-permute-start(bf16[48,128]{1,0:T(8,128)(2,1)S(1)} %get-tuple-element.83), channel_id=1, source_target_pairs={{0,1},{1,0},{2,3},{3,2},{4,5},{5,4},{6,7},{7,6},{8,9},{9,8},{10,11... | collective-permute-start | bytes 36872 | tf_op jit(solution)/shard_map/ppermute | solution.py:568
  27.3 6.7 %collective-permute-start.10 = (bf16[144,128]{1,0:T(8,128)(2,1)S(1)}, bf16[144,128]{1,0:T(8,128)(2,1)S(1)}, u32[]{:S(2)}, u32[]{:S(2)}) collective-permute-start(bf16[144,128]{1,0:T(8,128)(2,1)S(1)} %get-tuple-element.107), channel_id=1, source_target_pairs={{0,4},{1,5},{2,6},{3,7},{4,0},{5,1},{6,2},{7,3},{8,12},{9,13},{10,... | collective-permute-start | bytes 110600 | tf_op jit(solution)/shard_map/ppermute | solution.py:560
  27.4 6.6 %collective-permute-start.11 = (bf16[144,128]{1,0:T(8,128)(2,1)S(1)}, bf16[144,128]{1,0:T(8,128)(2,1)S(1)}, u32[]{:S(2)}, u32[]{:S(2)}) collective-permute-start(bf16[144,128]{1,0:T(8,128)(2,1)S(1)} %get-tuple-element.106), channel_id=1, source_target_pairs={{0,12},{1,13},{2,14},{3,15},{4,8},{5,9},{6,10},{7,11},{8,4},{9,5},... | collective-permute-start | bytes 110600 | tf_op jit(solution)/shard_map/ppermute | solution.py:560
  29.2 4.8 %collective-permute-start.12 = (bf16[96,128]{1,0:T(8,128)(2,1)S(1)}, bf16[96,128]{1,0:T(8,128)(2,1)S(1)}, u32[]{:S(2)}, u32[]{:S(2)}) collective-permute-start(bf16[96,128]{1,0:T(8,128)(2,1)S(1)} %bitcast.23), channel_id=1, source_target_pairs={{0,8},{1,9},{2,10},{3,11},{4,12},{5,13},{6,14},{7,15},{8,0},{9,1},... | collective-permute-start | bytes 73736 | tf_op jit(solution)/shard_map/ppermute | solution.py:560
  34.0 1.8 %collective-permute-start.13 = (f32[96,128]{1,0:T(8,128)S(1)}, f32[96,128]{1,0:T(8,128)S(1)}, u32[]{:S(2)}, u32[]{:S(2)}) collective-permute-start(f32[96,128]{1,0:T(8,128)S(1)} %add_add_fusion.own), channel_id=1, source_target_pairs={{0,1},{1,0},{2,3},{3,2},{4,5},{5,4},{6,7},{7,6},{8,9},{9,8},{10,11... | collective-permute-start | bytes 147464 | tf_op jit(solution)/shard_map/ppermute | solution.py:560

commit v3 on v2

--- a/solution.py
+++ b/solution.py
@@ -63,12 +63,12 @@
         total = total + pltpu.roll(tiles[t], 2 * t, 1)
     low = iota((C, LANES), 1) < 64
     rows = jnp.where(low, first, last)
-    return jnp.concatenate([rows, total], axis=1).astype(BF)
+    return jnp.concatenate([rows, total], axis=1)
 
 
 def edge_only(values):
     at_left, at_right = lane_masks()
-    return jnp.where(at_left | at_right, values, 0.0)
+    return jnp.where(at_left | at_right, values, jnp.zeros_like(values))
 
 
 def roles(spaces):
@@ -85,29 +85,37 @@
     )
 
 
-def send_matrices(tables, spaces):
+def send_choice(tables, spaces):
     me, even, inner = roles(spaces)
     hop = spaces // 4
-    row = iota((256, LANES), 0)
-    lane = iota((256, LANES), 1)
-    line, place = line_lanes(row)
-    out = []
+    line, place = line_lanes(iota((256, 1), 0))
+    lane = iota((1, LANES), 1)
+    low = lane < 64
+    spot = lane & 63
+    chosen = []
     for edge in swap_edges(even, inner):
         offset = jnp.where(edge == 0, -1, jnp.where(edge == 1, hop, jnp.where(edge == 2, 1, -hop)))
         target = lax.rem(me - offset + spaces, spaces)
         k = tables[1, edge, target]
         r = tables[2, edge, target]
         turned = (r == 1) | (r == 2)
-        want = jnp.where(turned, 63 - place, place)
-        top = (line == k) & (lane == want)
-        own = (line == lax.rem(edge + 2, 4)) & (lane - 64 == place)
-        out.append(jnp.concatenate([jnp.where(top, 1.0, 0.0), jnp.where(own, 1.0, 0.0)], axis=0).astype(BF))
-    return out
+        wanted = jnp.where(low, k, lax.rem(edge + 2, 4)) * 64 + jnp.where(low & turned, 63 - spot, spot)
+        chosen.append(jnp.where(line * 64 + place == wanted, 1.0, 0.0).astype(BF))
+    return jnp.concatenate(chosen, axis=1)
+
+
+def send_blocks(choice, field, border):
+    moved = dot(jnp.concatenate([field, border], axis=0), choice)
+    blocks = []
+    for swap in range(4):
+        at = slice(swap * LANES, (swap + 1) * LANES)
+        blocks.append(jnp.where(iota((C, LANES), 1) < 64, moved[0:C, at], moved[C : 2 * C, at]).astype(BF))
+    return blocks
 
 
 def by_edge(spaces, swaps):
     _, even, inner = roles(spaces)
-    m1, m2, n1, n2 = [ref[0:C].astype(F32) for ref in swaps]
+    m1, m2, n1, n2 = [ref[0:C] for ref in swaps]
     order = (
         jnp.where(even, m2, m1),
         jnp.where(inner, n1, n2),
@@ -117,7 +125,7 @@
     low = iota((C, LANES), 1) < 64
     turned = [pltpu.roll(block, 64, 1) for block in order]
     lines = [jnp.where(low, order[e], turned[e + 1]) for e in (0, 2)]
-    return jnp.concatenate(lines, axis=1).astype(BF), [block.astype(BF)[:, 0:64] for block in turned]
+    return jnp.concatenate(lines, axis=1), [block[:, 0:64] for block in turned]
 
 
 CHUNKS = 4
@@ -140,20 +148,19 @@
             copy.start()
         copies.append(pair)
     fetch.wait()
-    matrices = send_matrices(tables, spaces)
+    choice = send_choice(tables, spaces)
     parts = [[], []]
     for part in range(CHUNKS):
         for field, ref in enumerate((x_ref, g_ref)):
             copies[part][field].wait()
             for t in range(part * TILES // CHUNKS, (part + 1) * TILES // CHUNKS):
-                parts[field].append(edge_only(tile(ref, t).astype(F32)))
+                parts[field].append(edge_only(tile(ref, t)))
     both = [
-        lines_from(parts[field], tile(ref, 0).astype(F32), tile(ref, TILES - 1).astype(F32))
+        lines_from(parts[field], tile(ref, 0), tile(ref, TILES - 1))
         for field, ref in enumerate((x_ref, g_ref))
     ]
-    both = jnp.concatenate(both, axis=1)
-    for out, matrix in zip((m1, m2, n1, n2), matrices):
-        out[...] = dot(both, matrix).astype(BF)
+    for out, block in zip((m1, m2, n1, n2), send_blocks(choice, *both)):
+        out[...] = block
 
 
 def weights_of(rules, where, corner):
@@ -213,16 +220,15 @@
     columns = dot(lines, halo[...]).astype(BF)
     low = iota((C, LANES), 1) < 64
     at_left, at_right = lane_masks()
-    upper = lines[:, 0:LANES].astype(F32)
-    lower = lines[:, LANES:].astype(F32)
-    rows = jnp.where(low, upper, pltpu.roll(lower, 64, 1))
+    rows = jnp.where(low, lines[:, 0:LANES], pltpu.roll(lines[:, LANES:], 64, 1))
+    none = jnp.zeros_like(rows)
     moved = (
-        jnp.where(at_left, 0.0, pltpu.roll(rows, 1, 1)),
+        jnp.where(at_left, none, pltpu.roll(rows, 1, 1)),
         rows,
-        jnp.where(at_right, 0.0, pltpu.roll(rows, LANES - 1, 1)),
+        jnp.where(at_right, none, pltpu.roll(rows, LANES - 1, 1)),
     )
     parts = [
-        jnp.concatenate([moved[s].astype(BF), columns[:, s * LANES : (s + 1) * LANES]], axis=1) for s in range(3)
+        jnp.concatenate([moved[s], columns[:, s * LANES : (s + 1) * LANES]], axis=1) for s in range(3)
     ]
     return jnp.concatenate(parts, axis=0)
 
@@ -396,8 +402,6 @@
         d_pre = (grad * slope).astype(BF)
         act_ref[:, at] = act
         d_ref[:, at] = d_pre
-        act = act.astype(F32)
-        d_pre = d_pre.astype(F32)
         act_edges.append(edge_only(act))
         d_edges.append(edge_only(d_pre))
         if t in (0, TILES - 1):
@@ -406,10 +410,9 @@
     d_l = lines_from(d_edges, ends[0][1], ends[TILES - 1][1])
     act_lines[...] = act_l
     d_lines[...] = d_l
-    both = jnp.concatenate([act_l, d_l], axis=1)
     fetch.wait()
-    for out, matrix in zip((p0, p1, p2, p3), send_matrices(tables, spaces)):
-        out[...] = dot(both, matrix).astype(BF)
+    for out, block in zip((p0, p1, p2, p3), send_blocks(send_choice(tables, spaces), act_l, d_l)):
+        out[...] = block
 
 
 WIDE = 512
@@ -431,9 +434,9 @@
     twos = jnp.zeros((C, LANES), F32)
     for start in range(0, TILES, width):
         at = slice(start * LANES, (start + width) * LANES)
-        g_tiles = [tile(g_ref, t).astype(F32) for t in range(start, start + width)]
-        after = [jnp.where(at_right, 0.0, pltpu.roll(g, LANES - 1, 1)).astype(BF) for g in g_tiles]
-        before = [jnp.where(at_left, 0.0, pltpu.roll(g, 1, 1)).astype(BF) for g in g_tiles]
+        g_tiles = [tile(g_ref, t) for t in range(start, start + width)]
+        after = [jnp.where(at_right, zero, pltpu.roll(g, LANES - 1, 1)) for g in g_tiles]
+        before = [jnp.where(at_left, zero, pltpu.roll(g, 1, 1)) for g in g_tiles]
         g_now = [jnp.concatenate(after, axis=1), g_ref[:, at], jnp.concatenate(before, axis=1)]
         g_now = jnp.concatenate(g_now, axis=0)
         x_now = jnp.concatenate([x_side[0:C, at], x_ref[:, at], x_side[C : 2 * C, at]], axis=0)
@@ -441,12 +444,12 @@
         one = one + dot_nt(stack_of(half_d, d_ref, start, width), x_now)
         for t in range(start, start + width):
             ones = ones + tile(d_ref, t).astype(F32)
-            twos = twos + g_tiles[t - start]
+            twos = twos + g_tiles[t - start].astype(F32)
     held_one[...] = one
     held_two[...] = two
     line, _ = line_lanes(iota((C, 256), 1))
-    d_l = d_lines[...].astype(F32)
-    d_by_edge = jnp.concatenate([jnp.where(line == e, d_l, 0.0) for e in range(4)], axis=0).astype(BF)
+    d_l = d_lines[...]
+    d_by_edge = jnp.concatenate([jnp.where(line == e, d_l, jnp.zeros_like(d_l)) for e in range(4)], axis=0)
     near_one[...] = dot_nt(d_by_edge, beside[...])
     near_two[...] = dot_nt(users[...], act_lines[...])
 
@@ -511,14 +514,30 @@
     conv_tiles(wf, half, act_ref, None, visit)
 
 
-def finish_kernel(spaces, partial, d_in, m1, m2, n1, n2, halo, route, sides_ref, back, out, grad_in):
+def finish_kernel(
+    spaces, partial, d_in, m1, m2, n1, n2, halo, route, sides_ref, back,
+    out_hbm, grad_in_hbm, out, grad_in, out_sem, grad_in_sem,
+):
     lines, borders = by_edge(spaces, (m1, m2, n1, n2))
     rows, sides = edge_terms(sides_ref[2 * C :], sides_ref[0 : 2 * C], beside_lines(lines, halo))
+    wide = PIX // CHUNKS
+    copies = []
+
+    def finish(src, dst, sem, before, row_terms, side_terms):
+        for t in range(TILES):
+            at = slice(t * LANES, (t + 1) * LANES)
+            src[:, at] = add_edges(t, before[:, at], row_terms, side_terms).astype(BF)
+            if (t + 1) % (TILES // CHUNKS) == 0:
+                part = t // (TILES // CHUNKS)
+                done = slice(part * wide, (part + 1) * wide)
+                copies.append(pltpu.make_async_copy(src.at[:, done], dst.at[:, done], sem.at[part]))
+                copies[-1].start()
+
+    finish(out, out_hbm, out_sem, partial, rows, sides)
     line_grads = dot(back[...], users_values(route, borders))
-    for t in range(TILES):
-        at = slice(t * LANES, (t + 1) * LANES)
-        out[:, at] = add_edges(t, partial[:, at], rows, sides).astype(BF)
-        grad_in[:, at] = add_edges(t, d_in[:, at], line_grads[:, 0:LANES], line_grads[:, LANES : 2 * LANES]).astype(BF)
+    finish(grad_in, grad_in_hbm, grad_in_sem, d_in, line_grads[:, 0:LANES], line_grads[:, LANES:])
+    for copy in copies:
+        copy.wait()
 
 
 def unpack_kernel(share, own, got, grad_one, bias_one, grad_two, bias_two):
@@ -537,14 +556,14 @@
         bias[...] = jnp.sum(jnp.where(eye, tail, 0.0), axis=0, keepdims=True)[:, 0:share]
 
 
-def call(kernel, outs, specs, args, scratch=(), read=0, room=16 * 2**20):
+def call(kernel, outs, specs, args, scratch=(), read=0, out_specs=None):
     return pl.pallas_call(
         kernel,
         out_shape=[jax.ShapeDtypeStruct(shape, dtype) for shape, dtype in outs],
         in_specs=specs,
-        out_specs=[VMEM] * len(outs),
+        out_specs=out_specs or [VMEM] * len(outs),
         scratch_shapes=list(scratch),
-        compiler_params=pltpu.CompilerParams(vmem_limit_bytes=room),
+        compiler_params=pltpu.CompilerParams(vmem_limit_bytes=16 * 2**20),
         cost_estimate=pl.CostEstimate(flops=0, bytes_accessed=read, transcendentals=0),
     )(*args)
 
@@ -592,13 +611,14 @@
     return (a.astype(F32) + b.astype(F32)) + (c.astype(F32) + d.astype(F32))
 
 
-def last_round(held, blocks, spaces, devices):
+def last_round(held, blocks, spaces, devices, others):
     hop = spaces // 4
     held = held.astype(BF)
     joined = [jnp.concatenate([block, held], axis=0) for block in blocks]
     near, far = swap_across(joined, spaces, devices)
     opposite = swapped(held, 2 * hop, devices)
-    return near, far, total_of(held, near[C:], opposite, far[C:])
+    held, *others = lax.optimization_barrier((held, *others))
+    return near, far, total_of(held, near[C:], opposite, far[C:]), others
 
 
 def reduced(held, bits, devices, spaces, beside):
@@ -643,7 +663,7 @@
         read=COST * 2,
     )
     devices = parts * spaces
-    arrived = swap_along(sent[:2], spaces, 4) + swap_across(sent[2:], spaces, devices)
+    arrived = swap_along(sent[:2], spaces, 2) + swap_across(sent[2:], spaces, devices)
     edges = ((4 * C, 3 * C), BF)
     back = ((C, 12 * C), BF)
     d_act, pre_in, x_side, route, halo, w_edge, back2, w_one, w_two, b_one, b_two = call(
@@ -678,16 +698,18 @@
         partial_kernel, [wide, edges, back], [VMEM] * 5, (x, act, w_one, w_two, b_two), [half], read=COST * 3 // 2
     )
     held = mine + swapped(other, 1, devices)
-    held, d_in, *blocks = lax.optimization_barrier((held, d_in, *middle[2:6]))
-    again = swap_along(blocks[:2], spaces, 4)
+    blocks = middle[2:6]
+    again = swap_along(blocks[:2], spaces, 2)
     for bits in first_rounds(parts, spaces):
         held, again = reduced(held, bits, devices, spaces, again)
-    held, partial = lax.optimization_barrier((held, partial))
-    near, far, own = last_round(held[0], blocks[2:], spaces, devices)
+    near, far, own, (partial, d_in) = last_round(held[0], blocks[2:], spaces, devices, (partial, d_in))
     got = swapped(own, 1, devices)
     output, grad_in = call(
         functools.partial(finish_kernel, spaces), [image, image], [VMEM] * 10,
-        (partial, d_in, *again, near, far, halo, route, edges_two, back_one), read=COST * 3 // 2,
+        (partial, d_in, *again, near, far, halo, route, edges_two, back_one),
+        [pltpu.VMEM((C, PIX), BF), pltpu.VMEM((C, PIX), BF), pltpu.SemaphoreType.DMA((CHUNKS,)),
+         pltpu.SemaphoreType.DMA((CHUNKS,))],
+        read=COST * 3 // 2, out_specs=[HBM, HBM],
     )
     taps = ((9, share, C), F32)
     bias = ((1, share), F32)

time: 36.8 us -> 35.6 us (0.967)
  waiting for transfers between devices: 6.25 us -> 4.9 us
    ppermute x10, waiting for transfers between devices: 5.91 us -> 3.72 us  [swapped(): lax.ppermute(block, ('dp', 'space'), [(i, i ^ mask) for i in range(device...]
    ppermute x2, waiting for transfers between devices: 0.34 us -> 1.18 us  [swap_along(): lax.ppermute(blocks[0], 'space', [(i, i ^ 1) for i in range(spaces)])]
  transfers between devices with their start and end apart: 14 -> 14, of which waited for: 6 -> 5; matrix products, arithmetic and copies ran while one was open for 0% -> 0% of each run, Pallas kernels for 16% -> 16%
where the time goes in v3:
time: 35.6 us; the launch traced here: 35.3 us
  starting transfers between devices  17.2 us (48%)
  Pallas kernels  11.7 us (33%)
  waiting for transfers between devices  4.9 us (14%)
  between operations  0.82 us (2%)
  local copies, waits for them, and re-layouts  0.68 us (2%)
    pallas_call x8, Pallas kernels, call(): pl.pallas_call(kernel, out_shape=[jax.ShapeDtypeStruct(shape, dtype) for...  11.7 us
    ppermute x10, starting transfers between devices, swapped(): lax.ppermute(block, ('dp', 'space'), [(i, i ^ mask) for i in range(device...  8.93 us
    ppermute x2, starting transfers between devices, swap_along(): lax.ppermute(jnp.concatenate([blocks[1]] * more, axis=0) if more > 1 else...  8.24 us
    ppermute x10, waiting for transfers between devices, swapped(): lax.ppermute(block, ('dp', 'space'), [(i, i ^ mask) for i in range(device...  3.72 us
    ppermute x2, waiting for transfers between devices, swap_along(): lax.ppermute(blocks[0], 'space', [(i, i ^ 1) for i in range(spaces)])  1.18 us
  transfers between devices with their start and end apart: 14, of which 5 were waited for; matrix products, arithmetic and copies ran while one was open for 0% of the time, Pallas kernels for 16%

profile of v3, /device:TPU:0, one launch (start us, length us, event | category | flops | bytes accessed | tf_op | source)
XLA Modules:
  0.0 35.3 jit_solution(11263383899022180042)
XLA Ops:
  0.6 0.0 copy-start.2
  0.6 0.0 copy-start.3
  0.7 1.7 %shard_map.127 = (bf16[48,128]{1,0:T(8,128)(2,1)S(1)}, bf16[48,128]{1,0:T(8,128)(2,1)S(1)}, bf16[48,128]{1,0:T(8,128)(2,1)S(1)}, bf16[48,128]{1,0:T(8,128)(2,1)S...) custom-call(s32[3,4,16]{2,1,0:T(4,128)} %bitcast.20, bf16[48,4096]{1,0:T(8,128)(2,1)} %bitcast.15, ...), custom_call_target="tpu_custom_call" | custom-call | bytes 7380000 | tf_op jit(solution)/shard_map/pallas_call | solution.py:560
  2.4 5.5 %collective-permute-start.1 = (bf16[96,128]{1,0:T(8,128)(2,1)S(1)}, bf16[96,128]{1,0:T(8,128)(2,1)S(1)}, u32[]{:S(2)}, u32[]{:S(2)}) collective-permute-start(bf16[96,128]{1,0:T(8,128)(2,1)S(1)} %pad_maximum_fusion.2), channel_id=1, source_target_pairs={{0,15},{1,2},{2,1},{3,4},{4,3},{5,6},{6,5},{7,8},{8,7},{9,10},{10,... | collective-permute-start | bytes 73736 | tf_op jit(solution)/shard_map/ppermute | solution.py:588
  7.9 0.0 collective-permute-start
  7.9 0.0 collective-permute-start.2
  7.9 1.7 %collective-permute-start.3 = (bf16[48,128]{1,0:T(8,128)(2,1)S(1)}, bf16[48,128]{1,0:T(8,128)(2,1)S(1)}, u32[]{:S(2)}, u32[]{:S(2)}) collective-permute-start(bf16[48,128]{1,0:T(8,128)(2,1)S(1)} %get-tuple-element.53), channel_id=1, source_target_pairs={{0,12},{1,13},{2,14},{3,15},{4,8},{5,9},{6,10},{7,11},{8,4},{9,5},... | collective-permute-start | bytes 36872 | tf_op jit(solution)/shard_map/ppermute | solution.py:579
  9.6 0.0 copy-start.4
  9.6 0.0 copy-start.5
  9.6 0.0 copy-done.2
  9.6 0.0 copy-done.3
  9.6 0.6 %copy-done.4 = f32[48]{0:T(128)S(1)} copy-done((f32[48]{0:T(128)S(1)}, f32[48]{0:T(128)}, u32[]{:S(2)}) %copy-start.4) | copy-done | bytes 216
  10.2 0.0 copy-done.5
  10.3 2.3 %shard_map.128 = (f32[48,4096]{1,0:T(8,128)S(1)}, f32[48,4096]{1,0:T(8,128)S(1)}, bf16[96,4096]{1,0:T(8,128)(2,1)S(1)}, bf16[4,64,768]{2,1,0:T(8,128)(2,1)S(1)},...) custom-call(s32[3,4,16]{2,1,0:T(4,128)} %bitcast.21, ...), custom_call_target="tpu_custom_call" | custom-call | bytes 11070000 | tf_op jit(solution)/shard_map/pallas_call | solution.py:560
  12.5 0.0 collective-permute-done.m1
  12.5 0.0 collective-permute-done.2.n1
  12.5 0.8 %collective-permute-done.3.n2 = bf16[48,128]{1,0:T(8,128)(2,1)S(1)} collective-permute-done((bf16[48,128]{1,0:T(8,128)(2,1)S(1)}, bf16[48,128]{1,0:T(8,128)(2,1)S(1)}, u32[]{:S(2)}, u32[]{:S(2)}) %collective-permute-start.3) | collective-permute-done | bytes 12320 | tf_op jit(solution)/shard_map/ppermute | solution.py:579
  13.4 0.0 collective-permute-done.1.m2
  13.4 0.0 copy-start
  13.4 0.0 copy-start.1
  13.4 2.2 %shard_map.129 = (bf16[48,4096]{1,0:T(8,128)(2,1)S(1)}, bf16[48,4096]{1,0:T(8,128)(2,1)S(1)}, bf16[48,128]{1,0:T(8,128)(2,1)S(1)}, bf16[48,128]{1,0:T(8,128)(2,1...) custom-call(s32[3,4,16]{2,1,0:T(4,128)} %bitcast.22, ...), custom_call_target="tpu_custom_call" | custom-call | bytes 8302500 | tf_op jit(solution)/shard_map/pallas_call | solution.py:560
  15.6 0.0 copy-done
  15.6 0.0 copy-done.1
  15.6 1.2 %shard_map.130 = (f32[2,96,128]{2,1,0:T(8,128)S(1)}, f32[2,96,128]{2,1,0:T(8,128)S(1)}) custom-call(bf16[48,4096]{1,0:T(8,128)(2,1)S(1)} %bitcast.16, bf16[48,4096]{1,0:T(8,128)(2,1)S(1)} %bitcast.13, bf16[48,4096]{1,0:T(8,128)(2,1)S(1)} %get-tuple-element.63.act_ref, bf16[48,4096]{1,0:T(8,128)(2,1)S(1)} %get-tuple-element.64.d_ref, ...), custom_call_target="tpu_custom_call" | custom-call | bytes 4612500 | tf_op jit(solution)/shard_map/pallas_call | solution.py:560
  16.9 0.1 collective-permute-start.4
  17.0 2.8 %collective-permute-start.6 = (bf16[96,128]{1,0:T(8,128)(2,1)S(1)}, bf16[96,128]{1,0:T(8,128)(2,1)S(1)}, u32[]{:S(2)}, u32[]{:S(2)}) collective-permute-start(bf16[96,128]{1,0:T(8,128)(2,1)S(1)} %pad_maximum_fusion.3), channel_id=1, source_target_pairs={{0,15},{1,2},{2,1},{3,4},{4,3},{5,6},{6,5},{7,8},{8,7},{9,10},{10,... | collective-permute-start | bytes 73736 | tf_op jit(solution)/shard_map/ppermute | solution.py:588
  19.7 0.0 collective-permute-done.4
  19.8 1.6 %collective-permute-start.7 = (bf16[1,96,128]{2,1,0:T(8,128)(2,1)S(1)}, bf16[1,96,128]{2,1,0:T(8,128)(2,1)S(1)}, u32[]{:S(2)}, u32[]{:S(2)}) collective-permute-start(bf16[1,96,128]{2,1,0:T(8,128)(2,1)S(1)} %get-tuple-element.95), channel_id=1, source_target_pairs={{0,16},{1,17},{2,18},{3,19},{4,20},{5,21},{6,22},{7,23},{8,24},{9,... | collective-permute-start | bytes 73736 | tf_op jit(solution)/shard_map/ppermute | solution.py:579
  21.3 0.0 collective-permute-start.8
  21.3 2.0 %collective-permute-start.9 = (bf16[1,96,128]{2,1,0:T(8,128)(2,1)S(1)}, bf16[1,96,128]{2,1,0:T(8,128)(2,1)S(1)}, u32[]{:S(2)}, u32[]{:S(2)}) collective-permute-start(bf16[1,96,128]{2,1,0:T(8,128)(2,1)S(1)} %get-tuple-element.95), channel_id=1, source_target_pairs={{0,18},{1,19},{2,16},{3,17},{4,22},{5,23},{6,20},{7,21},{8,26},{9,... | collective-permute-start | bytes 73736 | tf_op jit(solution)/shard_map/ppermute | solution.py:579
  23.3 0.0 collective-permute-start.5
  23.3 1.2 %collective-permute-done.5.m1 = bf16[48,128]{1,0:T(8,128)(2,1)S(1)} collective-permute-done((bf16[48,128]{1,0:T(8,128)(2,1)S(1)}, bf16[48,128]{1,0:T(8,128)(2,1)S(1)}, u32[]{:S(2)}, u32[]{:S(2)}) %collective-permute-start.5) | collective-permute-done | bytes 12320 | tf_op jit(solution)/shard_map/ppermute | solution.py:587
  24.5 0.0 collective-permute-done.6.m2
  24.5 0.0 collective-permute-done.7
  24.5 0.7 %collective-permute-done.8 = bf16[1,96,128]{2,1,0:T(8,128)(2,1)S(1)} collective-permute-done((bf16[1,96,128]{2,1,0:T(8,128)(2,1)S(1)}, bf16[1,96,128]{2,1,0:T(8,128)(2,1)S(1)}, u32[]{:S(2)}, u32[]{:S(2)}) %collective-permute-start.8) | collective-permute-done | bytes 24608 | tf_op jit(solution)/shard_map/ppermute | solution.py:579
  25.2 0.9 %collective-permute-done.9 = bf16[1,96,128]{2,1,0:T(8,128)(2,1)S(1)} collective-permute-done((bf16[1,96,128]{2,1,0:T(8,128)(2,1)S(1)}, bf16[1,96,128]{2,1,0:T(8,128)(2,1)S(1)}, u32[]{:S(2)}, u32[]{:S(2)}) %collective-permute-start.9) | collective-permute-done | bytes 24608 | tf_op jit(solution)/shard_map/ppermute | solution.py:579
  26.1 0.1 collective-permute-start.10
  26.2 1.8 %collective-permute-start.11 = (bf16[144,128]{1,0:T(8,128)(2,1)S(1)}, bf16[144,128]{1,0:T(8,128)(2,1)S(1)}, u32[]{:S(2)}, u32[]{:S(2)}) collective-permute-start(bf16[144,128]{1,0:T(8,128)(2,1)S(1)} %get-tuple-element.96), channel_id=1, source_target_pairs={{0,12},{1,13},{2,14},{3,15},{4,8},{5,9},{6,10},{7,11},{8,4},{9,5},... | collective-permute-start | bytes 110600 | tf_op jit(solution)/shard_map/ppermute | solution.py:579
  28.0 1.7 %collective-permute-start.12 = (bf16[96,128]{1,0:T(8,128)(2,1)S(1)}, bf16[96,128]{1,0:T(8,128)(2,1)S(1)}, u32[]{:S(2)}, u32[]{:S(2)}) collective-permute-start(bf16[96,128]{1,0:T(8,128)(2,1)S(1)} %fusion), channel_id=1, source_target_pairs={{0,8},{1,9},{2,10},{3,11},{4,12},{5,13},{6,14},{7,15},{8,0},{9,1},... | collective-permute-start | bytes 73736 | tf_op jit(solution)/shard_map/ppermute | solution.py:579
  29.7 0.9 %shard_map.132.d_in = f32[48,4096]{1,0:T(8,128)S(1)} custom-call(bf16[48,4096]{1,0:T(8,128)(2,1)S(1)} %bitcast.14, bf16[48,4096]{1,0:T(8,128)(2,1)S(1)} %get-tuple-element.64.d_ref, bf16[9,48,48]{2,1,0:T(8,128)(2,1)S(1)} %get-tuple-element.75.w1_ref.w_ref), custom_call_target="tpu_custom_call" | custom-call | bytes 3690000 | tf_op jit(solution)/shard_map/pallas_call | solution.py:560
  30.6 0.9 %shard_map.131 = (f32[48,4096]{1,0:T(8,128)S(1)}, bf16[192,144]{1,0:T(8,128)(2,1)S(1)}, bf16[48,576]{1,0:T(8,128)(2,1)S(1)}) custom-call(bf16[48,4096]{1,0:T(8,128)(2,1)S(1)} %bitcast.17, bf16[48,4096]{1,0:T(8,128)(2,1)S(1)} %get-tuple-element.63.act_ref, bf16[9,48,48]{2,1,0:T(8,128)(2,1)S(1)} %get-tuple-element.75.w1_ref.w_ref, ...), custom_call_target="tpu_custom_call" | custom-call | bytes 5535000 | tf_op jit(solution)/shard_map/pallas_call | solution.py:560
  31.4 1.3 %collective-permute-done.12 = bf16[96,128]{1,0:T(8,128)(2,1)S(1)} collective-permute-done((bf16[96,128]{1,0:T(8,128)(2,1)S(1)}, bf16[96,128]{1,0:T(8,128)(2,1)S(1)}, u32[]{:S(2)}, u32[]{:S(2)}) %collective-permute-start.12) | collective-permute-done | bytes 24608 | tf_op jit(solution)/shard_map/ppermute | solution.py:579
  32.7 0.0 collective-permute-done.10.n1
  32.7 0.0 collective-permute-done.11.n2
  32.7 0.1 collective-permute-start.13
  32.8 1.7 %shard_map.133 = (bf16[48,4096]{1,0:T(8,128)(2,1)}, bf16[48,4096]{1,0:T(8,128)(2,1)}) custom-call(f32[48,4096]{1,0:T(8,128)S(1)} %get-tuple-element.79.partial, f32[48,4096]{1,0:T(8,128)S(1)} %shard_map.132.d_in, bf16[48,128]{1,0:T(8,128)(2,1)S(1)} %collective-permute-done.5.m1, bf16[96,128]{1,0:T(8,128)(2,1)S(1)} %collective-permute-done.6.m2, ...), custom_call_target="tpu_custom_call" | custom-call | bytes 5535000 | tf_op jit(solution)/shard_map/pallas_call | solution.py:560
  34.5 0.0 collective-permute-done.13.got
  34.5 0.8 %shard_map.134 = (f32[9,24,48]{2,1,0:T(8,128)}, f32[1,24]{1,0:T(1,128)}, f32[9,24,48]{2,1,0:T(8,128)}, f32[1,24]{1,0:T(1,128)}) custom-call(f32[96,128]{1,0:T(8,128)S(1)} %add_add_fusion.own, f32[96,128]{1,0:T(8,128)S(1)} %collective-permute-done.13.got), custom_call_target="tpu_custom_call" | custom-call | bytes 100000 | tf_op jit(solution)/shard_map/pallas_call | solution.py:560
  (7 shorter events, 0.1 us)
Async XLA Ops:
  0.6 9.0 %copy-start.2 = (bf16[9,48,48]{2,1,0:T(8,128)(2,1)S(1)}, bf16[9,48,48]{2,1,0:T(8,128)(2,1)}, u32[]{:S(2)}) copy-start(bf16[9,48,48]{2,1,0:T(8,128)(2,1)} %w1_ref.1) | copy-start | bytes 124420
  0.6 8.9 %copy-start.3 = (bf16[9,48,48]{2,1,0:T(8,128)(2,1)S(1)}, bf16[9,48,48]{2,1,0:T(8,128)(2,1)}, u32[]{:S(2)}) copy-start(bf16[9,48,48]{2,1,0:T(8,128)(2,1)} %w2_ref.1) | copy-start | bytes 124420
  2.4 11.0 %collective-permute-start.1 = (bf16[96,128]{1,0:T(8,128)(2,1)S(1)}, bf16[96,128]{1,0:T(8,128)(2,1)S(1)}, u32[]{:S(2)}, u32[]{:S(2)}) collective-permute-start(bf16[96,128]{1,0:T(8,128)(2,1)S(1)} %pad_maximum_fusion.2), channel_id=1, source_target_pairs={{0,15},{1,2},{2,1},{3,4},{4,3},{5,6},{6,5},{7,8},{8,7},{9,10},{10,... | collective-permute-start | bytes 73736 | tf_op jit(solution)/shard_map/ppermute | solution.py:588
  7.9 4.6 %collective-permute-start = (bf16[48,128]{1,0:T(8,128)(2,1)S(1)}, bf16[48,128]{1,0:T(8,128)(2,1)S(1)}, u32[]{:S(2)}, u32[]{:S(2)}) collective-permute-start(bf16[48,128]{1,0:T(8,128)(2,1)S(1)} %get-tuple-element.50), channel_id=1, source_target_pairs={{0,1},{1,0},{2,3},{3,2},{4,5},{5,4},{6,7},{7,6},{8,9},{9,8},{10,11... | collective-permute-start | bytes 36872 | tf_op jit(solution)/shard_map/ppermute | solution.py:587
  7.9 4.6 %collective-permute-start.2 = (bf16[48,128]{1,0:T(8,128)(2,1)S(1)}, bf16[48,128]{1,0:T(8,128)(2,1)S(1)}, u32[]{:S(2)}, u32[]{:S(2)}) collective-permute-start(bf16[48,128]{1,0:T(8,128)(2,1)S(1)} %get-tuple-element.52), channel_id=1, source_target_pairs={{0,4},{1,5},{2,6},{3,7},{4,0},{5,1},{6,2},{7,3},{8,12},{9,13},{10,... | collective-permute-start | bytes 36872 | tf_op jit(solution)/shard_map/ppermute | solution.py:579
  7.9 5.5 %collective-permute-start.3 = (bf16[48,128]{1,0:T(8,128)(2,1)S(1)}, bf16[48,128]{1,0:T(8,128)(2,1)S(1)}, u32[]{:S(2)}, u32[]{:S(2)}) collective-permute-start(bf16[48,128]{1,0:T(8,128)(2,1)S(1)} %get-tuple-element.53), channel_id=1, source_target_pairs={{0,12},{1,13},{2,14},{3,15},{4,8},{5,9},{6,10},{7,11},{8,4},{9,5},... | collective-permute-start | bytes 36872 | tf_op jit(solution)/shard_map/ppermute | solution.py:579
  9.6 0.7 %copy-start.4 = (f32[48]{0:T(128)S(1)}, f32[48]{0:T(128)}, u32[]{:S(2)}) copy-start(f32[48]{0:T(128)} %param.11) | copy-start | bytes 580
  9.6 0.7 %copy-start.5 = (f32[48]{0:T(128)S(1)}, f32[48]{0:T(128)}, u32[]{:S(2)}) copy-start(f32[48]{0:T(128)} %param.13) | copy-start | bytes 580
  13.4 2.2 %copy-start = (bf16[1,1,48,4096]{3,2,1,0:T(8,128)(2,1)S(1)}, bf16[1,1,48,4096]{3,2,1,0:T(8,128)(2,1)}, u32[]{:S(2)}) copy-start(bf16[1,1,48,4096]{3,2,1,0:T(8,128)(2,1)} %param.9) | copy-start | bytes 1179652
  13.4 2.2 %copy-start.1 = (bf16[1,1,48,4096]{3,2,1,0:T(8,128)(2,1)S(1)}, bf16[1,1,48,4096]{3,2,1,0:T(8,128)(2,1)}, u32[]{:S(2)}) copy-start(bf16[1,1,48,4096]{3,2,1,0:T(8,128)(2,1)} %param.8) | copy-start | bytes 1179652
  16.9 2.9 %collective-permute-start.4 = (f32[2,96,128]{2,1,0:T(8,128)S(1)}, f32[2,96,128]{2,1,0:T(8,128)S(1)}, u32[]{:S(2)}, u32[]{:S(2)}) collective-permute-start(f32[2,96,128]{2,1,0:T(8,128)S(1)} %get-tuple-element.71), channel_id=1, source_target_pairs={{0,1},{1,0},{2,3},{3,2},{4,5},{5,4},{6,7},{7,6},{8,9},{9,8},{10,11... | collective-permute-start | bytes 294920 | tf_op jit(solution)/shard_map/ppermute | solution.py:579
  17.0 7.5 %collective-permute-start.6 = (bf16[96,128]{1,0:T(8,128)(2,1)S(1)}, bf16[96,128]{1,0:T(8,128)(2,1)S(1)}, u32[]{:S(2)}, u32[]{:S(2)}) collective-permute-start(bf16[96,128]{1,0:T(8,128)(2,1)S(1)} %pad_maximum_fusion.3), channel_id=1, source_target_pairs={{0,15},{1,2},{2,1},{3,4},{4,3},{5,6},{6,5},{7,8},{8,7},{9,10},{10,... | collective-permute-start | bytes 73736 | tf_op jit(solution)/shard_map/ppermute | solution.py:588
  19.8 4.7 %collective-permute-start.7 = (bf16[1,96,128]{2,1,0:T(8,128)(2,1)S(1)}, bf16[1,96,128]{2,1,0:T(8,128)(2,1)S(1)}, u32[]{:S(2)}, u32[]{:S(2)}) collective-permute-start(bf16[1,96,128]{2,1,0:T(8,128)(2,1)S(1)} %get-tuple-element.95), channel_id=1, source_target_pairs={{0,16},{1,17},{2,18},{3,19},{4,20},{5,21},{6,22},{7,23},{8,24},{9,... | collective-permute-start | bytes 73736 | tf_op jit(solution)/shard_map/ppermute | solution.py:579
  21.3 3.8 %collective-permute-start.8 = (bf16[1,96,128]{2,1,0:T(8,128)(2,1)S(1)}, bf16[1,96,128]{2,1,0:T(8,128)(2,1)S(1)}, u32[]{:S(2)}, u32[]{:S(2)}) collective-permute-start(bf16[1,96,128]{2,1,0:T(8,128)(2,1)S(1)} %get-tuple-element.74), channel_id=1, source_target_pairs={{0,2},{1,3},{2,0},{3,1},{4,6},{5,7},{6,4},{7,5},{8,10},{9,11},{10,... | collective-permute-start | bytes 73736 | tf_op jit(solution)/shard_map/ppermute | solution.py:579
  21.3 4.7 %collective-permute-start.9 = (bf16[1,96,128]{2,1,0:T(8,128)(2,1)S(1)}, bf16[1,96,128]{2,1,0:T(8,128)(2,1)S(1)}, u32[]{:S(2)}, u32[]{:S(2)}) collective-permute-start(bf16[1,96,128]{2,1,0:T(8,128)(2,1)S(1)} %get-tuple-element.95), channel_id=1, source_target_pairs={{0,18},{1,19},{2,16},{3,17},{4,22},{5,23},{6,20},{7,21},{8,26},{9,... | collective-permute-start | bytes 73736 | tf_op jit(solution)/shard_map/ppermute | solution.py:579
  23.3 1.2 %collective-permute-start.5 = (bf16[48,128]{1,0:T(8,128)(2,1)S(1)}, bf16[48,128]{1,0:T(8,128)(2,1)S(1)}, u32[]{:S(2)}, u32[]{:S(2)}) collective-permute-start(bf16[48,128]{1,0:T(8,128)(2,1)S(1)} %get-tuple-element.72), channel_id=1, source_target_pairs={{0,1},{1,0},{2,3},{3,2},{4,5},{5,4},{6,7},{7,6},{8,9},{9,8},{10,11... | collective-permute-start | bytes 36872 | tf_op jit(solution)/shard_map/ppermute | solution.py:587
  26.1 6.6 %collective-permute-start.10 = (bf16[144,128]{1,0:T(8,128)(2,1)S(1)}, bf16[144,128]{1,0:T(8,128)(2,1)S(1)}, u32[]{:S(2)}, u32[]{:S(2)}) collective-permute-start(bf16[144,128]{1,0:T(8,128)(2,1)S(1)} %get-tuple-element.97), channel_id=1, source_target_pairs={{0,4},{1,5},{2,6},{3,7},{4,0},{5,1},{6,2},{7,3},{8,12},{9,13},{10,... | collective-permute-start | bytes 110600 | tf_op jit(solution)/shard_map/ppermute | solution.py:579
  26.2 6.5 %collective-permute-start.11 = (bf16[144,128]{1,0:T(8,128)(2,1)S(1)}, bf16[144,128]{1,0:T(8,128)(2,1)S(1)}, u32[]{:S(2)}, u32[]{:S(2)}) collective-permute-start(bf16[144,128]{1,0:T(8,128)(2,1)S(1)} %get-tuple-element.96), channel_id=1, source_target_pairs={{0,12},{1,13},{2,14},{3,15},{4,8},{5,9},{6,10},{7,11},{8,4},{9,5},... | collective-permute-start | bytes 110600 | tf_op jit(solution)/shard_map/ppermute | solution.py:579
  28.0 4.7 %collective-permute-start.12 = (bf16[96,128]{1,0:T(8,128)(2,1)S(1)}, bf16[96,128]{1,0:T(8,128)(2,1)S(1)}, u32[]{:S(2)}, u32[]{:S(2)}) collective-permute-start(bf16[96,128]{1,0:T(8,128)(2,1)S(1)} %fusion), channel_id=1, source_target_pairs={{0,8},{1,9},{2,10},{3,11},{4,12},{5,13},{6,14},{7,15},{8,0},{9,1},... | collective-permute-start | bytes 73736 | tf_op jit(solution)/shard_map/ppermute | solution.py:579
  32.7 1.8 %collective-permute-start.13 = (f32[96,128]{1,0:T(8,128)S(1)}, f32[96,128]{1,0:T(8,128)S(1)}, u32[]{:S(2)}, u32[]{:S(2)}) collective-permute-start(f32[96,128]{1,0:T(8,128)S(1)} %add_add_fusion.own), channel_id=1, source_target_pairs={{0,1},{1,0},{2,3},{3,2},{4,5},{5,4},{6,7},{7,6},{8,9},{9,8},{10,11... | collective-permute-start | bytes 147464 | tf_op jit(solution)/shard_map/ppermute | solution.py:579

commit v4 on v3

--- a/solution.py
+++ b/solution.py
@@ -621,7 +621,7 @@
     return near, far, total_of(held, near[C:], opposite, far[C:]), others
 
 
-def reduced(held, bits, devices, spaces, beside):
+def reduced(held, bits, devices, spaces):
     where = lax.axis_index("dp")
     keep = give = held.astype(BF)
     masks = []
@@ -632,10 +632,9 @@
             low, high = keep[: keep.shape[0] // 2], keep[keep.shape[0] // 2 :]
             keep, give = jnp.where(upper, high, low), jnp.where(upper, low, high)
     first = swapped(give, masks[0], devices)
-    kept, *beside = lax.optimization_barrier((keep, *beside))
     if len(masks) == 1:
-        return kept.astype(F32) + first.astype(F32), beside
-    return total_of(kept, first, swapped(keep, masks[1], devices), swapped(give, masks[0] ^ masks[1], devices)), beside
+        return keep.astype(F32) + first.astype(F32)
+    return total_of(keep, first, swapped(keep, masks[1], devices), swapped(give, masks[0] ^ masks[1], devices))
 
 
 COST = 3_690_000
@@ -693,15 +692,16 @@
          pltpu.VMEM((4 * C, 3 * C), F32), pltpu.VMEM((12 * C, C), F32)],
         read=COST * 5 // 4,
     )
-    (d_in,) = call(inner_kernel, [wide], [VMEM] * 3, (g, d_pre, w_one), [half], read=COST)
+    blocks = middle[2:6]
+    again = swap_along(blocks[:2], spaces, 3)
+    act_late, d_late, *again = lax.optimization_barrier((act, d_pre, *again))
+    (d_in,) = call(inner_kernel, [wide], [VMEM] * 3, (g, d_late, w_one), [half], read=COST)
     partial, edges_two, back_one = call(
-        partial_kernel, [wide, edges, back], [VMEM] * 5, (x, act, w_one, w_two, b_two), [half], read=COST * 3 // 2
+        partial_kernel, [wide, edges, back], [VMEM] * 5, (x, act_late, w_one, w_two, b_two), [half], read=COST * 3 // 2
     )
     held = mine + swapped(other, 1, devices)
-    blocks = middle[2:6]
-    again = swap_along(blocks[:2], spaces, 2)
     for bits in first_rounds(parts, spaces):
-        held, again = reduced(held, bits, devices, spaces, again)
+        held = reduced(held, bits, devices, spaces)
     near, far, own, (partial, d_in) = last_round(held[0], blocks[2:], spaces, devices, (partial, d_in))
     got = swapped(own, 1, devices)
     output, grad_in = call(

time: 35.6 us -> 34.7 us (0.975)
  starting transfers between devices: 17.2 us -> 16 us
    ppermute x2, starting transfers between devices: 8.24 us -> 7.06 us  [swap_along(): lax.ppermute(jnp.concatenate([blocks[1]] * more, axis=0) if more > 1 else...]
  transfers between devices with their start and end apart: 14 -> 14, of which waited for: 5 -> 6; matrix products, arithmetic and copies ran while one was open for 0% -> 0% of each run, Pallas kernels for 16% -> 16%
where the time goes in v4:
time: 34.7 us; the launch traced here: 34.4 us
  starting transfers between devices  16 us (46%)
  Pallas kernels  11.6 us (33%)
  waiting for transfers between devices  5.25 us (15%)
  between operations  0.81 us (2%)
  local copies, waits for them, and re-layouts  0.68 us (2%)
    pallas_call x8, Pallas kernels, call(): pl.pallas_call(kernel, out_shape=[jax.ShapeDtypeStruct(shape, dtype) for...  11.6 us
    ppermute x10, starting transfers between devices, swapped(): lax.ppermute(block, ('dp', 'space'), [(i, i ^ mask) for i in range(device...  8.94 us
    ppermute x2, starting transfers between devices, swap_along(): lax.ppermute(jnp.concatenate([blocks[1]] * more, axis=0) if more > 1 else...  7.06 us
    ppermute x10, waiting for transfers between devices, swapped(): lax.ppermute(block, ('dp', 'space'), [(i, i ^ mask) for i in range(device...  4.07 us
    ppermute x2, waiting for transfers between devices, swap_along(): lax.ppermute(blocks[0], 'space', [(i, i ^ 1) for i in range(spaces)])  1.18 us
  transfers between devices with their start and end apart: 14, of which 6 were waited for; matrix products, arithmetic and copies ran while one was open for 0% of the time, Pallas kernels for 16%

profile of v4, /device:TPU:0, one launch (start us, length us, event | category | flops | bytes accessed | tf_op | source)
XLA Modules:
  0.0 34.4 jit_solution(7789850416283985548)
XLA Ops:
  0.6 0.0 copy-start.2
  0.6 0.0 copy-start.3
  0.7 1.7 %shard_map.127 = (bf16[48,128]{1,0:T(8,128)(2,1)S(1)}, bf16[48,128]{1,0:T(8,128)(2,1)S(1)}, bf16[48,128]{1,0:T(8,128)(2,1)S(1)}, bf16[48,128]{1,0:T(8,128)(2,1)S...) custom-call(s32[3,4,16]{2,1,0:T(4,128)} %bitcast.20, bf16[48,4096]{1,0:T(8,128)(2,1)} %bitcast.15, ...), custom_call_target="tpu_custom_call" | custom-call | bytes 7380000 | tf_op jit(solution)/shard_map/pallas_call | solution.py:560
  2.4 5.5 %collective-permute-start.1 = (bf16[96,128]{1,0:T(8,128)(2,1)S(1)}, bf16[96,128]{1,0:T(8,128)(2,1)S(1)}, u32[]{:S(2)}, u32[]{:S(2)}) collective-permute-start(bf16[96,128]{1,0:T(8,128)(2,1)S(1)} %pad_maximum_fusion.3), channel_id=1, source_target_pairs={{0,15},{1,2},{2,1},{3,4},{4,3},{5,6},{6,5},{7,8},{8,7},{9,10},{10,... | collective-permute-start | bytes 73736 | tf_op jit(solution)/shard_map/ppermute | solution.py:588
  7.9 0.0 collective-permute-start
  7.9 0.0 collective-permute-start.2
  7.9 1.7 %collective-permute-start.3 = (bf16[48,128]{1,0:T(8,128)(2,1)S(1)}, bf16[48,128]{1,0:T(8,128)(2,1)S(1)}, u32[]{:S(2)}, u32[]{:S(2)}) collective-permute-start(bf16[48,128]{1,0:T(8,128)(2,1)S(1)} %get-tuple-element.54), channel_id=1, source_target_pairs={{0,12},{1,13},{2,14},{3,15},{4,8},{5,9},{6,10},{7,11},{8,4},{9,5},... | collective-permute-start | bytes 36872 | tf_op jit(solution)/shard_map/ppermute | solution.py:579
  9.6 0.0 copy-start.4
  9.6 0.0 copy-start.5
  9.6 0.0 copy-done.2
  9.6 0.0 copy-done.3
  9.6 0.6 %copy-done.4 = f32[48]{0:T(128)S(1)} copy-done((f32[48]{0:T(128)S(1)}, f32[48]{0:T(128)}, u32[]{:S(2)}) %copy-start.4) | copy-done | bytes 216
  10.2 0.0 copy-done.5
  10.3 2.3 %shard_map.128 = (f32[48,4096]{1,0:T(8,128)S(1)}, f32[48,4096]{1,0:T(8,128)S(1)}, bf16[96,4096]{1,0:T(8,128)(2,1)S(1)}, bf16[4,64,768]{2,1,0:T(8,128)(2,1)S(1)},...) custom-call(s32[3,4,16]{2,1,0:T(4,128)} %bitcast.21, ...), custom_call_target="tpu_custom_call" | custom-call | bytes 11070000 | tf_op jit(solution)/shard_map/pallas_call | solution.py:560
  12.5 0.0 collective-permute-done.m1
  12.5 0.0 collective-permute-done.2.n1
  12.5 0.8 %collective-permute-done.3.n2 = bf16[48,128]{1,0:T(8,128)(2,1)S(1)} collective-permute-done((bf16[48,128]{1,0:T(8,128)(2,1)S(1)}, bf16[48,128]{1,0:T(8,128)(2,1)S(1)}, u32[]{:S(2)}, u32[]{:S(2)}) %collective-permute-start.3) | collective-permute-done | bytes 12320 | tf_op jit(solution)/shard_map/ppermute | solution.py:579
  13.4 0.0 collective-permute-done.1.m2
  13.4 0.0 copy-start
  13.4 0.0 copy-start.1
  13.4 2.2 %shard_map.129 = (bf16[48,4096]{1,0:T(8,128)(2,1)S(1)}, bf16[48,4096]{1,0:T(8,128)(2,1)S(1)}, bf16[48,128]{1,0:T(8,128)(2,1)S(1)}, bf16[48,128]{1,0:T(8,128)(2,1...) custom-call(s32[3,4,16]{2,1,0:T(4,128)} %bitcast.22, ...), custom_call_target="tpu_custom_call" | custom-call | bytes 8302500 | tf_op jit(solution)/shard_map/pallas_call | solution.py:560
  15.6 0.0 copy-done
  15.6 0.0 copy-done.1
  15.6 1.2 %shard_map.130 = (f32[2,96,128]{2,1,0:T(8,128)S(1)}, f32[2,96,128]{2,1,0:T(8,128)S(1)}) custom-call(bf16[48,4096]{1,0:T(8,128)(2,1)S(1)} %bitcast.16, bf16[48,4096]{1,0:T(8,128)(2,1)S(1)} %bitcast.13, bf16[48,4096]{1,0:T(8,128)(2,1)S(1)} %get-tuple-element.75.act_ref, bf16[48,4096]{1,0:T(8,128)(2,1)S(1)} %get-tuple-element.80.d_ref, ...), custom_call_target="tpu_custom_call" | custom-call | bytes 4612500 | tf_op jit(solution)/shard_map/pallas_call | solution.py:560
  16.8 0.1 collective-permute-start.4
  16.9 1.3 %collective-permute-done.4 = f32[2,96,128]{2,1,0:T(8,128)S(1)} collective-permute-done((f32[2,96,128]{2,1,0:T(8,128)S(1)}, f32[2,96,128]{2,1,0:T(8,128)S(1)}, u32[]{:S(2)}, u32[]{:S(2)}) %collective-permute-start.4) | collective-permute-done | bytes 98336 | tf_op jit(solution)/shard_map/ppermute | solution.py:579
  18.2 1.6 %collective-permute-start.5 = (bf16[1,96,128]{2,1,0:T(8,128)(2,1)S(1)}, bf16[1,96,128]{2,1,0:T(8,128)(2,1)S(1)}, u32[]{:S(2)}, u32[]{:S(2)}) collective-permute-start(bf16[1,96,128]{2,1,0:T(8,128)(2,1)S(1)} %get-tuple-element.97), channel_id=1, source_target_pairs={{0,16},{1,17},{2,18},{3,19},{4,20},{5,21},{6,22},{7,23},{8,24},{9,... | collective-permute-start | bytes 73736 | tf_op jit(solution)/shard_map/ppermute | solution.py:579
  19.8 0.7 %collective-permute-start.7 = (bf16[1,96,128]{2,1,0:T(8,128)(2,1)S(1)}, bf16[1,96,128]{2,1,0:T(8,128)(2,1)S(1)}, u32[]{:S(2)}, u32[]{:S(2)}) collective-permute-start(bf16[1,96,128]{2,1,0:T(8,128)(2,1)S(1)} %get-tuple-element.97), channel_id=1, source_target_pairs={{0,18},{1,19},{2,16},{3,17},{4,22},{5,23},{6,20},{7,21},{8,26},{9,... | collective-permute-start | bytes 73736 | tf_op jit(solution)/shard_map/ppermute | solution.py:579
  20.5 1.3 %collective-permute-start.6 = (bf16[1,96,128]{2,1,0:T(8,128)(2,1)S(1)}, bf16[1,96,128]{2,1,0:T(8,128)(2,1)S(1)}, u32[]{:S(2)}, u32[]{:S(2)}) collective-permute-start(bf16[1,96,128]{2,1,0:T(8,128)(2,1)S(1)} %get-tuple-element.96), channel_id=1, source_target_pairs={{0,2},{1,3},{2,0},{3,1},{4,6},{5,7},{6,4},{7,5},{8,10},{9,11},{10,... | collective-permute-start | bytes 73736 | tf_op jit(solution)/shard_map/ppermute | solution.py:579
  21.8 1.6 %collective-permute-start.9 = (bf16[144,128]{1,0:T(8,128)(2,1)S(1)}, bf16[144,128]{1,0:T(8,128)(2,1)S(1)}, u32[]{:S(2)}, u32[]{:S(2)}) collective-permute-start(bf16[144,128]{1,0:T(8,128)(2,1)S(1)} %pad_maximum_fusion.2), channel_id=1, source_target_pairs={{0,15},{1,2},{2,1},{3,4},{4,3},{5,6},{6,5},{7,8},{8,7},{9,10},{10,... | collective-permute-start | bytes 110600 | tf_op jit(solution)/shard_map/ppermute | solution.py:588
  23.4 0.0 collective-permute-done.5
  23.4 1.0 %collective-permute-done.6 = bf16[1,96,128]{2,1,0:T(8,128)(2,1)S(1)} collective-permute-done((bf16[1,96,128]{2,1,0:T(8,128)(2,1)S(1)}, bf16[1,96,128]{2,1,0:T(8,128)(2,1)S(1)}, u32[]{:S(2)}, u32[]{:S(2)}) %collective-permute-start.6) | collective-permute-done | bytes 24608 | tf_op jit(solution)/shard_map/ppermute | solution.py:579
  24.4 0.2 collective-permute-done.7
  24.6 0.3 collective-permute-start.10
  24.9 2.2 %collective-permute-start.11 = (bf16[144,128]{1,0:T(8,128)(2,1)S(1)}, bf16[144,128]{1,0:T(8,128)(2,1)S(1)}, u32[]{:S(2)}, u32[]{:S(2)}) collective-permute-start(bf16[144,128]{1,0:T(8,128)(2,1)S(1)} %get-tuple-element.98), channel_id=1, source_target_pairs={{0,12},{1,13},{2,14},{3,15},{4,8},{5,9},{6,10},{7,11},{8,4},{9,5},... | collective-permute-start | bytes 110600 | tf_op jit(solution)/shard_map/ppermute | solution.py:579
  27.1 1.0 %collective-permute-start.12 = (bf16[96,128]{1,0:T(8,128)(2,1)S(1)}, bf16[96,128]{1,0:T(8,128)(2,1)S(1)}, u32[]{:S(2)}, u32[]{:S(2)}) collective-permute-start(bf16[96,128]{1,0:T(8,128)(2,1)S(1)} %fusion), channel_id=1, source_target_pairs={{0,8},{1,9},{2,10},{3,11},{4,12},{5,13},{6,14},{7,15},{8,0},{9,1},... | collective-permute-start | bytes 73736 | tf_op jit(solution)/shard_map/ppermute | solution.py:579
  28.1 0.0 collective-permute-start.8
  28.1 1.2 %collective-permute-done.8.m1 = bf16[48,128]{1,0:T(8,128)(2,1)S(1)} collective-permute-done((bf16[48,128]{1,0:T(8,128)(2,1)S(1)}, bf16[48,128]{1,0:T(8,128)(2,1)S(1)}, u32[]{:S(2)}, u32[]{:S(2)}) %collective-permute-start.8) | collective-permute-done | bytes 12320 | tf_op jit(solution)/shard_map/ppermute | solution.py:587
  29.3 0.0 collective-permute-done.9.m2
  29.3 0.9 %shard_map.132.d_in = f32[48,4096]{1,0:T(8,128)S(1)} custom-call(bf16[48,4096]{1,0:T(8,128)(2,1)S(1)} %bitcast.14, bf16[48,4096]{1,0:T(8,128)(2,1)S(1)} %get-tuple-element.80.d_ref, bf16[9,48,48]{2,1,0:T(8,128)(2,1)S(1)} %get-tuple-element.76.w1_ref.w_ref), custom_call_target="tpu_custom_call" | custom-call | bytes 3690000 | tf_op jit(solution)/shard_map/pallas_call | solution.py:560
  30.2 0.8 %shard_map.131 = (f32[48,4096]{1,0:T(8,128)S(1)}, bf16[192,144]{1,0:T(8,128)(2,1)S(1)}, bf16[48,576]{1,0:T(8,128)(2,1)S(1)}) custom-call(bf16[48,4096]{1,0:T(8,128)(2,1)S(1)} %bitcast.17, bf16[48,4096]{1,0:T(8,128)(2,1)S(1)} %get-tuple-element.75.act_ref, bf16[9,48,48]{2,1,0:T(8,128)(2,1)S(1)} %get-tuple-element.76.w1_ref.w_ref, ...), custom_call_target="tpu_custom_call" | custom-call | bytes 5535000 | tf_op jit(solution)/shard_map/pallas_call | solution.py:560
  31.1 0.8 %collective-permute-done.12 = bf16[96,128]{1,0:T(8,128)(2,1)S(1)} collective-permute-done((bf16[96,128]{1,0:T(8,128)(2,1)S(1)}, bf16[96,128]{1,0:T(8,128)(2,1)S(1)}, u32[]{:S(2)}, u32[]{:S(2)}) %collective-permute-start.12) | collective-permute-done | bytes 24608 | tf_op jit(solution)/shard_map/ppermute | solution.py:579
  31.8 0.0 collective-permute-done.10.n1
  31.8 0.0 collective-permute-done.11.n2
  31.9 0.1 collective-permute-start.13
  31.9 1.7 %shard_map.133 = (bf16[48,4096]{1,0:T(8,128)(2,1)}, bf16[48,4096]{1,0:T(8,128)(2,1)}) custom-call(f32[48,4096]{1,0:T(8,128)S(1)} %get-tuple-element.81.partial, f32[48,4096]{1,0:T(8,128)S(1)} %shard_map.132.d_in, bf16[48,128]{1,0:T(8,128)(2,1)S(1)} %collective-permute-done.8.m1, bf16[144,128]{1,0:T(8,128)(2,1)S(1)} %collective-permute-done.9.m2, ...), custom_call_target="tpu_custom_call" | custom-call | bytes 5535000 | tf_op jit(solution)/shard_map/pallas_call | solution.py:560
  33.6 0.0 collective-permute-done.13.got
  33.6 0.8 %shard_map.134 = (f32[9,24,48]{2,1,0:T(8,128)}, f32[1,24]{1,0:T(1,128)}, f32[9,24,48]{2,1,0:T(8,128)}, f32[1,24]{1,0:T(1,128)}) custom-call(f32[96,128]{1,0:T(8,128)S(1)} %add_add_fusion.own, f32[96,128]{1,0:T(8,128)S(1)} %collective-permute-done.13.got), custom_call_target="tpu_custom_call" | custom-call | bytes 100000 | tf_op jit(solution)/shard_map/pallas_call | solution.py:560
  (7 shorter events, 0.1 us)
Async XLA Ops:
  0.6 9.0 %copy-start.2 = (bf16[9,48,48]{2,1,0:T(8,128)(2,1)S(1)}, bf16[9,48,48]{2,1,0:T(8,128)(2,1)}, u32[]{:S(2)}) copy-start(bf16[9,48,48]{2,1,0:T(8,128)(2,1)} %w1_ref.1) | copy-start | bytes 124420
  0.6 8.9 %copy-start.3 = (bf16[9,48,48]{2,1,0:T(8,128)(2,1)S(1)}, bf16[9,48,48]{2,1,0:T(8,128)(2,1)}, u32[]{:S(2)}) copy-start(bf16[9,48,48]{2,1,0:T(8,128)(2,1)} %w2_ref.1) | copy-start | bytes 124420
  2.4 11.0 %collective-permute-start.1 = (bf16[96,128]{1,0:T(8,128)(2,1)S(1)}, bf16[96,128]{1,0:T(8,128)(2,1)S(1)}, u32[]{:S(2)}, u32[]{:S(2)}) collective-permute-start(bf16[96,128]{1,0:T(8,128)(2,1)S(1)} %pad_maximum_fusion.3), channel_id=1, source_target_pairs={{0,15},{1,2},{2,1},{3,4},{4,3},{5,6},{6,5},{7,8},{8,7},{9,10},{10,... | collective-permute-start | bytes 73736 | tf_op jit(solution)/shard_map/ppermute | solution.py:588
  7.9 4.6 %collective-permute-start = (bf16[48,128]{1,0:T(8,128)(2,1)S(1)}, bf16[48,128]{1,0:T(8,128)(2,1)S(1)}, u32[]{:S(2)}, u32[]{:S(2)}) collective-permute-start(bf16[48,128]{1,0:T(8,128)(2,1)S(1)} %get-tuple-element.51), channel_id=1, source_target_pairs={{0,1},{1,0},{2,3},{3,2},{4,5},{5,4},{6,7},{7,6},{8,9},{9,8},{10,11... | collective-permute-start | bytes 36872 | tf_op jit(solution)/shard_map/ppermute | solution.py:587
  7.9 4.6 %collective-permute-start.2 = (bf16[48,128]{1,0:T(8,128)(2,1)S(1)}, bf16[48,128]{1,0:T(8,128)(2,1)S(1)}, u32[]{:S(2)}, u32[]{:S(2)}) collective-permute-start(bf16[48,128]{1,0:T(8,128)(2,1)S(1)} %get-tuple-element.53), channel_id=1, source_target_pairs={{0,4},{1,5},{2,6},{3,7},{4,0},{5,1},{6,2},{7,3},{8,12},{9,13},{10,... | collective-permute-start | bytes 36872 | tf_op jit(solution)/shard_map/ppermute | solution.py:579
  7.9 5.5 %collective-permute-start.3 = (bf16[48,128]{1,0:T(8,128)(2,1)S(1)}, bf16[48,128]{1,0:T(8,128)(2,1)S(1)}, u32[]{:S(2)}, u32[]{:S(2)}) collective-permute-start(bf16[48,128]{1,0:T(8,128)(2,1)S(1)} %get-tuple-element.54), channel_id=1, source_target_pairs={{0,12},{1,13},{2,14},{3,15},{4,8},{5,9},{6,10},{7,11},{8,4},{9,5},... | collective-permute-start | bytes 36872 | tf_op jit(solution)/shard_map/ppermute | solution.py:579
  9.6 0.7 %copy-start.4 = (f32[48]{0:T(128)S(1)}, f32[48]{0:T(128)}, u32[]{:S(2)}) copy-start(f32[48]{0:T(128)} %param.11) | copy-start | bytes 580
  9.6 0.7 %copy-start.5 = (f32[48]{0:T(128)S(1)}, f32[48]{0:T(128)}, u32[]{:S(2)}) copy-start(f32[48]{0:T(128)} %param.13) | copy-start | bytes 580
  13.4 2.2 %copy-start = (bf16[1,1,48,4096]{3,2,1,0:T(8,128)(2,1)S(1)}, bf16[1,1,48,4096]{3,2,1,0:T(8,128)(2,1)}, u32[]{:S(2)}) copy-start(bf16[1,1,48,4096]{3,2,1,0:T(8,128)(2,1)} %param.9) | copy-start | bytes 1179652
  13.4 2.2 %copy-start.1 = (bf16[1,1,48,4096]{3,2,1,0:T(8,128)(2,1)S(1)}, bf16[1,1,48,4096]{3,2,1,0:T(8,128)(2,1)}, u32[]{:S(2)}) copy-start(bf16[1,1,48,4096]{3,2,1,0:T(8,128)(2,1)} %param.8) | copy-start | bytes 1179652
  16.8 1.4 %collective-permute-start.4 = (f32[2,96,128]{2,1,0:T(8,128)S(1)}, f32[2,96,128]{2,1,0:T(8,128)S(1)}, u32[]{:S(2)}, u32[]{:S(2)}) collective-permute-start(f32[2,96,128]{2,1,0:T(8,128)S(1)} %get-tuple-element.72), channel_id=1, source_target_pairs={{0,1},{1,0},{2,3},{3,2},{4,5},{5,4},{6,7},{7,6},{8,9},{9,8},{10,11... | collective-permute-start | bytes 294920 | tf_op jit(solution)/shard_map/ppermute | solution.py:579
  18.2 5.1 %collective-permute-start.5 = (bf16[1,96,128]{2,1,0:T(8,128)(2,1)S(1)}, bf16[1,96,128]{2,1,0:T(8,128)(2,1)S(1)}, u32[]{:S(2)}, u32[]{:S(2)}) collective-permute-start(bf16[1,96,128]{2,1,0:T(8,128)(2,1)S(1)} %get-tuple-element.97), channel_id=1, source_target_pairs={{0,16},{1,17},{2,18},{3,19},{4,20},{5,21},{6,22},{7,23},{8,24},{9,... | collective-permute-start | bytes 73736 | tf_op jit(solution)/shard_map/ppermute | solution.py:579
  19.8 4.7 %collective-permute-start.7 = (bf16[1,96,128]{2,1,0:T(8,128)(2,1)S(1)}, bf16[1,96,128]{2,1,0:T(8,128)(2,1)S(1)}, u32[]{:S(2)}, u32[]{:S(2)}) collective-permute-start(bf16[1,96,128]{2,1,0:T(8,128)(2,1)S(1)} %get-tuple-element.97), channel_id=1, source_target_pairs={{0,18},{1,19},{2,16},{3,17},{4,22},{5,23},{6,20},{7,21},{8,26},{9,... | collective-permute-start | bytes 73736 | tf_op jit(solution)/shard_map/ppermute | solution.py:579
  20.5 3.8 %collective-permute-start.6 = (bf16[1,96,128]{2,1,0:T(8,128)(2,1)S(1)}, bf16[1,96,128]{2,1,0:T(8,128)(2,1)S(1)}, u32[]{:S(2)}, u32[]{:S(2)}) collective-permute-start(bf16[1,96,128]{2,1,0:T(8,128)(2,1)S(1)} %get-tuple-element.96), channel_id=1, source_target_pairs={{0,2},{1,3},{2,0},{3,1},{4,6},{5,7},{6,4},{7,5},{8,10},{9,11},{10,... | collective-permute-start | bytes 73736 | tf_op jit(solution)/shard_map/ppermute | solution.py:579
  21.8 7.5 %collective-permute-start.9 = (bf16[144,128]{1,0:T(8,128)(2,1)S(1)}, bf16[144,128]{1,0:T(8,128)(2,1)S(1)}, u32[]{:S(2)}, u32[]{:S(2)}) collective-permute-start(bf16[144,128]{1,0:T(8,128)(2,1)S(1)} %pad_maximum_fusion.2), channel_id=1, source_target_pairs={{0,15},{1,2},{2,1},{3,4},{4,3},{5,6},{6,5},{7,8},{8,7},{9,10},{10,... | collective-permute-start | bytes 110600 | tf_op jit(solution)/shard_map/ppermute | solution.py:588
  24.6 7.3 %collective-permute-start.10 = (bf16[144,128]{1,0:T(8,128)(2,1)S(1)}, bf16[144,128]{1,0:T(8,128)(2,1)S(1)}, u32[]{:S(2)}, u32[]{:S(2)}) collective-permute-start(bf16[144,128]{1,0:T(8,128)(2,1)S(1)} %get-tuple-element.99), channel_id=1, source_target_pairs={{0,4},{1,5},{2,6},{3,7},{4,0},{5,1},{6,2},{7,3},{8,12},{9,13},{10,... | collective-permute-start | bytes 110600 | tf_op jit(solution)/shard_map/ppermute | solution.py:579
  24.9 7.0 %collective-permute-start.11 = (bf16[144,128]{1,0:T(8,128)(2,1)S(1)}, bf16[144,128]{1,0:T(8,128)(2,1)S(1)}, u32[]{:S(2)}, u32[]{:S(2)}) collective-permute-start(bf16[144,128]{1,0:T(8,128)(2,1)S(1)} %get-tuple-element.98), channel_id=1, source_target_pairs={{0,12},{1,13},{2,14},{3,15},{4,8},{5,9},{6,10},{7,11},{8,4},{9,5},... | collective-permute-start | bytes 110600 | tf_op jit(solution)/shard_map/ppermute | solution.py:579
  27.1 4.7 %collective-permute-start.12 = (bf16[96,128]{1,0:T(8,128)(2,1)S(1)}, bf16[96,128]{1,0:T(8,128)(2,1)S(1)}, u32[]{:S(2)}, u32[]{:S(2)}) collective-permute-start(bf16[96,128]{1,0:T(8,128)(2,1)S(1)} %fusion), channel_id=1, source_target_pairs={{0,8},{1,9},{2,10},{3,11},{4,12},{5,13},{6,14},{7,15},{8,0},{9,1},... | collective-permute-start | bytes 73736 | tf_op jit(solution)/shard_map/ppermute | solution.py:579
  28.1 1.2 %collective-permute-start.8 = (bf16[48,128]{1,0:T(8,128)(2,1)S(1)}, bf16[48,128]{1,0:T(8,128)(2,1)S(1)}, u32[]{:S(2)}, u32[]{:S(2)}) collective-permute-start(bf16[48,128]{1,0:T(8,128)(2,1)S(1)} %get-tuple-element.73), channel_id=1, source_target_pairs={{0,1},{1,0},{2,3},{3,2},{4,5},{5,4},{6,7},{7,6},{8,9},{9,8},{10,11... | collective-permute-start | bytes 36872 | tf_op jit(solution)/shard_map/ppermute | solution.py:587
  31.9 1.8 %collective-permute-start.13 = (f32[96,128]{1,0:T(8,128)S(1)}, f32[96,128]{1,0:T(8,128)S(1)}, u32[]{:S(2)}, u32[]{:S(2)}) collective-permute-start(f32[96,128]{1,0:T(8,128)S(1)} %add_add_fusion.own), channel_id=1, source_target_pairs={{0,1},{1,0},{2,3},{3,2},{4,5},{5,4},{6,7},{7,6},{8,9},{9,8},{10,11... | collective-permute-start | bytes 147464 | tf_op jit(solution)/shard_map/ppermute | solution.py:579

commit v5 on v4

--- a/solution.py
+++ b/solution.py
@@ -88,7 +88,8 @@
 def send_choice(tables, spaces):
     me, even, inner = roles(spaces)
     hop = spaces // 4
-    line, place = line_lanes(iota((256, 1), 0))
+    line, place = line_lanes(iota((256, LANES), 0))
+    code = line * 64 + place
     lane = iota((1, LANES), 1)
     low = lane < 64
     spot = lane & 63
@@ -100,7 +101,7 @@
         r = tables[2, edge, target]
         turned = (r == 1) | (r == 2)
         wanted = jnp.where(low, k, lax.rem(edge + 2, 4)) * 64 + jnp.where(low & turned, 63 - spot, spot)
-        chosen.append(jnp.where(line * 64 + place == wanted, 1.0, 0.0).astype(BF))
+        chosen.append(jnp.where(code == wanted, 1.0, 0.0).astype(BF))
     return jnp.concatenate(chosen, axis=1)
 
 
@@ -132,7 +133,7 @@
 
 
 def send_kernel(
-    spaces, tables_hbm, x_hbm, g_hbm, m1, m2, n1, n2, x_ref, g_ref, tables, table_sem, x_sem, g_sem,
+    spaces, tables_hbm, x_hbm, g_hbm, m1, m2, n1, n2, x_ref, g_ref, choice_out, tables, table_sem, x_sem, g_sem,
 ):
     wide = PIX // CHUNKS
     fetch = pltpu.make_async_copy(tables_hbm, tables, table_sem)
@@ -149,6 +150,7 @@
         copies.append(pair)
     fetch.wait()
     choice = send_choice(tables, spaces)
+    choice_out[...] = choice
     parts = [[], []]
     for part in range(CHUNKS):
         for field, ref in enumerate((x_ref, g_ref)):
@@ -296,7 +298,7 @@
 
 def prepare_kernel(
     spaces, tables_hbm, rules_hbm, x_ref, g_ref, w1_ref, w2_ref, b1_ref, b2_ref,
-    d_act, pre_in, x_side, route, halo, w_edge, back2, w1_out, w2_out, b1_out, b2_out,
+    d_act, pre_in, x_side, route, halo, w_edge, back2, b1_out, b2_out,
     half, tables, rules, table_sem,
 ):
     fetches = [
@@ -312,8 +314,6 @@
     w_edge[0 : 2 * C] = row_form(taps1)
     w_edge[2 * C :] = jnp.concatenate([wf1[0:C], wf1[2 * C : 3 * C]], axis=0)
     back2[...] = return_form(taps2)
-    w1_out[...] = w1_ref[...]
-    w2_out[...] = w2_ref[...]
     b1_out[...] = column(b1_ref)
     b2_out[...] = column(b2_ref)
     zero = jnp.zeros((C, LANES), BF)
@@ -371,11 +371,9 @@
 
 
 def middle_kernel(
-    spaces, tables_hbm, m1, m2, n1, n2, d_act, pre_in, route, halo, w_edge, back, bias,
-    act_ref, d_ref, p0, p1, p2, p3, beside_ref, users_ref, act_lines, d_lines, tables, table_sem,
+    spaces, choice, m1, m2, n1, n2, d_act, pre_in, route, halo, w_edge, back, bias,
+    act_ref, d_ref, p0, p1, p2, p3, beside_ref, users_ref, act_lines, d_lines,
 ):
-    fetch = pltpu.make_async_copy(tables_hbm, tables, table_sem)
-    fetch.start()
     lines, borders = by_edge(spaces, (m1, m2, n1, n2))
     beside = beside_lines(lines, halo)
     beside_ref[...] = beside
@@ -410,8 +408,7 @@
     d_l = lines_from(d_edges, ends[0][1], ends[TILES - 1][1])
     act_lines[...] = act_l
     d_lines[...] = d_l
-    fetch.wait()
-    for out, block in zip((p0, p1, p2, p3), send_blocks(send_choice(tables, spaces), act_l, d_l)):
+    for out, block in zip((p0, p1, p2, p3), send_blocks(choice[...], act_l, d_l)):
         out[...] = block
 
 
@@ -653,10 +650,9 @@
     tables = neighbours.transpose(2, 1, 0)
     rules = corner_rule.transpose(1, 0)
 
-    weights = (conv_one.shape, BF)
     bias = ((C, LANES), F32)
-    *sent, x_near, g_near = call(
-        functools.partial(send_kernel, spaces), [line] * 4 + [image, image], [HBM] * 3, (in_hbm(tables), in_hbm(x), in_hbm(g)),
+    *sent, x_near, g_near, choice = call(
+        functools.partial(send_kernel, spaces), [line] * 4 + [image, image, ((256, 512), BF)], [HBM] * 3, (in_hbm(tables), in_hbm(x), in_hbm(g)),
         [pltpu.SMEM(tables.shape, jnp.int32), pltpu.SemaphoreType.DMA, pltpu.SemaphoreType.DMA((CHUNKS,)),
          pltpu.SemaphoreType.DMA((CHUNKS,))],
         read=COST * 2,
@@ -665,10 +661,10 @@
     arrived = swap_along(sent[:2], spaces, 2) + swap_across(sent[2:], spaces, devices)
     edges = ((4 * C, 3 * C), BF)
     back = ((C, 12 * C), BF)
-    d_act, pre_in, x_side, route, halo, w_edge, back2, w_one, w_two, b_one, b_two = call(
+    d_act, pre_in, x_side, route, halo, w_edge, back2, b_one, b_two = call(
         functools.partial(prepare_kernel, spaces),
         [wide, wide, ((2 * C, PIX), BF), ((4, SIDE, 768), BF), ((256, 384), BF), edges, back,
-         weights, weights, bias, bias],
+         bias, bias],
         [HBM, HBM] + [VMEM] * 6,
         (in_hbm(tables), in_hbm(rules), x_near, g_near, conv_one, conv_two, bias_one.reshape(1, C), bias_two.reshape(1, C)),
         [half, pltpu.SMEM(tables.shape, jnp.int32), pltpu.SMEM(rules.shape, jnp.int32), pltpu.SemaphoreType.DMA((2,))],
@@ -677,9 +673,8 @@
     middle = call(
         functools.partial(middle_kernel, spaces),
         [image, image] + [line] * 4 + [((3 * C, 256), BF), ((12 * C, 256), BF), ((C, 256), BF), ((C, 256), BF)],
-        [HBM] + [VMEM] * 11,
-        (in_hbm(tables), *arrived, d_act, pre_in, route, halo, w_edge, back2, b_one),
-        [pltpu.SMEM(tables.shape, jnp.int32), pltpu.SemaphoreType.DMA],
+        [VMEM] * 12,
+        (choice, *arrived, d_act, pre_in, route, halo, w_edge, back2, b_one),
         read=COST * 9 // 4,
     )
     act, d_pre = middle[:2]
@@ -695,9 +690,9 @@
     blocks = middle[2:6]
     again = swap_along(blocks[:2], spaces, 3)
     act_late, d_late, *again = lax.optimization_barrier((act, d_pre, *again))
-    (d_in,) = call(inner_kernel, [wide], [VMEM] * 3, (g, d_late, w_one), [half], read=COST)
+    (d_in,) = call(inner_kernel, [wide], [VMEM] * 3, (g, d_late, conv_one), [half], read=COST)
     partial, edges_two, back_one = call(
-        partial_kernel, [wide, edges, back], [VMEM] * 5, (x, act_late, w_one, w_two, b_two), [half], read=COST * 3 // 2
+        partial_kernel, [wide, edges, back], [VMEM] * 5, (x, act_late, conv_one, conv_two, b_two), [half], read=COST * 3 // 2
     )
     held = mine + swapped(other, 1, devices)
     for bits in first_rounds(parts, spaces):

time: 34.7 us -> 33.8 us (0.974)
  Pallas kernels: 11.6 us -> 10.8 us
    pallas_call x8, Pallas kernels: 11.6 us -> 10.8 us  [call(): pl.pallas_call(kernel, out_shape=[jax.ShapeDtypeStruct(shape, dtype) for...]
  transfers between devices with their start and end apart: 14 -> 14, of which waited for: 6 -> 6; matrix products, arithmetic and copies ran while one was open for 0% -> 0% of each run, Pallas kernels for 16% -> 17%
where the time goes in v5:
time: 33.8 us; the launch traced here: 33.6 us
  starting transfers between devices  16 us (47%)
  Pallas kernels  10.8 us (32%)
  waiting for transfers between devices  5.24 us (16%)
  between operations  0.81 us (2%)
  local copies, waits for them, and re-layouts  0.68 us (2%)
    pallas_call x8, Pallas kernels, call(): pl.pallas_call(kernel, out_shape=[jax.ShapeDtypeStruct(shape, dtype) for...  10.8 us
    ppermute x10, starting transfers between devices, swapped(): lax.ppermute(block, ('dp', 'space'), [(i, i ^ mask) for i in range(device...  8.94 us
    ppermute x2, starting transfers between devices, swap_along(): lax.ppermute(jnp.concatenate([blocks[1]] * more, axis=0) if more > 1 else...  7.07 us
    ppermute x10, waiting for transfers between devices, swapped(): lax.ppermute(block, ('dp', 'space'), [(i, i ^ mask) for i in range(device...  4.06 us
    ppermute x2, waiting for transfers between devices, swap_along(): lax.ppermute(blocks[0], 'space', [(i, i ^ 1) for i in range(spaces)])  1.18 us
    unnamed x12, local copies, waits for them, and re-layouts  0.68 us
  transfers between devices with their start and end apart: 14, of which 6 were waited for; matrix products, arithmetic and copies ran while one was open for 0% of the time, Pallas kernels for 17%

profile of v5, /device:TPU:0, one launch (start us, length us, event | category | flops | bytes accessed | tf_op | source)
XLA Modules:
  0.0 33.6 jit_solution(984004538826249225)
XLA Ops:
  0.6 0.0 copy-start.2
  0.6 0.0 copy-start.3
  0.7 1.7 %shard_map.127 = (bf16[48,128]{1,0:T(8,128)(2,1)S(1)}, bf16[48,128]{1,0:T(8,128)(2,1)S(1)}, bf16[48,128]{1,0:T(8,128)(2,1)S(1)}, bf16[48,128]{1,0:T(8,128)(2,1)S...) custom-call(s32[3,4,16]{2,1,0:T(4,128)} %bitcast.20, ...), custom_call_target="tpu_custom_call" | custom-call | bytes 7380000 | tf_op jit(solution)/shard_map/pallas_call | solution.py:557
  2.4 5.5 %collective-permute-start.1 = (bf16[96,128]{1,0:T(8,128)(2,1)S(1)}, bf16[96,128]{1,0:T(8,128)(2,1)S(1)}, u32[]{:S(2)}, u32[]{:S(2)}) collective-permute-start(bf16[96,128]{1,0:T(8,128)(2,1)S(1)} %pad_maximum_fusion.3), channel_id=1, source_target_pairs={{0,15},{1,2},{2,1},{3,4},{4,3},{5,6},{6,5},{7,8},{8,7},{9,10},{10,... | collective-permute-start | bytes 73736 | tf_op jit(solution)/shard_map/ppermute | solution.py:585
  7.9 0.0 collective-permute-start
  7.9 0.0 collective-permute-start.2
  7.9 1.7 %collective-permute-start.3 = (bf16[48,128]{1,0:T(8,128)(2,1)S(1)}, bf16[48,128]{1,0:T(8,128)(2,1)S(1)}, u32[]{:S(2)}, u32[]{:S(2)}) collective-permute-start(bf16[48,128]{1,0:T(8,128)(2,1)S(1)} %get-tuple-element.54), channel_id=1, source_target_pairs={{0,12},{1,13},{2,14},{3,15},{4,8},{5,9},{6,10},{7,11},{8,4},{9,5},... | collective-permute-start | bytes 36872 | tf_op jit(solution)/shard_map/ppermute | solution.py:576
  9.6 0.0 copy-start.4
  9.6 0.0 copy-start.5
  9.6 0.0 copy-done.2
  9.6 0.0 copy-done.3
  9.6 0.6 %copy-done.4 = f32[48]{0:T(128)S(1)} copy-done((f32[48]{0:T(128)S(1)}, f32[48]{0:T(128)}, u32[]{:S(2)}) %copy-start.4) | copy-done | bytes 216
  10.2 0.0 copy-done.5
  10.3 2.2 %shard_map.128 = (f32[48,4096]{1,0:T(8,128)S(1)}, f32[48,4096]{1,0:T(8,128)S(1)}, bf16[96,4096]{1,0:T(8,128)(2,1)S(1)}, bf16[4,64,768]{2,1,0:T(8,128)(2,1)S(1)},...) custom-call(s32[3,4,16]{2,1,0:T(4,128)} %bitcast.21, ...), custom_call_target="tpu_custom_call" | custom-call | bytes 11070000 | tf_op jit(solution)/shard_map/pallas_call | solution.py:557
  12.5 0.0 collective-permute-done.m1
  12.5 0.0 collective-permute-done.2.n1
  12.5 0.9 %collective-permute-done.3.n2 = bf16[48,128]{1,0:T(8,128)(2,1)S(1)} collective-permute-done((bf16[48,128]{1,0:T(8,128)(2,1)S(1)}, bf16[48,128]{1,0:T(8,128)(2,1)S(1)}, u32[]{:S(2)}, u32[]{:S(2)}) %collective-permute-start.3) | collective-permute-done | bytes 12320 | tf_op jit(solution)/shard_map/ppermute | solution.py:576
  13.4 0.0 collective-permute-done.1.m2
  13.4 0.0 copy-start
  13.4 0.0 copy-start.1
  13.4 1.4 %shard_map.129 = (bf16[48,4096]{1,0:T(8,128)(2,1)S(1)}, bf16[48,4096]{1,0:T(8,128)(2,1)S(1)}, bf16[48,128]{1,0:T(8,128)(2,1)S(1)}, bf16[48,128]{1,0:T(8,128)(2,1...) custom-call(bf16[256,512]{1,0:T(8,128)(2,1)S(1)} %get-tuple-element., ...), custom_call_target="tpu_custom_call" | custom-call | bytes 8302500 | tf_op jit(solution)/shard_map/pallas_call | solution.py:557
  14.8 0.0 copy-done
  14.8 0.0 copy-done.1
  14.8 1.2 %shard_map.130 = (f32[2,96,128]{2,1,0:T(8,128)S(1)}, f32[2,96,128]{2,1,0:T(8,128)S(1)}) custom-call(bf16[48,4096]{1,0:T(8,128)(2,1)S(1)} %bitcast.16, bf16[48,4096]{1,0:T(8,128)(2,1)S(1)} %bitcast.13, bf16[48,4096]{1,0:T(8,128)(2,1)S(1)} %get-tuple-element.75.act_ref, bf16[48,4096]{1,0:T(8,128)(2,1)S(1)} %get-tuple-element.78.d_ref, ...), custom_call_target="tpu_custom_call" | custom-call | bytes 4612500 | tf_op jit(solution)/shard_map/pallas_call | solution.py:557
  16.0 0.1 collective-permute-start.4
  16.1 1.3 %collective-permute-done.4 = f32[2,96,128]{2,1,0:T(8,128)S(1)} collective-permute-done((f32[2,96,128]{2,1,0:T(8,128)S(1)}, f32[2,96,128]{2,1,0:T(8,128)S(1)}, u32[]{:S(2)}, u32[]{:S(2)}) %collective-permute-start.4) | collective-permute-done | bytes 98336 | tf_op jit(solution)/shard_map/ppermute | solution.py:576
  17.4 1.6 %collective-permute-start.5 = (bf16[1,96,128]{2,1,0:T(8,128)(2,1)S(1)}, bf16[1,96,128]{2,1,0:T(8,128)(2,1)S(1)}, u32[]{:S(2)}, u32[]{:S(2)}) collective-permute-start(bf16[1,96,128]{2,1,0:T(8,128)(2,1)S(1)} %get-tuple-element.95), channel_id=1, source_target_pairs={{0,16},{1,17},{2,18},{3,19},{4,20},{5,21},{6,22},{7,23},{8,24},{9,... | collective-permute-start | bytes 73736 | tf_op jit(solution)/shard_map/ppermute | solution.py:576
  19.0 0.7 %collective-permute-start.7 = (bf16[1,96,128]{2,1,0:T(8,128)(2,1)S(1)}, bf16[1,96,128]{2,1,0:T(8,128)(2,1)S(1)}, u32[]{:S(2)}, u32[]{:S(2)}) collective-permute-start(bf16[1,96,128]{2,1,0:T(8,128)(2,1)S(1)} %get-tuple-element.95), channel_id=1, source_target_pairs={{0,18},{1,19},{2,16},{3,17},{4,22},{5,23},{6,20},{7,21},{8,26},{9,... | collective-permute-start | bytes 73736 | tf_op jit(solution)/shard_map/ppermute | solution.py:576
  19.7 1.3 %collective-permute-start.6 = (bf16[1,96,128]{2,1,0:T(8,128)(2,1)S(1)}, bf16[1,96,128]{2,1,0:T(8,128)(2,1)S(1)}, u32[]{:S(2)}, u32[]{:S(2)}) collective-permute-start(bf16[1,96,128]{2,1,0:T(8,128)(2,1)S(1)} %get-tuple-element.94), channel_id=1, source_target_pairs={{0,2},{1,3},{2,0},{3,1},{4,6},{5,7},{6,4},{7,5},{8,10},{9,11},{10,... | collective-permute-start | bytes 73736 | tf_op jit(solution)/shard_map/ppermute | solution.py:576
  21.0 1.6 %collective-permute-start.9 = (bf16[144,128]{1,0:T(8,128)(2,1)S(1)}, bf16[144,128]{1,0:T(8,128)(2,1)S(1)}, u32[]{:S(2)}, u32[]{:S(2)}) collective-permute-start(bf16[144,128]{1,0:T(8,128)(2,1)S(1)} %pad_maximum_fusion.2), channel_id=1, source_target_pairs={{0,15},{1,2},{2,1},{3,4},{4,3},{5,6},{6,5},{7,8},{8,7},{9,10},{10,... | collective-permute-start | bytes 110600 | tf_op jit(solution)/shard_map/ppermute | solution.py:585
  22.6 0.0 collective-permute-done.5
  22.6 1.0 %collective-permute-done.6 = bf16[1,96,128]{2,1,0:T(8,128)(2,1)S(1)} collective-permute-done((bf16[1,96,128]{2,1,0:T(8,128)(2,1)S(1)}, bf16[1,96,128]{2,1,0:T(8,128)(2,1)S(1)}, u32[]{:S(2)}, u32[]{:S(2)}) %collective-permute-start.6) | collective-permute-done | bytes 24608 | tf_op jit(solution)/shard_map/ppermute | solution.py:576
  23.5 0.2 collective-permute-done.7
  23.8 0.3 collective-permute-start.10
  24.1 2.2 %collective-permute-start.11 = (bf16[144,128]{1,0:T(8,128)(2,1)S(1)}, bf16[144,128]{1,0:T(8,128)(2,1)S(1)}, u32[]{:S(2)}, u32[]{:S(2)}) collective-permute-start(bf16[144,128]{1,0:T(8,128)(2,1)S(1)} %get-tuple-element.96), channel_id=1, source_target_pairs={{0,12},{1,13},{2,14},{3,15},{4,8},{5,9},{6,10},{7,11},{8,4},{9,5},... | collective-permute-start | bytes 110600 | tf_op jit(solution)/shard_map/ppermute | solution.py:576
  26.3 1.0 %collective-permute-start.12 = (bf16[96,128]{1,0:T(8,128)(2,1)S(1)}, bf16[96,128]{1,0:T(8,128)(2,1)S(1)}, u32[]{:S(2)}, u32[]{:S(2)}) collective-permute-start(bf16[96,128]{1,0:T(8,128)(2,1)S(1)} %fusion), channel_id=1, source_target_pairs={{0,8},{1,9},{2,10},{3,11},{4,12},{5,13},{6,14},{7,15},{8,0},{9,1},... | collective-permute-start | bytes 73736 | tf_op jit(solution)/shard_map/ppermute | solution.py:576
  27.3 0.0 collective-permute-start.8
  27.3 1.2 %collective-permute-done.8.m1 = bf16[48,128]{1,0:T(8,128)(2,1)S(1)} collective-permute-done((bf16[48,128]{1,0:T(8,128)(2,1)S(1)}, bf16[48,128]{1,0:T(8,128)(2,1)S(1)}, u32[]{:S(2)}, u32[]{:S(2)}) %collective-permute-start.8) | collective-permute-done | bytes 12320 | tf_op jit(solution)/shard_map/ppermute | solution.py:584
  28.5 0.0 collective-permute-done.9.m2
  28.5 0.9 %shard_map.132.d_in = f32[48,4096]{1,0:T(8,128)S(1)} custom-call(bf16[48,4096]{1,0:T(8,128)(2,1)S(1)} %bitcast.14, bf16[48,4096]{1,0:T(8,128)(2,1)S(1)} %get-tuple-element.78.d_ref, bf16[9,48,48]{2,1,0:T(8,128)(2,1)S(1)} %copy-done.2), custom_call_target="tpu_custom_call" | custom-call | bytes 3690000 | tf_op jit(solution)/shard_map/pallas_call | solution.py:557
  29.4 0.8 %shard_map.131 = (f32[48,4096]{1,0:T(8,128)S(1)}, bf16[192,144]{1,0:T(8,128)(2,1)S(1)}, bf16[48,576]{1,0:T(8,128)(2,1)S(1)}) custom-call(bf16[48,4096]{1,0:T(8,128)(2,1)S(1)} %bitcast.17, bf16[48,4096]{1,0:T(8,128)(2,1)S(1)} %get-tuple-element.75.act_ref, bf16[9,48,48]{2,1,0:T(8,128)(2,1)S(1)} %copy-done.2, bf16[9,48,48]{2,1,0:T(8,128)(2,1)S(1)} %copy-done.3, ...), custom_call_target="tpu_custom_call" | custom-call | bytes 5535000 | tf_op jit(solution)/shard_map/pallas_call | solution.py:557
  30.3 0.7 %collective-permute-done.12 = bf16[96,128]{1,0:T(8,128)(2,1)S(1)} collective-permute-done((bf16[96,128]{1,0:T(8,128)(2,1)S(1)}, bf16[96,128]{1,0:T(8,128)(2,1)S(1)}, u32[]{:S(2)}, u32[]{:S(2)}) %collective-permute-start.12) | collective-permute-done | bytes 24608 | tf_op jit(solution)/shard_map/ppermute | solution.py:576
  31.0 0.0 collective-permute-done.10.n1
  31.0 0.0 collective-permute-done.11.n2
  31.0 0.1 collective-permute-start.13
  31.1 1.7 %shard_map.133 = (bf16[48,4096]{1,0:T(8,128)(2,1)}, bf16[48,4096]{1,0:T(8,128)(2,1)}) custom-call(f32[48,4096]{1,0:T(8,128)S(1)} %get-tuple-element.79.partial, f32[48,4096]{1,0:T(8,128)S(1)} %shard_map.132.d_in, bf16[48,128]{1,0:T(8,128)(2,1)S(1)} %collective-permute-done.8.m1, bf16[144,128]{1,0:T(8,128)(2,1)S(1)} %collective-permute-done.9.m2, ...), custom_call_target="tpu_custom_call" | custom-call | bytes 5535000 | tf_op jit(solution)/shard_map/pallas_call | solution.py:557
  32.8 0.0 collective-permute-done.13.got
  32.8 0.8 %shard_map.134 = (f32[9,24,48]{2,1,0:T(8,128)}, f32[1,24]{1,0:T(1,128)}, f32[9,24,48]{2,1,0:T(8,128)}, f32[1,24]{1,0:T(1,128)}) custom-call(f32[96,128]{1,0:T(8,128)S(1)} %add_add_fusion.own, f32[96,128]{1,0:T(8,128)S(1)} %collective-permute-done.13.got), custom_call_target="tpu_custom_call" | custom-call | bytes 100000 | tf_op jit(solution)/shard_map/pallas_call | solution.py:557
  (7 shorter events, 0.1 us)
Async XLA Ops:
  0.6 9.0 %copy-start.2 = (bf16[9,48,48]{2,1,0:T(8,128)(2,1)S(1)}, bf16[9,48,48]{2,1,0:T(8,128)(2,1)}, u32[]{:S(2)}) copy-start(bf16[9,48,48]{2,1,0:T(8,128)(2,1)} %w_ref.1) | copy-start | bytes 124420
  0.6 8.9 %copy-start.3 = (bf16[9,48,48]{2,1,0:T(8,128)(2,1)S(1)}, bf16[9,48,48]{2,1,0:T(8,128)(2,1)}, u32[]{:S(2)}) copy-start(bf16[9,48,48]{2,1,0:T(8,128)(2,1)} %w2_ref.3) | copy-start | bytes 124420
  2.4 11.0 %collective-permute-start.1 = (bf16[96,128]{1,0:T(8,128)(2,1)S(1)}, bf16[96,128]{1,0:T(8,128)(2,1)S(1)}, u32[]{:S(2)}, u32[]{:S(2)}) collective-permute-start(bf16[96,128]{1,0:T(8,128)(2,1)S(1)} %pad_maximum_fusion.3), channel_id=1, source_target_pairs={{0,15},{1,2},{2,1},{3,4},{4,3},{5,6},{6,5},{7,8},{8,7},{9,10},{10,... | collective-permute-start | bytes 73736 | tf_op jit(solution)/shard_map/ppermute | solution.py:585
  7.9 4.6 %collective-permute-start = (bf16[48,128]{1,0:T(8,128)(2,1)S(1)}, bf16[48,128]{1,0:T(8,128)(2,1)S(1)}, u32[]{:S(2)}, u32[]{:S(2)}) collective-permute-start(bf16[48,128]{1,0:T(8,128)(2,1)S(1)} %get-tuple-element.51), channel_id=1, source_target_pairs={{0,1},{1,0},{2,3},{3,2},{4,5},{5,4},{6,7},{7,6},{8,9},{9,8},{10,11... | collective-permute-start | bytes 36872 | tf_op jit(solution)/shard_map/ppermute | solution.py:584
  7.9 4.6 %collective-permute-start.2 = (bf16[48,128]{1,0:T(8,128)(2,1)S(1)}, bf16[48,128]{1,0:T(8,128)(2,1)S(1)}, u32[]{:S(2)}, u32[]{:S(2)}) collective-permute-start(bf16[48,128]{1,0:T(8,128)(2,1)S(1)} %get-tuple-element.53), channel_id=1, source_target_pairs={{0,4},{1,5},{2,6},{3,7},{4,0},{5,1},{6,2},{7,3},{8,12},{9,13},{10,... | collective-permute-start | bytes 36872 | tf_op jit(solution)/shard_map/ppermute | solution.py:576
  7.9 5.5 %collective-permute-start.3 = (bf16[48,128]{1,0:T(8,128)(2,1)S(1)}, bf16[48,128]{1,0:T(8,128)(2,1)S(1)}, u32[]{:S(2)}, u32[]{:S(2)}) collective-permute-start(bf16[48,128]{1,0:T(8,128)(2,1)S(1)} %get-tuple-element.54), channel_id=1, source_target_pairs={{0,12},{1,13},{2,14},{3,15},{4,8},{5,9},{6,10},{7,11},{8,4},{9,5},... | collective-permute-start | bytes 36872 | tf_op jit(solution)/shard_map/ppermute | solution.py:576
  9.6 0.7 %copy-start.4 = (f32[48]{0:T(128)S(1)}, f32[48]{0:T(128)}, u32[]{:S(2)}) copy-start(f32[48]{0:T(128)} %param.11) | copy-start | bytes 580
  9.6 0.7 %copy-start.5 = (f32[48]{0:T(128)S(1)}, f32[48]{0:T(128)}, u32[]{:S(2)}) copy-start(f32[48]{0:T(128)} %param.13) | copy-start | bytes 580
  13.4 1.4 %copy-start = (bf16[1,1,48,4096]{3,2,1,0:T(8,128)(2,1)S(1)}, bf16[1,1,48,4096]{3,2,1,0:T(8,128)(2,1)}, u32[]{:S(2)}) copy-start(bf16[1,1,48,4096]{3,2,1,0:T(8,128)(2,1)} %param.9) | copy-start | bytes 1179652
  13.4 1.4 %copy-start.1 = (bf16[1,1,48,4096]{3,2,1,0:T(8,128)(2,1)S(1)}, bf16[1,1,48,4096]{3,2,1,0:T(8,128)(2,1)}, u32[]{:S(2)}) copy-start(bf16[1,1,48,4096]{3,2,1,0:T(8,128)(2,1)} %param.8) | copy-start | bytes 1179652
  16.0 1.4 %collective-permute-start.4 = (f32[2,96,128]{2,1,0:T(8,128)S(1)}, f32[2,96,128]{2,1,0:T(8,128)S(1)}, u32[]{:S(2)}, u32[]{:S(2)}) collective-permute-start(f32[2,96,128]{2,1,0:T(8,128)S(1)} %get-tuple-element.72), channel_id=1, source_target_pairs={{0,1},{1,0},{2,3},{3,2},{4,5},{5,4},{6,7},{7,6},{8,9},{9,8},{10,11... | collective-permute-start | bytes 294920 | tf_op jit(solution)/shard_map/ppermute | solution.py:576
  17.4 5.1 %collective-permute-start.5 = (bf16[1,96,128]{2,1,0:T(8,128)(2,1)S(1)}, bf16[1,96,128]{2,1,0:T(8,128)(2,1)S(1)}, u32[]{:S(2)}, u32[]{:S(2)}) collective-permute-start(bf16[1,96,128]{2,1,0:T(8,128)(2,1)S(1)} %get-tuple-element.95), channel_id=1, source_target_pairs={{0,16},{1,17},{2,18},{3,19},{4,20},{5,21},{6,22},{7,23},{8,24},{9,... | collective-permute-start | bytes 73736 | tf_op jit(solution)/shard_map/ppermute | solution.py:576
  19.0 4.7 %collective-permute-start.7 = (bf16[1,96,128]{2,1,0:T(8,128)(2,1)S(1)}, bf16[1,96,128]{2,1,0:T(8,128)(2,1)S(1)}, u32[]{:S(2)}, u32[]{:S(2)}) collective-permute-start(bf16[1,96,128]{2,1,0:T(8,128)(2,1)S(1)} %get-tuple-element.95), channel_id=1, source_target_pairs={{0,18},{1,19},{2,16},{3,17},{4,22},{5,23},{6,20},{7,21},{8,26},{9,... | collective-permute-start | bytes 73736 | tf_op jit(solution)/shard_map/ppermute | solution.py:576
  19.7 3.8 %collective-permute-start.6 = (bf16[1,96,128]{2,1,0:T(8,128)(2,1)S(1)}, bf16[1,96,128]{2,1,0:T(8,128)(2,1)S(1)}, u32[]{:S(2)}, u32[]{:S(2)}) collective-permute-start(bf16[1,96,128]{2,1,0:T(8,128)(2,1)S(1)} %get-tuple-element.94), channel_id=1, source_target_pairs={{0,2},{1,3},{2,0},{3,1},{4,6},{5,7},{6,4},{7,5},{8,10},{9,11},{10,... | collective-permute-start | bytes 73736 | tf_op jit(solution)/shard_map/ppermute | solution.py:576
  21.0 7.5 %collective-permute-start.9 = (bf16[144,128]{1,0:T(8,128)(2,1)S(1)}, bf16[144,128]{1,0:T(8,128)(2,1)S(1)}, u32[]{:S(2)}, u32[]{:S(2)}) collective-permute-start(bf16[144,128]{1,0:T(8,128)(2,1)S(1)} %pad_maximum_fusion.2), channel_id=1, source_target_pairs={{0,15},{1,2},{2,1},{3,4},{4,3},{5,6},{6,5},{7,8},{8,7},{9,10},{10,... | collective-permute-start | bytes 110600 | tf_op jit(solution)/shard_map/ppermute | solution.py:585
  23.8 7.2 %collective-permute-start.10 = (bf16[144,128]{1,0:T(8,128)(2,1)S(1)}, bf16[144,128]{1,0:T(8,128)(2,1)S(1)}, u32[]{:S(2)}, u32[]{:S(2)}) collective-permute-start(bf16[144,128]{1,0:T(8,128)(2,1)S(1)} %get-tuple-element.97), channel_id=1, source_target_pairs={{0,4},{1,5},{2,6},{3,7},{4,0},{5,1},{6,2},{7,3},{8,12},{9,13},{10,... | collective-permute-start | bytes 110600 | tf_op jit(solution)/shard_map/ppermute | solution.py:576
  24.1 6.9 %collective-permute-start.11 = (bf16[144,128]{1,0:T(8,128)(2,1)S(1)}, bf16[144,128]{1,0:T(8,128)(2,1)S(1)}, u32[]{:S(2)}, u32[]{:S(2)}) collective-permute-start(bf16[144,128]{1,0:T(8,128)(2,1)S(1)} %get-tuple-element.96), channel_id=1, source_target_pairs={{0,12},{1,13},{2,14},{3,15},{4,8},{5,9},{6,10},{7,11},{8,4},{9,5},... | collective-permute-start | bytes 110600 | tf_op jit(solution)/shard_map/ppermute | solution.py:576
  26.3 4.7 %collective-permute-start.12 = (bf16[96,128]{1,0:T(8,128)(2,1)S(1)}, bf16[96,128]{1,0:T(8,128)(2,1)S(1)}, u32[]{:S(2)}, u32[]{:S(2)}) collective-permute-start(bf16[96,128]{1,0:T(8,128)(2,1)S(1)} %fusion), channel_id=1, source_target_pairs={{0,8},{1,9},{2,10},{3,11},{4,12},{5,13},{6,14},{7,15},{8,0},{9,1},... | collective-permute-start | bytes 73736 | tf_op jit(solution)/shard_map/ppermute | solution.py:576
  27.3 1.2 %collective-permute-start.8 = (bf16[48,128]{1,0:T(8,128)(2,1)S(1)}, bf16[48,128]{1,0:T(8,128)(2,1)S(1)}, u32[]{:S(2)}, u32[]{:S(2)}) collective-permute-start(bf16[48,128]{1,0:T(8,128)(2,1)S(1)} %get-tuple-element.73), channel_id=1, source_target_pairs={{0,1},{1,0},{2,3},{3,2},{4,5},{5,4},{6,7},{7,6},{8,9},{9,8},{10,11... | collective-permute-start | bytes 36872 | tf_op jit(solution)/shard_map/ppermute | solution.py:584
  31.0 1.8 %collective-permute-start.13 = (f32[96,128]{1,0:T(8,128)S(1)}, f32[96,128]{1,0:T(8,128)S(1)}, u32[]{:S(2)}, u32[]{:S(2)}) collective-permute-start(f32[96,128]{1,0:T(8,128)S(1)} %add_add_fusion.own), channel_id=1, source_target_pairs={{0,1},{1,0},{2,3},{3,2},{4,5},{5,4},{6,7},{7,6},{8,9},{9,8},{10,11... | collective-permute-start | bytes 147464 | tf_op jit(solution)/shard_map/ppermute | solution.py:576
